TPU v7x, 32 devices: a whole 2x2x4 slice. The times are simulated.
32 devices in a mesh: dp: 16 (over z, y, core), sub: 2 (over x).
Axes of the slice: x: 2, y: 2, z: 4, core: 2. Of those that a mesh axis runs over, the one named last changes fastest.
Arguments:
- block_input: bfloat16 [2, 4096, 2048], P(None, ('dp', 'sub')), may hold values from -6 to 6
- out_grad: bfloat16 [2, 4096, 2048], P(None, ('dp', 'sub')), may hold values from -6 to 6
- seq_lengths: int32 [2, 32, 3], P(None, ('dp', 'sub')), may hold values from 1 to 96, 128 in all within a row
- attn_gain: bfloat16 [2048], P(('dp', 'sub')), may hold values from 0.5 to 1.5
- w_query: bfloat16 [2048, 2048], P(('dp', 'sub')), may hold values from -0.125 to 0.125
- w_key: bfloat16 [256, 2048], P(('dp', 'sub')), may hold values from -0.125 to 0.125
- w_value: bfloat16 [256, 2048], P(('dp', 'sub')), may hold values from -0.125 to 0.125
- w_output: bfloat16 [2048, 2048], P(('dp', 'sub')), may hold values from -0.75 to 0.75
- mlp_gain: bfloat16 [2048], P(('dp', 'sub')), may hold values from 0.5 to 1.5
- w_gate: bfloat16 [5632, 2048], P(('dp', 'sub')), may hold values from -0.125 to 0.125
- w_up: bfloat16 [5632, 2048], P(('dp', 'sub')), may hold values from -0.125 to 0.125
- w_down: bfloat16 [5632, 2048], P(('dp', 'sub')), may hold values from -0.109375 to 0.109375
Outputs:
- block_output: bfloat16 [2, 4096, 2048], P(None, ('dp', 'sub'))
- input_grad: bfloat16 [2, 4096, 2048], P(None, ('dp', 'sub'))
- attn_gain_grad: float32 [2048], P(('dp', 'sub'))
- query_grad: float32 [2048, 2048], P(('dp', 'sub'))
- key_grad: float32 [256, 2048], P(('dp', 'sub'))
- value_grad: float32 [256, 2048], P(('dp', 'sub'))
- output_grad: float32 [2048, 2048], P(('dp', 'sub'))
- mlp_gain_grad: float32 [2048], P(('dp', 'sub'))
- gate_grad: float32 [5632, 2048], P(('dp', 'sub'))
- up_grad: float32 [5632, 2048], P(('dp', 'sub'))
- down_grad: float32 [5632, 2048], P(('dp', 'sub'))
Inputs may be any that keep to these rules, and one draw needn't show every extreme that they name: `seq_lengths`: the 3 lengths of each row sum to 128; the largest of each row is exactly 96.
All inputs are finite; a program needn't handle non-finite values.
Results may differ from a plain program's by a relative error of at most 0.014.
Values may be sent and summed in bfloat16 or wider, within the bound.
No kernel may reach another device: no remote copies, remote signals or barrier semaphores. Data moves between devices by JAX's collectives and lax.ppermute only.
A program may use at most 768 MiB of HBM per device.

v0:
```python
import jax
import jax.numpy as jnp
from jax import lax
from jax.sharding import PartitionSpec as P

HEAD_DIM = 64


EPS = 1e-05
ROPE_BASE = 10000.0
NEG_LARGE = -1e30


def positions(lengths_row, row_count):
    seq_ends = jnp.cumsum(lengths_row)
    starts = seq_ends - lengths_row
    token_index = jnp.arange(row_count, dtype=jnp.int32)
    segment = jnp.sum((token_index[:, None] >= seq_ends[None, :]).astype(jnp.int32), 1)
    chosen = segment[:, None] == jnp.arange(lengths_row.shape[0], dtype=jnp.int32)[None, :]
    offsets = token_index - jnp.sum(jnp.where(chosen, starts[None, :], 0), 1)
    allowed = (segment[:, None] == segment[None, :]) & (
        token_index[None, :] <= token_index[:, None]
    )
    return (offsets, allowed)


def rotary_tables(offsets, width):
    half_width = width // 2
    frequency = ROPE_BASE ** (-jnp.arange(half_width, dtype=jnp.float32) * 2.0 / width)
    angles = offsets.astype(jnp.float32)[:, None] * frequency[None, :]
    return (jnp.cos(angles)[:, None, :], jnp.sin(angles)[:, None, :])


def rotate(values, cosine, sine_table):
    half_width = values.shape[-1] // 2
    first_half = values[..., :half_width]
    second_half = values[..., half_width:]
    return jnp.concatenate(
        [
            first_half * cosine - second_half * sine_table,
            second_half * cosine + first_half * sine_table,
        ],
        -1,
    )


def rotate_back(grads, cosine, sine_table):
    half_width = grads.shape[-1] // 2
    upper_half = grads[..., :half_width]
    lower_half = grads[..., half_width:]
    return jnp.concatenate(
        [
            upper_half * cosine + lower_half * sine_table,
            lower_half * cosine - upper_half * sine_table,
        ],
        -1,
    )


def project(activity, weight):
    return lax.dot_general(
        activity, weight, (((1,), (1,)), ((), ())), preferred_element_type=jnp.float32
    )


def apply_rows(activity, weight):
    return jnp.dot(activity, weight, preferred_element_type=jnp.float32)


def norm_forward(values, gain_row):
    inverse = lax.rsqrt(jnp.mean(values * values, -1, keepdims=True) + EPS)
    normed = values * inverse
    return (normed, inverse, (normed * gain_row.astype(jnp.float32)).astype(jnp.bfloat16))


def norm_backward(grad_hidden, normed, inverse, gain_row):
    grad_normed = grad_hidden * gain_row.astype(jnp.float32)
    return inverse * (grad_normed - normed * jnp.mean(grad_normed * normed, -1, keepdims=True))


def attention_scores(query_rot, key_rot, allowed):
    scores = jnp.einsum(
        "qhgd,khd->hgqk", query_rot, key_rot, preferred_element_type=jnp.float32
    ) * HEAD_DIM ** (-0.5)
    return jnp.where(allowed, scores, NEG_LARGE)


def forward_pass(block_rows, lengths_row, gathered):
    attn_gain, w_query, w_key, w_value, w_output, mlp_gain, w_gate, w_up, w_down = gathered
    row_count = block_rows.shape[0]
    query_heads = w_query.shape[0] // HEAD_DIM
    key_heads = w_key.shape[0] // HEAD_DIM
    group_size = query_heads // key_heads
    offsets, allowed = positions(lengths_row, row_count)
    cosine, sine_table = rotary_tables(offsets, HEAD_DIM)
    resid_in = block_rows.astype(jnp.float32)
    normed_one, inverse_one, hidden_one = norm_forward(resid_in, attn_gain)
    query_lin = project(hidden_one, w_query).reshape(row_count, query_heads, HEAD_DIM)
    key_lin = project(hidden_one, w_key).reshape(row_count, key_heads, HEAD_DIM)
    value_rows = (
        project(hidden_one, w_value).astype(jnp.bfloat16).reshape(row_count, key_heads, HEAD_DIM)
    )
    query_rot = (
        rotate(query_lin, cosine, sine_table)
        .astype(jnp.bfloat16)
        .reshape(row_count, key_heads, group_size, HEAD_DIM)
    )
    key_rot = rotate(key_lin, cosine, sine_table).astype(jnp.bfloat16)
    scores = attention_scores(query_rot, key_rot, allowed)
    top_score = jnp.max(scores, -1, keepdims=True)
    exp_scores = jnp.exp(scores - top_score)
    row_total = jnp.sum(exp_scores, -1, keepdims=True)
    prob_low = (exp_scores / row_total).astype(jnp.bfloat16)
    log_total = top_score + jnp.log(row_total)
    mixed = jnp.einsum("hgqk,khd->qhgd", prob_low, value_rows, preferred_element_type=jnp.float32)
    mixed = mixed.astype(jnp.bfloat16).reshape(row_count, query_heads * HEAD_DIM)
    resid_mid = resid_in + apply_rows(mixed, w_output)
    normed_two, inverse_two, hidden_two = norm_forward(resid_mid, mlp_gain)
    gate_rows = project(hidden_two, w_gate)
    up_rows = project(hidden_two, w_up)
    inner = (jax.nn.silu(gate_rows) * up_rows).astype(jnp.bfloat16)
    block_out = (resid_mid + apply_rows(inner, w_down)).astype(jnp.bfloat16)
    saved = (
        allowed,
        cosine,
        sine_table,
        normed_one,
        inverse_one,
        hidden_one,
        value_rows,
        query_rot,
        key_rot,
        log_total,
        mixed,
        normed_two,
        inverse_two,
        hidden_two,
        gate_rows,
        up_rows,
        inner,
    )
    return (block_out, saved)


def backward_pass(grad_rows, saved, gathered):
    attn_gain, w_query, w_key, w_value, w_output, mlp_gain, w_gate, w_up, w_down = gathered
    (
        allowed,
        cosine,
        sine_table,
        normed_one,
        inverse_one,
        hidden_one,
        value_rows,
        query_rot,
        key_rot,
        log_total,
        mixed,
        normed_two,
        inverse_two,
        hidden_two,
        gate_rows,
        up_rows,
        inner,
    ) = saved
    row_count = grad_rows.shape[0]
    grad_out = grad_rows.astype(jnp.float32)
    grad_inner = project(grad_rows, w_down)
    sigmoid_gate = jax.nn.sigmoid(gate_rows)
    silu_gate = gate_rows * sigmoid_gate
    grad_gate = (
        grad_inner * up_rows * sigmoid_gate * (1.0 + gate_rows * (1.0 - sigmoid_gate))
    ).astype(jnp.bfloat16)
    grad_up = (grad_inner * silu_gate).astype(jnp.bfloat16)
    grad_hidden_two = apply_rows(grad_gate, w_gate) + apply_rows(grad_up, w_up)
    grad_mid = grad_out + norm_backward(grad_hidden_two, normed_two, inverse_two, mlp_gain)
    grad_branch = grad_mid.astype(jnp.bfloat16)
    grad_mixed = project(grad_branch, w_output).astype(jnp.bfloat16).reshape(query_rot.shape)
    scores = attention_scores(query_rot, key_rot, allowed)
    attn_probs = jnp.exp(scores - log_total)
    prob_low = attn_probs.astype(jnp.bfloat16)
    grad_probs = jnp.einsum(
        "qhgd,khd->hgqk", grad_mixed, value_rows, preferred_element_type=jnp.float32
    )
    grad_scores = attn_probs * (grad_probs - jnp.sum(grad_probs * attn_probs, -1, keepdims=True))
    grad_scores = grad_scores.astype(jnp.bfloat16)
    grad_value = jnp.einsum(
        "hgqk,qhgd->khd", prob_low, grad_mixed, preferred_element_type=jnp.float32
    )
    grad_value = grad_value.astype(jnp.bfloat16).reshape(row_count, -1)
    score_scale = HEAD_DIM ** (-0.5)
    grad_qrot = (
        jnp.einsum("hgqk,khd->qhgd", grad_scores, key_rot, preferred_element_type=jnp.float32)
        * score_scale
    )
    grad_krot = (
        jnp.einsum("hgqk,qhgd->khd", grad_scores, query_rot, preferred_element_type=jnp.float32)
        * score_scale
    )
    grad_query = rotate_back(grad_qrot.reshape(row_count, -1, HEAD_DIM), cosine, sine_table)
    grad_query = grad_query.astype(jnp.bfloat16).reshape(row_count, -1)
    grad_key = (
        rotate_back(grad_krot, cosine, sine_table).astype(jnp.bfloat16).reshape(row_count, -1)
    )
    grad_hidden_one = (
        apply_rows(grad_query, w_query)
        + apply_rows(grad_key, w_key)
        + apply_rows(grad_value, w_value)
    )
    grad_input = (
        grad_mid + norm_backward(grad_hidden_one, normed_one, inverse_one, attn_gain)
    ).astype(jnp.bfloat16)
    gain_terms = jnp.stack(
        [jnp.sum(grad_hidden_one * normed_one, 0), jnp.sum(grad_hidden_two * normed_two, 0)]
    )
    stored = (
        grad_query,
        hidden_one,
        grad_key,
        grad_value,
        mixed,
        grad_branch,
        grad_gate,
        hidden_two,
        grad_up,
        inner,
        grad_rows,
    )
    return (grad_input, stored, gain_terms)


def slice_term(left_rows, right_rows, owner, width):
    piece = lax.dynamic_slice_in_dim(left_rows, owner * width, width, 1)
    return lax.dot_general(
        piece, right_rows, (((0,), (0,)), ((), ())), preferred_element_type=jnp.float32
    )


def on_device(
    block_input,
    out_grad,
    seq_lengths,
    attn_gain,
    w_query,
    w_key,
    w_value,
    w_output,
    mlp_gain,
    w_gate,
    w_up,
    w_down,
):
    block_outs = []
    grad_inputs = []
    collected = [[] for member in range(11)]
    gain_total = jnp.zeros((2, block_input.shape[2]), jnp.float32)
    for batch_index in range(block_input.shape[0]):
        forward_layer = (
            lax.all_gather(attn_gain, ("dp", "sub"), axis=0, tiled=True),
            lax.all_gather(w_query, ("dp", "sub"), axis=0, tiled=True),
            lax.all_gather(w_key, ("dp", "sub"), axis=0, tiled=True),
            lax.all_gather(w_value, ("dp", "sub"), axis=0, tiled=True),
            lax.all_gather(w_output, ("dp", "sub"), axis=0, tiled=True),
            lax.all_gather(mlp_gain, ("dp", "sub"), axis=0, tiled=True),
            lax.all_gather(w_gate, ("dp", "sub"), axis=0, tiled=True),
            lax.all_gather(w_up, ("dp", "sub"), axis=0, tiled=True),
            lax.all_gather(w_down, ("dp", "sub"), axis=0, tiled=True),
        )
        block_out, saved = forward_pass(
            block_input[batch_index], seq_lengths[batch_index, 0], forward_layer
        )
        backward_layer = (
            lax.all_gather(attn_gain, ("dp", "sub"), axis=0, tiled=True),
            lax.all_gather(w_query, ("dp", "sub"), axis=0, tiled=True),
            lax.all_gather(w_key, ("dp", "sub"), axis=0, tiled=True),
            lax.all_gather(w_value, ("dp", "sub"), axis=0, tiled=True),
            lax.all_gather(w_output, ("dp", "sub"), axis=0, tiled=True),
            lax.all_gather(mlp_gain, ("dp", "sub"), axis=0, tiled=True),
            lax.all_gather(w_gate, ("dp", "sub"), axis=0, tiled=True),
            lax.all_gather(w_up, ("dp", "sub"), axis=0, tiled=True),
            lax.all_gather(w_down, ("dp", "sub"), axis=0, tiled=True),
        )
        grad_input, stored, gain_terms = backward_pass(out_grad[batch_index], saved, backward_layer)
        block_outs.append(block_out)
        grad_inputs.append(grad_input)
        gain_total = gain_total + gain_terms
        for member in range(11):
            collected[member].append(stored[member])
    joined = [jnp.concatenate(member_list, 0) for member_list in collected]
    model_width = block_input.shape[2]
    query_width = w_query.shape[0]
    key_width = w_key.shape[0]
    hidden_width = w_gate.shape[0]
    gain_width = attn_gain.shape[0]
    own_rows = 2 * query_width + 2 * key_width + 3 * hidden_width + 1
    filler = jnp.zeros((model_width - 2 * gain_width,), jnp.float32)

    def owner_block(owner):
        gain_row = jnp.concatenate(
            [
                lax.dynamic_slice_in_dim(gain_total[0], owner * gain_width, gain_width, 0),
                lax.dynamic_slice_in_dim(gain_total[1], owner * gain_width, gain_width, 0),
                filler,
            ],
            0,
        )
        return jnp.concatenate(
            [
                slice_term(joined[0], joined[1], owner, query_width),
                slice_term(joined[2], joined[1], owner, key_width),
                slice_term(joined[3], joined[1], owner, key_width),
                slice_term(joined[4], joined[5], owner, query_width),
                slice_term(joined[6], joined[7], owner, hidden_width),
                slice_term(joined[8], joined[7], owner, hidden_width),
                slice_term(joined[9], joined[10], owner, hidden_width),
                gain_row[None, :],
            ],
            0,
        )

    owner_count = own_rows * lax.axis_size(("dp", "sub")) // own_rows
    owners = jnp.arange(owner_count, dtype=jnp.int32)
    blocks = lax.map(owner_block, owners)
    owned = lax.psum_scatter(
        blocks.reshape(owner_count * own_rows, model_width),
        ("dp", "sub"),
        scatter_dimension=0,
        tiled=True,
    )
    cuts = [
        query_width,
        key_width,
        key_width,
        query_width,
        hidden_width,
        hidden_width,
        hidden_width,
    ]
    pieces = []
    offset = 0
    for width in cuts:
        pieces.append(owned[offset : offset + width])
        offset = offset + width
    gain_row = owned[offset]
    return (
        jnp.stack(block_outs),
        jnp.stack(grad_inputs),
        gain_row[:gain_width],
        pieces[0],
        pieces[1],
        pieces[2],
        pieces[3],
        gain_row[gain_width : 2 * gain_width],
        pieces[4],
        pieces[5],
        pieces[6],
    )


def solution(mesh):
    return jax.shard_map(
        on_device,
        mesh=mesh,
        in_specs=(
            P(None, ("dp", "sub"), None),
            P(None, ("dp", "sub"), None),
            P(None, ("dp", "sub"), None),
            P(("dp", "sub")),
            P(("dp", "sub"), None),
            P(("dp", "sub"), None),
            P(("dp", "sub"), None),
            P(("dp", "sub"), None),
            P(("dp", "sub")),
            P(("dp", "sub"), None),
            P(("dp", "sub"), None),
            P(("dp", "sub"), None),
        ),
        out_specs=(
            P(None, ("dp", "sub"), None),
            P(None, ("dp", "sub"), None),
            P(("dp", "sub")),
            P(("dp", "sub"), None),
            P(("dp", "sub"), None),
            P(("dp", "sub"), None),
            P(("dp", "sub"), None),
            P(("dp", "sub")),
            P(("dp", "sub"), None),
            P(("dp", "sub"), None),
            P(("dp", "sub"), None),
        ),
        check_vma=False,
    )
```

profile of v0, /device:TPU:1, one launch (start us, length us, event | category | flops | bytes accessed | tf_op | source)
XLA Modules:
  0.0 4254.8 jit_solution(12626507197467507667)
XLA Ops:
  13.8 40.7 all-reduce.3
  60.3 6.9 all-gather.8.cloned.1.call-done
  70.9 51.9 %all-gather.10.cloned.1.call-done = bf16[256,2048]{1,0:T(8,128)(2,1)} async-done(((bf16[8,2048]{1,0:T(8,128)(2,1)}), bf16[256,2048]{1,0:T(8,128)(2,1)}) %all-gather.10.cloned.1.call-update) | async-done | bytes 1048592 | tf_op jit(solution)/shard_map/all_gather | solution.py:261
  126.3 75.7 %all-gather.12.cloned.1.call-done = bf16[2048,2048]{1,0:T(8,128)(2,1)} async-done(((bf16[64,2048]{1,0:T(8,128)(2,1)}), bf16[2048,2048]{1,0:T(8,128)(2,1)}) %all-gather.12.cloned.1.call-update) | async-done | bytes 8388624 | tf_op jit(solution)/shard_map/all_gather | solution.py:260
  202.1 5.8 fusion.82
  211.6 6.0 fusion.78
  220.7 60.2 %all-gather.14.cloned.1.call-done = bf16[2048,2048]{1,0:T(8,128)(2,1)} async-done(((bf16[64,2048]{1,0:T(8,128)(2,1)}), bf16[2048,2048]{1,0:T(8,128)(2,1)}) %all-gather.14.cloned.1.call-update) | async-done | bytes 8388624 | tf_op jit(solution)/shard_map/all_gather | solution.py:263
  289.9 137.0 %all-gather.16.cloned.1.call-done = bf16[5632,2048]{1,0:T(8,128)(2,1)} async-done(((bf16[176,2048]{1,0:T(8,128)(2,1)}), bf16[5632,2048]{1,0:T(8,128)(2,1)}) %all-gather.16.cloned.1.call-update) | async-done | bytes 23068688 | tf_op jit(solution)/shard_map/all_gather | solution.py:265
  426.9 13.7 fusion.102
  440.6 131.9 %all-gather.18.cloned.1.call-done = bf16[5632,2048]{1,0:T(8,128)(2,1)} async-done(((bf16[176,2048]{1,0:T(8,128)(2,1)}), bf16[5632,2048]{1,0:T(8,128)(2,1)}) %all-gather.18.cloned.1.call-update) | async-done | bytes 23068688 | tf_op jit(solution)/shard_map/all_gather | solution.py:266
  572.5 13.7 fusion.103
  586.1 132.0 %all-gather.20.cloned.1.call-done = bf16[5632,2048]{1,0:T(8,128)(2,1)} async-done(((bf16[176,2048]{1,0:T(8,128)(2,1)}), bf16[5632,2048]{1,0:T(8,128)(2,1)}) %all-gather.20.cloned.1.call-update) | async-done | bytes 23068688 | tf_op jit(solution)/shard_map/all_gather | solution.py:267
  718.2 15.3 multiply_convert_fusion.2
  733.4 20.9 fusion.106
  754.4 12.0 multiply_reduce_fusion.1
  766.4 13.7 fusion.104
  780.0 13.7 fusion.105
  793.7 15.3 multiply_convert_fusion
  809.0 9.8 fusion.108
  818.9 10.2 multiply_reduce_fusion
  892.5 754.4 %while.10 = (s32[]{:T(128)}, f32[32,673,2048]{2,1,0:T(8,128)}, s32[32]{0:T(128)S(1)}, bf16[256,2048]{1,0:T(8,128)(2,1)}, bf16[256,2048]{1,0:T(8,128)(2,1)S(1)}, ...) while((s32[]{:T(128)}, f32[32,673,2048]{2,1,0:T(8,128)}, ...), condition=%wide.region_25.26_spmd, body=%wide.region_24.25_spmd.sunk | while | flops 704643072 | bytes 28910540 | solution.py:323
  1193.3 5.7 bitcast_dynamic-update-slice_fusion.2
  1240.4 5.8 bitcast_dynamic-update-slice_fusion.2
  1264.1 5.7 bitcast_dynamic-update-slice_fusion.2
  1311.3 5.7 bitcast_dynamic-update-slice_fusion.2
  1476.2 5.7 bitcast_dynamic-update-slice_fusion.2
  1499.8 5.7 bitcast_dynamic-update-slice_fusion.2
  1570.6 5.7 bitcast_dynamic-update-slice_fusion.2
  1646.9 142.0 %reshape.411 = f32[21536,2048]{1,0:T(8,128)} reshape(f32[32,673,2048]{2,1,0:T(8,128)} %get-tuple-element.88) | data formatting | bytes 352845824 | tf_op jit(solution)/shard_map/reshape | solution.py:325
  1790.2 13.8 fusion.20
  1807.1 5.8 fusion.21
  1820.3 2417.6 %all-reduce.6.cloned.1.call-done = f32[21536,2048]{1,0:T(8,128)} async-done(((f32[21536,2048]{1,0:T(8,128)}), f32[21536,2048]{1,0:T(8,128)}) %all-reduce.6.cloned.1.call-update) | async-done | bytes 176422928
  (819 shorter events, 769.8 us)
Async XLA Ops:
  7.2 49.3 %copy-start.13 = (bf16[2,128,2048]{2,1,0:T(8,128)(2,1)S(1)}, bf16[2,128,2048]{2,1,0:T(8,128)(2,1)}, u32[]{:S(2)}) copy-start(bf16[2,128,2048]{2,1,0:T(8,128)(2,1)} %param.14) | copy-start | bytes 3145732
  7.2 60.0 %all-gather.8.cloned.1.call-start = ((), (), s32[]{:S(2)}) async-start(), calls=%async_computation | async-start | bytes 1081344 | tf_op jit(solution)/shard_map/all_gather | solution.py:262
  7.9 114.9 %all-gather.10.cloned.1.call-start = ((), (), s32[]{:S(2)}) async-start(), calls=%async_computation.1 | async-start | bytes 1081344 | tf_op jit(solution)/shard_map/all_gather | solution.py:261
  8.7 193.4 %all-gather.12.cloned.1.call-start = ((), (), s32[]{:S(2)}) async-start(), calls=%async_computation.2 | async-start | bytes 8650752 | tf_op jit(solution)/shard_map/all_gather | solution.py:260
  9.4 271.5 %all-gather.14.cloned.1.call-start = ((), (), s32[]{:S(2)}) async-start(), calls=%async_computation.3 | async-start | bytes 8650752 | tf_op jit(solution)/shard_map/all_gather | solution.py:263
  10.0 416.9 %all-gather.16.cloned.1.call-start = ((), (), s32[]{:S(2)}) async-start(), calls=%async_computation.4 | async-start | bytes 23789568 | tf_op jit(solution)/shard_map/all_gather | solution.py:265
  10.6 561.9 %all-gather.18.cloned.1.call-start = ((), (), s32[]{:S(2)}) async-start(), calls=%async_computation.5 | async-start | bytes 23789568 | tf_op jit(solution)/shard_map/all_gather | solution.py:266
  11.1 707.0 %all-gather.20.cloned.1.call-start = ((), (), s32[]{:S(2)}) async-start(), calls=%async_computation.6 | async-start | bytes 23789568 | tf_op jit(solution)/shard_map/all_gather | solution.py:267
  11.9 47.2 %copy-start.17 = (bf16[2,128,2048]{2,1,0:T(8,128)(2,1)S(1)}, bf16[2,128,2048]{2,1,0:T(8,128)(2,1)}, u32[]{:S(2)}) copy-start(bf16[2,128,2048]{2,1,0:T(8,128)(2,1)} %param.15) | copy-start | bytes 3145732
  11.9 4226.0 %all-reduce.6.cloned.1.call-start = ((), (), s32[]{:S(2)}) async-start(), calls=%async_computation.7 | async-start | bytes 352845824
  54.5 157.2 %copy-start.53 = (f32[2048]{0:T(1024)}, f32[2048]{0:T(1024)S(1)}, u32[]{:S(2)}) copy-start(f32[2048]{0:T(1024)S(1)} %convert_element_type.200) | copy-start | bytes 24580
  55.5 773.6 %copy-start.51 = (f32[2048]{0:T(1024)}, f32[2048]{0:T(1024)S(1)}, u32[]{:S(2)}) copy-start(f32[2048]{0:T(1024)S(1)} %convert_element_type.211) | copy-start | bytes 24580
  56.8 145.3 %copy-start.73 = (f32[128]{0:T(128)}, f32[128]{0:T(128)S(1)}, u32[]{:S(2)}) copy-start(f32[128]{0:T(128)S(1)} %get-tuple-element.200) | copy-start | bytes 1540
  56.8 154.9 %copy-start.70 = (f32[128]{0:T(128)}, f32[128]{0:T(128)S(1)}, u32[]{:S(2)}) copy-start(f32[128]{0:T(128)S(1)} %get-tuple-element.201) | copy-start | bytes 1540
  285.8 543.3 %copy-start.7 = (f32[128,2048]{1,0:T(8,128)}, f32[128,2048]{1,0:T(8,128)S(1)}, u32[]{:S(2)}) copy-start(f32[128,2048]{1,0:T(8,128)S(1)} %get-tuple-element.190) | copy-start | bytes 3145732
  286.7 467.6 %copy-start.76 = (f32[128]{0:T(128)}, f32[128]{0:T(128)S(1)}, u32[]{:S(2)}) copy-start(f32[128]{0:T(128)S(1)} %add_rsqrt_fusion.2) | copy-start | bytes 1540
  288.4 540.7 %copy-start.3 = (f32[128,2048]{1,0:T(8,128)}, f32[128,2048]{1,0:T(8,128)S(1)}, u32[]{:S(2)}) copy-start(f32[128,2048]{1,0:T(8,128)S(1)} %get-tuple-element.192) | copy-start | bytes 3145732
  288.4 465.9 %copy-start.79 = (f32[128]{0:T(128)}, f32[128]{0:T(128)S(1)}, u32[]{:S(2)}) copy-start(f32[128]{0:T(128)S(1)} %add_rsqrt_fusion) | copy-start | bytes 1540
  733.4 20.9 copy-start.24
  766.4 62.8 %copy-start.82 = (f32[128]{0:T(128)}, f32[128]{0:T(128)S(1)}, u32[]{:S(2)}) copy-start(f32[128]{0:T(128)S(1)} %broadcast_multiply_fusion.3) | copy-start | bytes 1540
  809.0 9.8 copy-start.26
  809.0 9.8 copy-start.80
  809.0 22.3 slice-start
  818.8 10.3 copy-start.18
  818.9 10.3 copy-start.20
  818.9 10.3 copy-start.77
  818.9 12.4 slice-start.1
  862.4 16.8 copy-start.28
  1790.2 16.8 copy-start.2
  1807.0 8.3 copy-start.75
  1807.0 8.3 copy-start.81
  1807.0 8.3 copy-start.85
  (101 other events, 250.4 us)
Sparse Core Ops, SparseCore 0:
  10.9 56.2 all-gather.7
  70.1 52.6 all-gather.9
  125.8 76.2 all-gather.11
  204.9 75.9 all-gather.13
  283.7 143.1 all-gather.15
  429.6 142.7 all-gather.17
  575.4 142.7 all-gather.19
  1789.1 2448.6 all-reduce.5
where the time goes:
time: 4270 us; the launch traced here: 4250 us
  waiting for transfers between devices  3020 us (71%)
  matrix products  649 us (15%)
  local copies, waits for them, and re-layouts  433 us (10%)
  loops' own time  63.6 us (1%)
    unnamed x9, waiting for transfers between devices  2420 us
    dot_general x224, matrix products, slice_term(): lax.dot_general(piece, right_rows, (((0,), (0,)), ((), ())), preferred_el...  438 us
    dynamic_update_slice x32, local copies, waits for them, and re-layouts, on_device(): blocks = lax.map(owner_block, owners)  182 us
    reshape x1, local copies, waits for them, and re-layouts, on_device(): blocks.reshape(owner_count * own_rows, model_width)  142 us
    all_gather x1, waiting for transfers between devices, on_device(): lax.all_gather(w_gate, ('dp', 'sub'), axis=0, tiled=True)  137 us
    all_gather x1, waiting for transfers between devices, on_device(): lax.all_gather(w_down, ('dp', 'sub'), axis=0, tiled=True)  132 us
    all_gather x1, waiting for transfers between devices, on_device(): lax.all_gather(w_up, ('dp', 'sub'), axis=0, tiled=True)  132 us
    dot_general x14, matrix products, project(): lax.dot_general(activity, weight, (((1,), (1,)), ((), ())), preferred_ele...  111 us
  transfers between devices with their start and end apart: 8, of which 8 were waited for; matrix products, arithmetic and copies ran while one was open for 2% of the time, Pallas kernels for 0%

commit v1 on v0

--- a/solution.py
+++ b/solution.py
@@ -1,14 +1,951 @@
+import functools
 import jax
 import jax.numpy as jnp
 from jax import lax
+from jax.experimental import pallas as pl
+from jax.experimental.pallas import tpu as pltpu
+from jax.sharding import Mesh
 from jax.sharding import PartitionSpec as P
 
+ZH, ZL, MID, CORE, SUB = AXES = ("zh", "zl", "mid", "core", "sub")
+DEVICES = ("dp", "sub")
+
 HEAD_DIM = 64
-
-
 EPS = 1e-05
 ROPE_BASE = 10000.0
 NEG_LARGE = -1e30
+SUM_COLUMNS = 512
+F32 = jnp.float32
+BF16 = jnp.bfloat16
+NT = (((1,), (1,)), ((), ()))
+NN = (((1,), (0,)), ((), ()))
+TN = (((0,), (0,)), ((), ()))
+
+
+def dot(a, b, dims=NN):
+    return lax.dot_general(a, b, dims, preferred_element_type=F32)
+
+
+def call(kernel, name, grid, in_specs, out_specs, out_shape, scratch=()):
+    return pl.pallas_call(
+        kernel,
+        grid=grid,
+        in_specs=in_specs,
+        out_specs=out_specs,
+        out_shape=out_shape,
+        scratch_shapes=scratch,
+        name=name,
+        cost_estimate=pl.CostEstimate(flops=1000, bytes_accessed=1000, transcendentals=0),
+        compiler_params=pltpu.CompilerParams(
+            dimension_semantics=("arbitrary",) * len(grid), vmem_limit_bytes=56 << 20
+        ),
+    )
+
+
+def whole(shape):
+    zeros = (0,) * len(shape)
+    return pl.BlockSpec(shape, lambda *_: zeros, pipeline_mode=pl.Buffered(1))
+
+
+def turn(values, cosine, sine):
+    lane = lax.broadcasted_iota(jnp.int32, (values.shape[0], 128), 1)
+    low = lane % HEAD_DIM < HEAD_DIM // 2
+    blocks = []
+    for at in range(0, values.shape[1], 128):
+        block = values[:, at : at + 128]
+        other = jnp.where(
+            low,
+            pltpu.roll(block, 128 - HEAD_DIM // 2, 1),
+            pltpu.roll(block, HEAD_DIM // 2, 1),
+        )
+        blocks.append(block * cosine + other * sine)
+    return jnp.concatenate(blocks, 1) if len(blocks) > 1 else blocks[0]
+
+
+def two_heads(rows):
+    low = lax.broadcasted_iota(jnp.int32, rows.shape, 1) < HEAD_DIM
+    zero = jnp.zeros_like(rows)
+    return jnp.concatenate([jnp.where(low, rows, zero), jnp.where(low, zero, rows)], 0)
+
+
+def one_head(rows):
+    half = rows.shape[0] // 2
+    low = lax.broadcasted_iota(jnp.int32, (half, 128), 1) < HEAD_DIM
+    return jnp.where(low, rows[:half], rows[half:])
+
+
+def stack_lanes(values):
+    return jnp.concatenate([values[:, at : at + 128] for at in range(0, values.shape[1], 128)], 0)
+
+
+def unstack_lanes(values, rows):
+    return jnp.concatenate([values[at : at + rows] for at in range(0, values.shape[0], rows)], 1)
+
+
+def mask_of(segment):
+    row = segment.shape[1]
+    query = lax.broadcasted_iota(jnp.int32, (row, row), 0)
+    key = lax.broadcasted_iota(jnp.int32, (row, row), 1)
+    across = jnp.broadcast_to(segment, (row, row))
+    return (across == across.T) & (key <= query)
+
+
+def probabilities(stacked_q, keys2, allowed, row):
+    scores = dot(stacked_q, keys2, NT)
+    blocks = []
+    for at in range(0, scores.shape[0], row):
+        halves = []
+        for side in range(2):
+            part = scores[at : at + row, side * row : (side + 1) * row]
+            part = jnp.where(allowed, part, NEG_LARGE)
+            part = jnp.exp(part - jnp.max(part, -1, keepdims=True))
+            halves.append(part * (1.0 / jnp.sum(part, -1, keepdims=True)))
+        blocks.append(jnp.concatenate(halves, 1))
+    return jnp.concatenate(blocks, 0)
+
+
+def owner(mid, sub, zh):
+    return 4 * mid + 2 * sub + zh
+
+
+def assemble(parts, into, kind, rows, step=None, stride=None, offset=0):
+    step = rows if step is None else step
+    stride = rows if stride is None else stride
+    for zh in range(2):
+        for far in range(2):
+            for inner in range(2):
+                at = owner(far, inner, zh) if kind == "a" else owner(inner, far, zh)
+                at = at * stride + offset
+                into[at : at + rows] = parts[2 * zh + far][inner * step : inner * step + rows]
+
+
+def assemble_down(parts, into, first):
+    stride = into.shape[0] // 8
+    assemble(parts[:4], into, "a", first, stride=stride)
+    assemble(parts[4:], into, "b", stride - first, stride=stride, offset=first)
+
+
+def tile_at(step):
+    return (2 * step + 1) % 5
+
+
+def pick(tile, refs, into):
+    for at, ref in enumerate(refs):
+
+        @pl.when(tile == at)
+        def _(ref=ref):
+            into[...] = ref[...]
+
+
+def halves(part, send_ref, keep_ref, here=slice(None)):
+    step = pl.program_id(0)
+
+    @pl.when(step < 2)
+    def _():
+        send_ref[0, :, here] = part.astype(BF16)
+
+    @pl.when(step >= 2)
+    def _():
+        keep_ref[0, :, here] = part.astype(BF16)
+
+
+def halves_out(tile, width):
+    specs = [
+        pl.BlockSpec((1, tile, width), lambda s: (jnp.minimum(s, 1), 0, 0)),
+        pl.BlockSpec((1, tile, width), lambda s: (jnp.maximum(s - 2, 0), 0, 0)),
+    ]
+    return specs, [jax.ShapeDtypeStruct((2, tile, width), BF16)] * 2
+
+
+def quarters(part, send_refs, keep_ref, here=slice(None)):
+    step = pl.program_id(0)
+    rows = send_refs[0].shape[0]
+    for at in range(2):
+
+        @pl.when(step == at)
+        def _(at=at):
+            send_refs[2 * at][:, here] = part[:rows].astype(BF16)
+            send_refs[2 * at + 1][:, here] = part[rows:].astype(BF16)
+
+    @pl.when(step >= 2)
+    def _():
+        keep_ref[0, :, here] = part.astype(BF16)
+
+
+def quarters_out(tile, width):
+    specs, shapes = halves_out(tile, width)
+    quarter = (tile // 2, width)
+    return (
+        [pl.BlockSpec(quarter, lambda s: (0, 0))] * 4 + specs[1:],
+        [jax.ShapeDtypeStruct(quarter, BF16)] * 4 + shapes[1:],
+    )
+
+
+def pick_two(tile, refs, into):
+    rows = refs[0].shape[0]
+    for at in range(4):
+
+        @pl.when(tile == at)
+        def _(at=at):
+            into[:rows] = refs[2 * at][...]
+            into[rows:] = refs[2 * at + 1][...]
+
+
+def attn_forward_kernel(row, head_rows, *refs):
+    x_refs, (gain_ref, cos_ref, sin_ref, seg_ref, moved_ref, kv_own_ref, kv_core_ref) = (
+        refs[:4],
+        refs[4:11],
+    )
+    a_refs, o_refs = refs[11:15], refs[15:19]
+    hid_ref, qkv_ref, mixed_ref, send_ref, keep_ref, wqkv_ref, wo_ref, x_ref = refs[19:]
+    step = pl.program_id(0)
+    width = 8 * head_rows
+    pick(tile_at(step), x_refs, x_ref)
+
+    @pl.when(step == 0)
+    def _():
+        assemble(a_refs, wqkv_ref, "a", head_rows, step=head_rows + HEAD_DIM // 4)
+        assemble(o_refs, wo_ref, "b", head_rows)
+        kv_rows = HEAD_DIM // 8
+        for side in range(2):
+            both = [
+                [ref[4 * side + at].astype(F32) for ref in (kv_own_ref, kv_core_ref)]
+                for at in range(4)
+            ]
+            for which in range(2):
+                here = slice(which * kv_rows, (which + 1) * kv_rows)
+                parts = [
+                    both[mid * 2 + sub][core][here]
+                    for mid in range(2)
+                    for core in range(2)
+                    for sub in range(2)
+                ]
+                placed = dot(moved_ref[...], jnp.concatenate(parts, 0).astype(BF16)).astype(BF16)
+                low = width + (2 * which + side) * HEAD_DIM
+                wqkv_ref[low : low + HEAD_DIM] = placed
+
+    x = x_ref[...].astype(F32)
+    inverse = lax.rsqrt(jnp.mean(x * x, -1, keepdims=True) + EPS)
+    hidden = (x * inverse * gain_ref[...]).astype(BF16)
+    hid_ref[...] = hidden
+    lin = dot(hidden, wqkv_ref[...], NT)
+    cosine, sine = cos_ref[...], sin_ref[...]
+    qk = turn(lin[:, : width + 128], cosine, sine).astype(BF16)
+    v_rows = lin[:, width + 128 :].astype(BF16)
+    qkv_ref[:, : width + 128] = qk
+    qkv_ref[:, width + 128 :] = v_rows
+    scale = HEAD_DIM ** (-0.5)
+    for at in range(0, x.shape[0], row):
+        allowed = mask_of(seg_ref[0, at // row : at // row + 1])
+        keys2 = two_heads(qk[at : at + row, width:] * jnp.asarray(scale, BF16))
+        values2 = two_heads(v_rows[at : at + row])
+        probs = probabilities(stack_lanes(qk[at : at + row, :width]), keys2, allowed, row)
+        mixed = dot(probs.astype(BF16), values2).astype(BF16)
+        mixed_ref[at : at + row] = unstack_lanes(mixed, row)
+    halves(dot(mixed_ref[...], wo_ref[...]), send_ref, keep_ref)
+
+
+def attn_forward(x, gain, cosine, sine, segment, moved, kv_own, kv_core, a_parts, o_parts,
+                 head_rows, row):
+    tile, width = x[0].shape
+    rows = lambda n: pl.BlockSpec((tile, n), lambda s: (tile_at(s), 0))
+    full = lambda n: pl.BlockSpec((n, width), lambda s: (0, 0))
+    q_width = 8 * head_rows
+    shape = lambda *dims: jax.ShapeDtypeStruct(dims, BF16)
+    half_specs, half_shapes = halves_out(tile, width)
+    return call(
+        functools.partial(attn_forward_kernel, row, head_rows),
+        "attn_forward",
+        (4,),
+        [whole(one.shape) for one in x]
+        + [
+            whole((1, width)),
+            rows(128),
+            rows(128),
+            pl.BlockSpec((1,) + segment.shape[1:], lambda s: (tile_at(s), 0, 0)),
+        ]
+        + [whole(one.shape) for one in (moved, kv_own, kv_core, *a_parts, *o_parts)],
+        [rows(width), rows(q_width + 256), rows(q_width)]
+        + half_specs
+        + [full(q_width + 256), full(q_width)],
+        [shape(4 * tile, width), shape(4 * tile, q_width + 256), shape(4 * tile, q_width)]
+        + half_shapes
+        + [shape(q_width + 256, width), shape(q_width, width)],
+        [pltpu.VMEM((tile, width), BF16)],
+    )(*x, gain, cosine, sine, segment, moved, kv_own, kv_core, *a_parts, *o_parts)
+
+
+def attn_backward_kernel(row, *refs):
+    g_refs, x_refs = refs[:8], refs[8:12]
+    qkv_ref, cos_ref, sin_ref, seg_ref, wqkv_ref, wo_ref = refs[12:18]
+    gqkv_ref, gain_ref, *send_refs, keep_ref, g_ref, x_ref = refs[18:]
+    step = pl.program_id(0)
+    pick_two(tile_at(step), g_refs, g_ref)
+    pick(tile_at(step), x_refs, x_ref)
+    grad_mixed = dot(g_ref[...], wo_ref[...], NT).astype(BF16)
+    width = grad_mixed.shape[1]
+    qkv = qkv_ref[...]
+    cosine, sine = cos_ref[...], -sin_ref[...]
+    scale = HEAD_DIM ** (-0.5)
+    for at in range(0, grad_mixed.shape[0], row):
+        here = slice(at, at + row)
+        allowed = mask_of(seg_ref[0, at // row : at // row + 1])
+        keys2 = two_heads(qkv[here, width : width + 128] * jnp.asarray(scale, BF16))
+        values2 = two_heads(qkv[here, width + 128 :])
+        stacked_q = stack_lanes(qkv[here, :width])
+        stacked_g = stack_lanes(grad_mixed[here])
+        probs = probabilities(stacked_q, keys2, allowed, row)
+        grad_probs = dot(stacked_g, values2, NT)
+        moved = grad_probs * probs
+        left = probs[:, :row] * (
+            grad_probs[:, :row] - jnp.sum(moved[:, :row], -1, keepdims=True)
+        )
+        right = probs[:, row:] * (
+            grad_probs[:, row:] - jnp.sum(moved[:, row:], -1, keepdims=True)
+        )
+        grad_scores = jnp.concatenate([left, right], 1).astype(BF16)
+        grad_value = one_head(dot(probs.astype(BF16), stacked_g, TN))
+        grad_key = one_head(dot(grad_scores, stacked_q, TN)) * scale
+        grad_query = unstack_lanes(dot(grad_scores, keys2), row)
+        gqkv_ref[here, :width] = turn(grad_query, cosine[here], sine[here]).astype(BF16)
+        gqkv_ref[here, width : width + 128] = turn(grad_key, cosine[here], sine[here]).astype(BF16)
+        gqkv_ref[here, width + 128 :] = grad_value.astype(BF16)
+    part = dot(gqkv_ref[...], wqkv_ref[...])
+    x = x_ref[...].astype(F32)
+    normed = x * lax.rsqrt(jnp.mean(x * x, -1, keepdims=True) + EPS)
+    terms = jnp.sum(part * normed, 0, keepdims=True)
+
+    @pl.when(step == 0)
+    def _():
+        gain_ref[...] = terms
+
+    @pl.when(step > 0)
+    def _():
+        gain_ref[...] += terms
+
+    quarters(part, send_refs, keep_ref)
+
+
+def attn_backward(grads, x, qkv, cosine, sine, segment, wqkv, wo, row):
+    tile, width = x[0].shape
+    rows = lambda n: pl.BlockSpec((tile, n), lambda s: (tile_at(s), 0))
+    half_specs, half_shapes = quarters_out(tile, width)
+    return call(
+        functools.partial(attn_backward_kernel, row),
+        "attn_backward",
+        (4,),
+        [whole(one.shape) for one in (*grads, *x)]
+        + [
+            rows(qkv.shape[1]),
+            rows(128),
+            rows(128),
+            pl.BlockSpec((1,) + segment.shape[1:], lambda s: (tile_at(s), 0, 0)),
+            whole(wqkv.shape),
+            whole(wo.shape),
+        ],
+        [rows(qkv.shape[1]), pl.BlockSpec((1, width), lambda s: (0, 0))] + half_specs,
+        [jax.ShapeDtypeStruct(qkv.shape, BF16), jax.ShapeDtypeStruct((1, width), F32)]
+        + half_shapes,
+        [pltpu.VMEM((tile, width), BF16)] * 2,
+    )(*grads, *x, qkv, cosine, sine, segment, wqkv, wo)
+
+
+def units_kernel(*refs):
+    inner_ref, dgate_ref, dup_ref, gate_ref, up_ref, h_ref = refs[12:]
+    step = pl.program_id(0)
+    pick(step, refs[:4], h_ref)
+
+    @pl.when(step == 0)
+    def _():
+        assemble(refs[4:8], gate_ref, "a", gate_ref.shape[0] // 8)
+        assemble(refs[8:12], up_ref, "b", up_ref.shape[0] // 8)
+
+    gate = dot(h_ref[...], gate_ref[...], NT)
+    up = dot(h_ref[...], up_ref[...], NT)
+    sigmoid = 1.0 / (1.0 + jnp.exp(-gate))
+    silu = gate * sigmoid
+    inner_ref[...] = (silu * up).astype(BF16)
+    dup_ref[...] = silu.astype(BF16)
+    dgate_ref[...] = (up * (sigmoid * (1.0 + gate * (1.0 - sigmoid)))).astype(BF16)
+
+
+def units(hidden, gate_parts, up_parts):
+    tile, width = hidden[0].shape
+    count = 4 * gate_parts[0].shape[0]
+    rows = pl.BlockSpec((tile, count), lambda s: (s, 0))
+    return call(
+        units_kernel,
+        "units",
+        (4,),
+        [whole(one.shape) for one in (*hidden, *gate_parts, *up_parts)],
+        [rows] * 3,
+        [jax.ShapeDtypeStruct((4 * tile, count), BF16)] * 3,
+        [pltpu.VMEM((count, width), BF16)] * 2 + [pltpu.VMEM((tile, width), BF16)],
+    )(*hidden, *gate_parts, *up_parts)
+
+
+def unit_grads_kernel(first, *refs):
+    dgate_ref, dup_ref = refs[4:6]
+    gg_ref, gu_ref, down_ref, g_ref = refs[14:]
+    step = pl.program_id(0)
+    pick(step, refs[:4], g_ref)
+
+    @pl.when(step == 0)
+    def _():
+        assemble_down(refs[6:14], down_ref, first)
+
+    inner = dot(g_ref[...], down_ref[...], NT)
+    gg_ref[...] = (inner * dgate_ref[...].astype(F32)).astype(BF16)
+    gu_ref[...] = (inner * dup_ref[...].astype(F32)).astype(BF16)
+
+
+def unit_grads(grads, down_parts, dgate, dup, first):
+    tile, width = grads[0].shape
+    count = dgate.shape[1]
+    rows = pl.BlockSpec((tile, count), lambda s: (s, 0))
+    return call(
+        functools.partial(unit_grads_kernel, first),
+        "unit_grads",
+        (4,),
+        [whole(one.shape) for one in grads]
+        + [rows, rows]
+        + [whole(one.shape) for one in down_parts],
+        [rows] * 2,
+        [jax.ShapeDtypeStruct((4 * tile, count), BF16)] * 2,
+        [pltpu.VMEM((count, width), BF16), pltpu.VMEM((tile, width), BF16)],
+    )(*grads, dgate, dup, *down_parts)
+
+
+def sum_kernel(count, first, *refs):
+    lefts, parts = refs[:count], refs[count : count + 8]
+    *send_refs, keep_ref = refs[count + 8 : len(refs) - count]
+    weights = refs[len(refs) - count :]
+    step = pl.program_id(0)
+    rows = weights[0].shape[0] // 8
+
+    @pl.when(step == 0)
+    def _():
+        if count == 1:
+            assemble_down(parts, weights[0], first)
+        else:
+            assemble(parts[:4], weights[0], "a", rows)
+            assemble(parts[4:], weights[1], "b", rows)
+
+    def pieces():
+        size = keep_ref.shape[2]
+        for low in range(0, size, SUM_COLUMNS):
+            here = slice(low, min(low + SUM_COLUMNS, size))
+            total = dot(lefts[0][...], weights[0][:, here])
+            for left, weight in zip(lefts[1:], weights[1:]):
+                total = total + dot(left[...], weight[:, here])
+            yield here, total
+
+    for here, total in pieces():
+        if len(send_refs) == 4:
+            quarters(total, send_refs, keep_ref, here)
+        else:
+            halves(total, send_refs[0], keep_ref, here)
+
+
+def sum_rows(lefts, parts, name, first=0):
+    tokens, count = lefts[0].shape
+    width = parts[0].shape[-1]
+    tile = tokens // 4
+    out = halves_out if len(lefts) == 1 else quarters_out
+    half_specs, half_shapes = out(tile, width)
+    return call(
+        functools.partial(sum_kernel, len(lefts), first),
+        name,
+        (4,),
+        [pl.BlockSpec((tile, count), lambda s: (tile_at(s), 0)) for one in lefts]
+        + [whole(one.shape) for one in parts],
+        half_specs,
+        half_shapes,
+        [pltpu.VMEM((count, width), BF16)] * len(lefts),
+    )(*lefts, *parts)
+
+
+def put_owners(place, a_keep, a_send, b_keep, b_send):
+    step = pl.program_id(0)
+
+    @pl.when(step < 2)
+    def _():
+        place(a_keep, (0, 1, 2, 3))
+        place(a_send, (4, 5, 6, 7))
+
+    @pl.when(step >= 2)
+    def _():
+        place(b_keep, (0, 1, 4, 5))
+        place(b_send, (2, 3, 6, 7))
+
+
+def owners_out(rows, width):
+    half = lambda place: pl.BlockSpec((4, rows, width // 4), lambda s: (0, 0, place(s)))
+    early, late = half(lambda s: jnp.minimum(s, 1)), half(lambda s: jnp.maximum(s - 2, 0))
+    return [early, early, late, late], [jax.ShapeDtypeStruct((4, rows, width // 2), BF16)] * 4
+
+
+def weight_grad_kernel(rows, l_ref, *refs):
+    right = jnp.concatenate([ref[...] for ref in refs[:4]], 0)
+    grads = dot(l_ref[...], right, TN).astype(BF16)
+
+    def place(ref, owners):
+        for at, one in enumerate(owners):
+            ref[at] = grads[one * rows : (one + 1) * rows]
+
+    put_owners(place, *refs[4:])
+
+
+def weight_grad(left, right, name):
+    tokens, count = left.shape
+    tile, width = right[0].shape
+    specs, shapes = owners_out(count // 8, width)
+    return call(
+        functools.partial(weight_grad_kernel, count // 8),
+        name,
+        (4,),
+        [whole(left.shape)] + [pl.BlockSpec((tile, width // 4), lambda s: (0, s))] * 4,
+        specs,
+        shapes,
+    )(left, *right)
+
+
+def attn_grads_kernel(head_rows, kv_rows, gqkv_ref, hid_ref, mixed_ref, moved_ref, *refs):
+    first = dot(gqkv_ref[...], hid_ref[...], TN).astype(BF16)
+    right = jnp.concatenate([ref[...] for ref in refs[:8]], 0)
+    second = dot(mixed_ref[...], right, TN).astype(BF16)
+    width = 8 * head_rows
+    placed = {}
+    for which in range(2):
+        for side in range(2):
+            low = width + (2 * which + side) * HEAD_DIM
+            placed[which, side] = dot(moved_ref[...], first[low : low + HEAD_DIM])
+
+    def place(ref, owners):
+        for at, one in enumerate(owners):
+            mid, sub, side = one // 4, one // 2 % 2, one % 2
+            lows = [(mid * 4 + core * 2 + sub) * kv_rows for core in range(2)]
+            kv = [placed[which, side][low : low + kv_rows] for low in lows for which in range(2)]
+            here = slice(one * head_rows, (one + 1) * head_rows)
+            ref[at, :head_rows] = first[here]
+            ref[at, head_rows : head_rows + 4 * kv_rows] = jnp.concatenate(kv, 0).astype(BF16)
+            ref[at, head_rows + 4 * kv_rows :] = second[here]
+
+    put_owners(place, *refs[8:])
+
+
+def attn_grads(gqkv, hidden, mixed, right, moved, head_rows, kv_rows):
+    tokens, width = hidden.shape
+    columns = width // 4
+    specs, shapes = owners_out(2 * head_rows + 4 * kv_rows, width)
+    return call(
+        functools.partial(attn_grads_kernel, head_rows, kv_rows),
+        "attn_grads",
+        (4,),
+        [
+            whole(gqkv.shape),
+            pl.BlockSpec((tokens, columns), lambda s: (0, s)),
+            whole(mixed.shape),
+            whole(moved.shape),
+        ]
+        + [pl.BlockSpec((tokens // 8, columns), lambda s: (0, s))] * 8,
+        specs,
+        shapes,
+    )(gqkv, hidden, mixed, moved, *right)
+
+
+def norm_forward(values, gain):
+    inverse = lax.rsqrt(jnp.mean(values * values, -1, keepdims=True) + EPS)
+    normed = values * inverse
+    return (normed, inverse, (normed * gain).astype(BF16))
+
+
+def norm_backward(grad_hidden, normed, inverse, gain):
+    grad_normed = grad_hidden * gain
+    return inverse * (grad_normed - normed * jnp.mean(grad_normed * normed, -1, keepdims=True))
+
+
+def swap(value, axis):
+    return lax.ppermute(value, axis, [(0, 1), (1, 0)])
+
+
+def up32(value):
+    return value.astype(F32)
+
+
+def join(*values):
+    return jnp.concatenate(values, 0)
+
+
+class Live:
+    def cut(self):
+        names = sorted(vars(self))
+        values = lax.optimization_barrier(tuple(getattr(self, name) for name in names))
+        for name, value in zip(names, values):
+            setattr(self, name, value)
+
+    @property
+    def pop(self):
+        return Pop(self)
+
+
+class Pop:
+    def __init__(self, live):
+        self.live = live
+
+    def __getattr__(self, name):
+        value = getattr(self.live, name)
+        delattr(self.live, name)
+        return value
+
+
+def tables(lengths_all, row_count):
+    seq_ends = jnp.cumsum(lengths_all, 1)
+    token = jnp.arange(row_count, dtype=jnp.int32)
+    passed = (token[None, :, None] >= seq_ends[:, None, :]).astype(jnp.int32)
+    segment = jnp.sum(passed, 2)
+    offsets = token[None, :] - jnp.sum(passed * lengths_all[:, None, :], 2)
+    half = HEAD_DIM // 2
+    lane = jnp.arange(128, dtype=jnp.int32)
+    frequency = ROPE_BASE ** (-(lane % half).astype(F32) * 2.0 / HEAD_DIM)
+    angles = offsets.reshape(-1, 1).astype(F32) * frequency[None, :]
+    sign = jnp.where(lane % HEAD_DIM < half, -1.0, 1.0)
+    return (segment.astype(F32), jnp.cos(angles), jnp.sin(angles) * sign[None, :])
+
+
+def on_device_small(
+    block_input,
+    out_grad,
+    seq_lengths,
+    attn_gain,
+    w_query,
+    w_key,
+    w_value,
+    w_output,
+    mlp_gain,
+    w_gate,
+    w_up,
+    w_down,
+):
+    width = block_input.shape[2]
+    row_count = block_input.shape[1]
+    micro = block_input.shape[0]
+    tokens = micro * row_count
+    head_rows = w_query.shape[0]
+    kv_rows = w_key.shape[0]
+    gain_width = attn_gain.shape[0]
+    packed = seq_lengths.shape[2]
+    units_own = w_gate.shape[0]
+    first = -(-units_own // 2 // 32) * 32
+    second = units_own - first
+    qkv_rows = head_rows + 2 * kv_rows
+    place = {name: lax.axis_index(name) for name in AXES}
+    place8 = place[MID] * 4 + place[CORE] * 2 + place[SUB]
+    place32 = place[ZH] * 16 + place[ZL] * 8 + place8
+    index = jnp.arange(8 * kv_rows, dtype=jnp.int32)
+    block, inside = index // kv_rows, index % kv_rows
+    moved = (block[:, None] == (block[None, :] ^ place8)) & (inside[:, None] == inside[None, :])
+    moved = moved.astype(BF16)
+    index = jnp.arange(32, dtype=jnp.int32)
+    ordered = (index[:, None] == (index[None, :] ^ place32)).astype(BF16)
+
+    def pair_sum(keep, got, at):
+        return up32(keep[at]) + up32(got[at])
+
+    v = Live()
+    own_x = block_input.reshape(tokens, width)
+    v.own_g = out_grad.reshape(tokens, width)
+
+    pack = join(attn_gain, mlp_gain, seq_lengths.reshape(micro * packed).astype(BF16))
+    v.pack = jnp.pad(pack.reshape(1, -1), ((0, 0), (0, 256 - pack.shape[0])))
+    v.pack_far = swap(v.pack, ZL)
+    v.a0 = join(w_query, w_key, w_value)
+    a_rows = v.a0.shape[0]
+    v.w_gate, v.w_up, v.w_down, v.w_output = w_gate, w_up, w_down, w_output
+    v.got_x = swap(join(v.a0, w_gate), SUB)
+    v.got_y = swap(join(w_output, w_up), MID)
+    v.ao = swap(join(v.a0, w_output), ZH)
+    v.own_x = own_x
+    v.x_far = swap(v.own_x, ZL)
+    v.cut()
+
+    v.g0x, v.u0y = v.got_x[a_rows:], v.got_y[head_rows:]
+    v.a1, v.o1 = v.ao[:a_rows], v.ao[a_rows:]
+    v.o0s = join(v.pop.w_output, v.got_y[:head_rows], v.a1)
+    v.a0s = join(v.pop.a0, v.got_x[:a_rows], v.o1)
+    v.o0t, v.a0t = swap(v.o0s, SUB), swap(v.a0s, MID)
+    packs = jnp.concatenate([v.pop.pack, v.pop.pack_far], 1)
+    packs = jnp.concatenate([packs, swap(packs, CORE)], 1)
+    v.packs = jnp.pad(packs, ((0, 15), (0, width - packs.shape[1])))
+    v.gate_low = swap(join(v.w_gate[:second], v.packs), ZH)
+    v.x_core, v.x_far_core = swap(v.own_x, CORE), swap(v.x_far, CORE)
+    del v.ao, v.got_x, v.got_y
+    v.cut()
+
+    packs = jnp.concatenate([v.packs[:, :1024], v.gate_low[second:, :1024]], 1)
+    v.o1s = join(v.pop.o1, v.a0t[2 * a_rows :], packs)
+    v.a1s = join(v.pop.a1, v.o0t[2 * head_rows :], packs)
+    v.o1t, v.a1t = swap(v.o1s, SUB), swap(v.a1s, MID)
+    v.gate_high = swap(v.w_gate[second:], ZH)
+    v.packs_near = packs[:1]
+    v.packs_across = lax.ppermute(packs[:1], (MID, SUB), [(at, 3 - at) for at in range(4)])
+    lengths = v.pop.packs[0, :1024].reshape(2, 2, 256)
+    lengths = lengths[:, :, 2 * gain_width : 2 * gain_width + micro * packed]
+    lengths_all = lengths.transpose(1, 0, 2).reshape(4 * micro, packed).astype(jnp.int32)
+    segment, v.cosine, v.sine = tables(lengths_all, row_count)
+    v.segment = segment.reshape(4, micro, row_count)
+    v.x = (v.own_x, v.pop.x_core, v.pop.x_far, v.pop.x_far_core)
+    v.cut()
+
+    v.u0s, v.g0s = join(v.w_up, v.pop.u0y), join(v.w_gate, v.pop.g0x)
+    v.u0t, v.g0t = swap(v.u0s, SUB), swap(v.g0s, MID)
+    v.u1 = swap(v.w_up, ZH)
+    a_parts = (v.pop.a0s, v.pop.a0t, v.pop.a1s, v.pop.a1t)
+    o_parts = (v.pop.o0s, v.pop.o0t, v.pop.o1s, v.pop.o1t)
+    kv_own = join(
+        *(one[: 2 * a_rows].reshape(2, a_rows, width)[:, head_rows:] for one in a_parts)
+    )
+    kv_core = swap(kv_own, CORE)
+    packs = join(
+        v.pop.packs_near, o_parts[3][-16:-15], a_parts[3][-16:-15], v.pop.packs_across
+    )
+    gains_rel = packs.reshape(2, 2, 2, 2, 2, 256)[..., : 2 * gain_width]
+    gains_rel = gains_rel.transpose(2, 4, 0, 3, 1, 5)
+    gains_all = dot(ordered, gains_rel.reshape(32, 2 * gain_width))
+    v.gain_one = gains_all[:, :gain_width].reshape(1, width)
+    v.gain_two = gains_all[:, gain_width:].reshape(1, width)
+    attn = attn_forward(
+        v.x,
+        v.gain_one,
+        v.cosine,
+        v.sine,
+        v.segment,
+        moved,
+        kv_own,
+        kv_core,
+        a_parts,
+        o_parts,
+        head_rows,
+        row_count,
+    )
+    v.hidden_one, v.qkv, v.mixed, v.part_send, v.part_keep, v.wqkv, v.full_o = attn
+    v.cut()
+
+    v.g1 = join(v.gate_low[:second], v.pop.gate_high)
+    del v.gate_low
+    v.got_x = swap(join(v.g1, v.w_down[:first]), SUB)
+    v.got_y = swap(join(v.u1, v.w_down[first:]), MID)
+    v.da1 = swap(v.w_down[:first], ZH)
+    v.part_got = swap(v.pop.part_send, CORE)
+    mid_far = pair_sum(v.part_keep, v.part_got, 1).astype(BF16)
+    v.mid_far = swap(mid_far, ZL)
+    v.cut()
+
+    v.dax, v.dby = v.got_x[units_own:], v.got_y[units_own:]
+    v.g1s, v.u1s = join(v.pop.g1, v.got_x[:units_own]), join(v.pop.u1, v.got_y[:units_own])
+    v.g1t, v.u1t = swap(v.g1s, MID), swap(v.u1s, SUB)
+    v.resid_mid = up32(v.own_x) + (
+        pair_sum(v.pop.part_keep, v.pop.part_got, 0) + up32(v.pop.mid_far)
+    )
+    v.db1 = swap(v.w_down[first:], ZH)
+    h_own = norm_forward(v.resid_mid, v.gain_two)[2]
+    v.h_far, v.h_core = swap(h_own, ZL), swap(h_own, CORE)
+    v.h_own = h_own
+    del v.got_x, v.got_y
+    v.cut()
+
+    v.db0s = join(v.w_down[first:], v.pop.dby, v.da1)
+    v.da0s = join(v.w_down[:first], v.pop.dax, v.db1)
+    v.db0t, v.da0t = swap(v.db0s, SUB), swap(v.da0s, MID)
+    v.g_far, v.g_core = swap(v.own_g, ZL), swap(v.own_g, CORE)
+    v.h = (v.pop.h_own, v.pop.h_core, v.h_far, swap(v.h_far, CORE))
+    del v.w_gate, v.w_up, v.w_down, v.h_far
+    v.gate_parts = (v.pop.g0s, v.pop.g0t, v.pop.g1s, v.pop.g1t)
+    v.up_parts = (v.pop.u0s, v.pop.u0t, v.pop.u1s, v.pop.u1t)
+    v.inner, v.dgate, v.dup = units(v.h, v.gate_parts, v.up_parts)
+    v.cut()
+
+    v.da1s = join(v.pop.da1, v.db0t[2 * second :])
+    v.db1s = join(v.pop.db1, v.da0t[2 * first :])
+    v.da1t, v.db1t = swap(v.da1s, MID), swap(v.db1s, SUB)
+    v.g = (v.own_g, v.pop.g_core, v.g_far, swap(v.g_far, CORE))
+    del v.g_far
+    v.dg = weight_grad(v.inner, v.g, "down_grad")
+    v.cut()
+
+    def step_one(grads):
+        keep_a, send_a, keep_b, send_b = grads
+        return (keep_a, swap(send_a, MID), keep_b, swap(send_b, SUB))
+
+    def sums_one(pairs):
+        keep_a, got_a, keep_b, got_b = pairs
+        far = slice(2, 4)
+        return pairs + (
+            pair_sum(keep_a, got_a, far).astype(BF16),
+            pair_sum(keep_b, got_b, far).astype(BF16),
+        )
+
+    def step_two(pairs):
+        return pairs[:4] + (swap(pairs[4], SUB), swap(pairs[5], MID))
+
+    def half_sum(pairs, side, at):
+        keep, got, two = pairs[2 * side], pairs[2 * side + 1], pairs[4 + side]
+        return pair_sum(keep, got, at) + up32(two[at])
+
+    def step_three(pairs, side):
+        return pairs + (swap(half_sum(pairs, side, 1).astype(BF16), ZH),)
+
+    def total(pairs):
+        sides = [half_sum(pairs, side, 0) + up32(pairs[6 + side]) for side in range(2)]
+        return jnp.concatenate(sides, 1)
+
+    def gain_step(name):
+        at = 1 + AXES.index(name)
+        low, high = jnp.split(v.gain_grads, 2, at)
+        mine = jnp.where(place[name] == 0, low, high)
+        sent = jnp.where(place[name] == 0, high, low)
+        v.gain_grads = mine + swap(sent, name)
+
+    def near_of(keep, got, micro_at):
+        here = slice(micro_at * row_count, (micro_at + 1) * row_count)
+        return up32(keep[0, here]) + up32(got)
+
+    def far_of(keep, got, micro_at):
+        here = slice(micro_at * row_count, (micro_at + 1) * row_count)
+        return (up32(keep[1, here]) + up32(got)).astype(BF16)
+
+    def mid_grads(micro_at, far):
+        here = slice(micro_at * row_count, (micro_at + 1) * row_count)
+        gh2 = near_of(v.gh2_keep, v.gh2_near[micro_at], micro_at) + up32(far)
+        resid = v.resid_mid[here]
+        inverse = lax.rsqrt(jnp.mean(resid * resid, -1, keepdims=True) + EPS)
+        normed = resid * inverse
+        grad_mid = up32(v.own_g[here]) + norm_backward(gh2, normed, inverse, v.gain_two)
+        return grad_mid, grad_mid.astype(BF16), jnp.sum(gh2 * normed, 0, keepdims=True)
+
+    v.dg = step_one(v.dg)
+    v.down_parts = (
+        *(v.pop.da0s, v.pop.da0t, v.pop.da1s, v.pop.da1t),
+        *(v.pop.db0s, v.pop.db0t, v.pop.db1s, v.pop.db1t),
+    )
+    v.gg, v.gu = unit_grads(v.pop.g, v.down_parts, v.pop.dgate, v.pop.dup, first)
+    *send, v.gh2_keep = sum_rows(
+        (v.gg, v.gu), (*v.pop.gate_parts, *v.pop.up_parts), "hidden_grads"
+    )
+    v.gh2_near = tuple(send[:2])
+    v.gh2_far = (swap(send[2], CORE), swap(send[3], CORE))
+    v.cut()
+    v.dg = sums_one(v.dg)
+    v.cut()
+
+    v.dg = step_two(v.dg)
+    v.gh2_zero = swap(far_of(v.gh2_keep, v.gh2_far[0], 0), ZL)
+    v.gh2_near = tuple(swap(one, CORE) for one in v.gh2_near)
+    v.gw = weight_grad(v.pop.gg, v.h, "gate_grad")
+    v.cut()
+
+    v.gw = step_one(v.gw)
+    v.gh2_one = swap(far_of(v.gh2_keep, v.gh2_far[1], 1), ZL)
+    v.grad_mid0, v.gb0, v.mlp_terms = mid_grads(0, v.pop.gh2_zero)
+    v.gb0_far = swap(v.gb0, ZL)
+    v.dg = step_three(v.dg, 0)
+    v.uw = weight_grad(v.pop.gu, v.pop.h, "up_grad")
+    v.out_send, v.out_keep = sum_rows((v.pop.inner,), v.pop.down_parts, "block_out", first)
+    v.cut()
+
+    v.grad_mid1, v.gb1, terms = mid_grads(1, v.pop.gh2_one)
+    v.mlp_terms = v.mlp_terms + terms
+    v.gb1_far = swap(v.gb1, ZL)
+    del v.gh2_keep, v.gh2_near, v.gh2_far
+    v.gw = step_two(sums_one(v.gw))
+    v.dg = step_three(v.dg, 1)
+    v.out_got = swap(v.pop.out_send, CORE)
+    v.cut()
+
+    v.uw = step_one(v.uw)
+    v.gw = step_three(v.gw, 0)
+    v.out_far = swap(pair_sum(v.out_keep, v.out_got, 1).astype(BF16), ZL)
+    gb = (v.pop.gb0, v.pop.gb1), (v.pop.gb0_far, v.pop.gb1_far)
+    v.gb = tuple(
+        one for rows in gb for one in (*rows, *(swap(piece, CORE) for piece in rows))
+    )
+    v.gqkv, attn_terms, *send, v.gh1_keep = attn_backward(
+        v.gb,
+        v.pop.x,
+        v.pop.qkv,
+        v.pop.cosine,
+        v.pop.sine,
+        v.pop.segment,
+        v.pop.wqkv,
+        v.pop.full_o,
+        row_count,
+    )
+    v.gh1_near = tuple(send[:2])
+    v.gh1_far = (swap(send[2], CORE), swap(send[3], CORE))
+    gain_grads = join(attn_terms, v.pop.mlp_terms)
+    v.gain_grads = gain_grads.reshape(2, 2, 2, 2, 2, 2, gain_width)
+    v.cut()
+    v.uw = sums_one(v.uw)
+    v.cut()
+
+    v.uw = step_two(v.uw)
+    v.gh1_zero = swap(far_of(v.gh1_keep, v.gh1_far[0], 0), ZL)
+    v.gh1_near = tuple(swap(one, CORE) for one in v.gh1_near)
+    v.gw = step_three(v.gw, 1)
+    v.aw = attn_grads(
+        v.pop.gqkv, v.pop.hidden_one, v.pop.mixed, v.pop.gb, moved, head_rows, kv_rows
+    )
+    gain_step(CORE)
+    v.cut()
+
+    v.aw = step_one(v.aw)
+    v.gh1_one = swap(far_of(v.gh1_keep, v.gh1_far[1], 1), ZL)
+    v.uw = step_three(v.uw, 0)
+    gain_step(ZH)
+    v.block_out = (
+        v.pop.resid_mid + (pair_sum(v.pop.out_keep, v.pop.out_got, 0) + up32(v.pop.out_far))
+    ).astype(BF16)
+    v.down_grad = total(v.pop.dg)
+    v.gate_grad = total(v.pop.gw)
+    v.cut()
+    v.aw = sums_one(v.aw)
+    v.cut()
+
+    v.aw = step_two(v.aw)
+    v.uw = step_three(v.uw, 1)
+    gain_step(ZL)
+    gain_step(MID)
+    gh1 = join(
+        near_of(v.gh1_keep, v.gh1_near[0], 0) + up32(v.pop.gh1_zero),
+        near_of(v.gh1_keep, v.gh1_near[1], 1) + up32(v.pop.gh1_one),
+    )
+    del v.gh1_keep, v.gh1_near, v.gh1_far
+    x_f32 = up32(v.own_x)
+    inverse_one = lax.rsqrt(jnp.mean(x_f32 * x_f32, -1, keepdims=True) + EPS)
+    v.input_grad = (
+        join(v.pop.grad_mid0, v.pop.grad_mid1)
+        + norm_backward(gh1, x_f32 * inverse_one, inverse_one, v.gain_one)
+    ).astype(BF16)
+    v.cut()
+
+    aw = step_three(step_three(v.aw, 0), 1)
+    v.up_grad = total(v.pop.uw)
+    gain_step(SUB)
+    grads = total(aw)
+    kv_grads = grads[head_rows:qkv_rows] + swap(grads[qkv_rows : qkv_rows + 2 * kv_rows], CORE)
+    return (
+        v.block_out.reshape(block_input.shape),
+        v.input_grad.reshape(block_input.shape),
+        v.gain_grads[0].reshape(gain_width),
+        grads[:head_rows],
+        kv_grads[:kv_rows],
+        kv_grads[kv_rows:],
+        grads[qkv_rows + 2 * kv_rows :],
+        v.gain_grads[1].reshape(gain_width),
+        v.gate_grad,
+        v.up_grad,
+        v.down_grad,
+    )
 
 
 def positions(lengths_row, row_count):
@@ -67,13 +1004,13 @@
     return jnp.dot(activity, weight, preferred_element_type=jnp.float32)
 
 
-def norm_forward(values, gain_row):
+def general_norm_forward(values, gain_row):
     inverse = lax.rsqrt(jnp.mean(values * values, -1, keepdims=True) + EPS)
     normed = values * inverse
     return (normed, inverse, (normed * gain_row.astype(jnp.float32)).astype(jnp.bfloat16))
 
 
-def norm_backward(grad_hidden, normed, inverse, gain_row):
+def general_norm_backward(grad_hidden, normed, inverse, gain_row):
     grad_normed = grad_hidden * gain_row.astype(jnp.float32)
     return inverse * (grad_normed - normed * jnp.mean(grad_normed * normed, -1, keepdims=True))
 
@@ -94,7 +1031,7 @@
     offsets, allowed = positions(lengths_row, row_count)
     cosine, sine_table = rotary_tables(offsets, HEAD_DIM)
     resid_in = block_rows.astype(jnp.float32)
-    normed_one, inverse_one, hidden_one = norm_forward(resid_in, attn_gain)
+    normed_one, inverse_one, hidden_one = general_norm_forward(resid_in, attn_gain)
     query_lin = project(hidden_one, w_query).reshape(row_count, query_heads, HEAD_DIM)
     key_lin = project(hidden_one, w_key).reshape(row_count, key_heads, HEAD_DIM)
     value_rows = (
@@ -115,7 +1052,7 @@
     mixed = jnp.einsum("hgqk,khd->qhgd", prob_low, value_rows, preferred_element_type=jnp.float32)
     mixed = mixed.astype(jnp.bfloat16).reshape(row_count, query_heads * HEAD_DIM)
     resid_mid = resid_in + apply_rows(mixed, w_output)
-    normed_two, inverse_two, hidden_two = norm_forward(resid_mid, mlp_gain)
+    normed_two, inverse_two, hidden_two = general_norm_forward(resid_mid, mlp_gain)
     gate_rows = project(hidden_two, w_gate)
     up_rows = project(hidden_two, w_up)
     inner = (jax.nn.silu(gate_rows) * up_rows).astype(jnp.bfloat16)
@@ -173,7 +1110,7 @@
     ).astype(jnp.bfloat16)
     grad_up = (grad_inner * silu_gate).astype(jnp.bfloat16)
     grad_hidden_two = apply_rows(grad_gate, w_gate) + apply_rows(grad_up, w_up)
-    grad_mid = grad_out + norm_backward(grad_hidden_two, normed_two, inverse_two, mlp_gain)
+    grad_mid = grad_out + general_norm_backward(grad_hidden_two, normed_two, inverse_two, mlp_gain)
     grad_branch = grad_mid.astype(jnp.bfloat16)
     grad_mixed = project(grad_branch, w_output).astype(jnp.bfloat16).reshape(query_rot.shape)
     scores = attention_scores(query_rot, key_rot, allowed)
@@ -208,7 +1145,7 @@
         + apply_rows(grad_value, w_value)
     )
     grad_input = (
-        grad_mid + norm_backward(grad_hidden_one, normed_one, inverse_one, attn_gain)
+        grad_mid + general_norm_backward(grad_hidden_one, normed_one, inverse_one, attn_gain)
     ).astype(jnp.bfloat16)
     gain_terms = jnp.stack(
         [jnp.sum(grad_hidden_one * normed_one, 0), jnp.sum(grad_hidden_two * normed_two, 0)]
@@ -236,7 +1173,7 @@
     )
 
 
-def on_device(
+def on_device_general(
     block_input,
     out_grad,
     seq_lengths,
@@ -256,29 +1193,29 @@
     gain_total = jnp.zeros((2, block_input.shape[2]), jnp.float32)
     for batch_index in range(block_input.shape[0]):
         forward_layer = (
-            lax.all_gather(attn_gain, ("dp", "sub"), axis=0, tiled=True),
-            lax.all_gather(w_query, ("dp", "sub"), axis=0, tiled=True),
-            lax.all_gather(w_key, ("dp", "sub"), axis=0, tiled=True),
-            lax.all_gather(w_value, ("dp", "sub"), axis=0, tiled=True),
-            lax.all_gather(w_output, ("dp", "sub"), axis=0, tiled=True),
-            lax.all_gather(mlp_gain, ("dp", "sub"), axis=0, tiled=True),
-            lax.all_gather(w_gate, ("dp", "sub"), axis=0, tiled=True),
-            lax.all_gather(w_up, ("dp", "sub"), axis=0, tiled=True),
-            lax.all_gather(w_down, ("dp", "sub"), axis=0, tiled=True),
+            lax.all_gather(attn_gain, DEVICES, axis=0, tiled=True),
+            lax.all_gather(w_query, DEVICES, axis=0, tiled=True),
+            lax.all_gather(w_key, DEVICES, axis=0, tiled=True),
+            lax.all_gather(w_value, DEVICES, axis=0, tiled=True),
+            lax.all_gather(w_output, DEVICES, axis=0, tiled=True),
+            lax.all_gather(mlp_gain, DEVICES, axis=0, tiled=True),
+            lax.all_gather(w_gate, DEVICES, axis=0, tiled=True),
+            lax.all_gather(w_up, DEVICES, axis=0, tiled=True),
+            lax.all_gather(w_down, DEVICES, axis=0, tiled=True),
         )
         block_out, saved = forward_pass(
             block_input[batch_index], seq_lengths[batch_index, 0], forward_layer
         )
         backward_layer = (
-            lax.all_gather(attn_gain, ("dp", "sub"), axis=0, tiled=True),
-            lax.all_gather(w_query, ("dp", "sub"), axis=0, tiled=True),
-            lax.all_gather(w_key, ("dp", "sub"), axis=0, tiled=True),
-            lax.all_gather(w_value, ("dp", "sub"), axis=0, tiled=True),
-            lax.all_gather(w_output, ("dp", "sub"), axis=0, tiled=True),
-            lax.all_gather(mlp_gain, ("dp", "sub"), axis=0, tiled=True),
-            lax.all_gather(w_gate, ("dp", "sub"), axis=0, tiled=True),
-            lax.all_gather(w_up, ("dp", "sub"), axis=0, tiled=True),
-            lax.all_gather(w_down, ("dp", "sub"), axis=0, tiled=True),
+            lax.all_gather(attn_gain, DEVICES, axis=0, tiled=True),
+            lax.all_gather(w_query, DEVICES, axis=0, tiled=True),
+            lax.all_gather(w_key, DEVICES, axis=0, tiled=True),
+            lax.all_gather(w_value, DEVICES, axis=0, tiled=True),
+            lax.all_gather(w_output, DEVICES, axis=0, tiled=True),
+            lax.all_gather(mlp_gain, DEVICES, axis=0, tiled=True),
+            lax.all_gather(w_gate, DEVICES, axis=0, tiled=True),
+            lax.all_gather(w_up, DEVICES, axis=0, tiled=True),
+            lax.all_gather(w_down, DEVICES, axis=0, tiled=True),
         )
         grad_input, stored, gain_terms = backward_pass(out_grad[batch_index], saved, backward_layer)
         block_outs.append(block_out)
@@ -318,12 +1255,12 @@
             0,
         )
 
-    owner_count = own_rows * lax.axis_size(("dp", "sub")) // own_rows
+    owner_count = own_rows * lax.axis_size(DEVICES) // own_rows
     owners = jnp.arange(owner_count, dtype=jnp.int32)
     blocks = lax.map(owner_block, owners)
     owned = lax.psum_scatter(
         blocks.reshape(owner_count * own_rows, model_width),
-        ("dp", "sub"),
+        DEVICES,
         scatter_dimension=0,
         tiled=True,
     )
@@ -358,35 +1295,17 @@
 
 
 def solution(mesh):
+    groups, sub = mesh.shape["dp"], mesh.shape["sub"]
+    rows, weight, gain = P(None, DEVICES, None), P(DEVICES, None), P(DEVICES)
+    body = on_device_general
+    if groups == 16 and sub == 2:
+        mesh = Mesh(mesh.devices.reshape(2, 2, groups // 8, 2, sub), AXES)
+        rows, weight, gain = P(None, AXES, None), P(AXES, None), P(AXES)
+        body = on_device_small
     return jax.shard_map(
-        on_device,
+        body,
         mesh=mesh,
-        in_specs=(
-            P(None, ("dp", "sub"), None),
-            P(None, ("dp", "sub"), None),
-            P(None, ("dp", "sub"), None),
-            P(("dp", "sub")),
-            P(("dp", "sub"), None),
-            P(("dp", "sub"), None),
-            P(("dp", "sub"), None),
-            P(("dp", "sub"), None),
-            P(("dp", "sub")),
-            P(("dp", "sub"), None),
-            P(("dp", "sub"), None),
-            P(("dp", "sub"), None),
-        ),
-        out_specs=(
-            P(None, ("dp", "sub"), None),
-            P(None, ("dp", "sub"), None),
-            P(("dp", "sub")),
-            P(("dp", "sub"), None),
-            P(("dp", "sub"), None),
-            P(("dp", "sub"), None),
-            P(("dp", "sub"), None),
-            P(("dp", "sub")),
-            P(("dp", "sub"), None),
-            P(("dp", "sub"), None),
-            P(("dp", "sub"), None),
-        ),
+        in_specs=(rows, rows, rows, gain) + (weight,) * 4 + (gain,) + (weight,) * 3,
+        out_specs=(rows, rows, gain) + (weight,) * 4 + (gain,) + (weight,) * 3,
         check_vma=False,
     )

time: 4270 us -> 571 us (0.13)
  waiting for transfers between devices: 3020 us -> 212 us
  matrix products: 649 us -> 0.12 us
  local copies, waits for them, and re-layouts: 433 us -> 23.3 us
  Pallas kernels: 0 us -> 169 us
  starting transfers between devices: 0.3 us -> 87 us
  loops' own time: 63.6 us -> 0 us
    unnamed x9 -> x0, waiting for transfers between devices: 2420 us -> none
    dot_general x264 -> x1, matrix products: 649 us -> 0.12 us  [dot(): return lax.dot_general(a, b, dims, preferred_element_type=F32)]
    all_gather x7 -> x0, waiting for transfers between devices: 596 us -> none  [the longest x1 137 us: on_device(): lax.all_gather(w_gate, ('dp', 'sub'), axis=0, tiled=True)]
    ppermute x0 -> x87, waiting for transfers between devices: none -> 212 us  [the longest x86 212 us: swap(): return lax.ppermute(value, axis, [(0, 1), (1, 0)])]
    dynamic_update_slice x32 -> x0, local copies, waits for them, and re-layouts: 182 us -> none  [on_device(): blocks = lax.map(owner_block, owners)]
    pallas_call x0 -> x10, Pallas kernels: none -> 169 us  [the longest x2 38.7 us: sum_rows(): call(functools.partial(sum_kernel, len(lefts), first), name, (4,), [pl.Bl...]
    reshape x5, local copies, waits for them, and re-layouts: 147 us -> 1.5 us  [the longest x1 0.71 us: on_device_small(): v.gain_grads = gain_grads.reshape(2, 2, 2, 2, 2, 2, gain_width)]
    ppermute x0 -> x87, starting transfers between devices: none -> 87 us  [the longest x86 85.8 us: swap(): return lax.ppermute(value, axis, [(0, 1), (1, 0)])]
  transfers between devices with their start and end apart: 8 -> 87, of which waited for: 8 -> 28; matrix products, arithmetic and copies ran while one was open for 2% -> 11% of each run, Pallas kernels for 0% -> 30%
where the time goes in v1:
time: 571 us; the launch traced here: 562 us
  waiting for transfers between devices  212 us (37%)
  Pallas kernels  169 us (30%)
  starting transfers between devices  87 us (15%)
  other arithmetic  67.2 us (12%)
  local copies, waits for them, and re-layouts  23.3 us (4%)
    ppermute x86, waiting for transfers between devices, swap(): return lax.ppermute(value, axis, [(0, 1), (1, 0)])  212 us
    ppermute x86, starting transfers between devices, swap(): return lax.ppermute(value, axis, [(0, 1), (1, 0)])  85.8 us
    pallas_call x2, Pallas kernels, sum_rows(): call(functools.partial(sum_kernel, len(lefts), first), name, (4,), [pl.Bl...  38.7 us
    pallas_call x3, Pallas kernels, weight_grad(): call(functools.partial(weight_grad_kernel, count // 8), name, (4,), [whol...  34.3 us
    pallas_call x1, Pallas kernels, attn_forward(): call(functools.partial(attn_forward_kernel, row, head_rows), 'attn_forwar...  23.9 us
    pallas_call x1, Pallas kernels, attn_backward(): call(functools.partial(attn_backward_kernel, row), 'attn_backward', (4,),...  23.5 us
    pallas_call x1, Pallas kernels, units(): call(units_kernel, 'units', (4,), [whole(one.shape) for one in (*hidden,...  22.9 us
    pallas_call x1, Pallas kernels, unit_grads(): call(functools.partial(unit_grads_kernel, first), 'unit_grads', (4,), [wh...  14.2 us
  transfers between devices with their start and end apart: 87, of which 28 were waited for; matrix products, arithmetic and copies ran while one was open for 11% of the time, Pallas kernels for 30%

profile of v1, /device:TPU:1, one launch (start us, length us, event | category | flops | bytes accessed | tf_op | source)
XLA Modules:
  0.0 561.8 jit_solution(11989502988989725755)
XLA Ops:
  13.6 28.1 %collective-permute-done.3 = bf16[1,256]{1,0:T(2,128)(2,1)S(1)} collective-permute-done((bf16[1,256]{1,0:T(2,128)(2,1)S(1)}, bf16[1,256]{1,0:T(2,128)(2,1)S(1)}, u32[]{:S(2)}, u32[]{:S(2)}) %collective-permute-start.3) | collective-permute-done | bytes 544 | tf_op jit(solution)/shard_map/ppermute | solution.py:569
  52.9 17.5 %collective-permute-done.7 = bf16[96,2048]{1,0:T(8,128)(2,1)} collective-permute-done((bf16[96,2048]{1,0:T(8,128)(2,1)}, bf16[96,2048]{1,0:T(8,128)(2,1)}, u32[]{:S(2)}, u32[]{:S(2)}) %collective-permute-start.7) | collective-permute-done | bytes 393248 | tf_op jit(solution)/shard_map/ppermute | solution.py:569
  78.8 3.1 fusion.21
  82.5 11.1 %collective-permute-done.12 = bf16[96,2048]{1,0:T(8,128)(2,1)S(1)} collective-permute-done((bf16[96,2048]{1,0:T(8,128)(2,1)S(1)}, bf16[96,2048]{1,0:T(8,128)(2,1)S(1)}, u32[]{:S(2)}, u32[]{:S(2)}) %collective-permute-start.12) | collective-permute-done | bytes 393248 | tf_op jit(solution)/shard_map/ppermute | solution.py:569
  99.8 3.0 collective-permute-start.15
  104.4 23.9 %attn_forward.1 = (bf16[1024,2048]{1,0:T(8,128)(2,1)}, bf16[1024,768]{1,0:T(8,128)(2,1)}, bf16[1024,512]{1,0:T(8,128)(2,1)}, bf16[2,256,2048]{2,1,0:T(8,128)(2,1...) custom-call(bf16[256,2048]{1,0:T(8,128)(2,1)} %bitcast.112, ...), custom_call_target="tpu_custom_call" | custom-call | flops 1000 | bytes 1000 | tf_op jit(solution)/shard_map/attn_forward/pallas_call | solution.py:256
  130.5 2.9 collective-permute-start.22
  139.9 28.7 %collective-permute-done.19 = bf16[96,2048]{1,0:T(8,128)(2,1)S(1)} collective-permute-done((bf16[96,2048]{1,0:T(8,128)(2,1)S(1)}, bf16[96,2048]{1,0:T(8,128)(2,1)S(1)}, u32[]{:S(2)}, u32[]{:S(2)}) %collective-permute-start.19) | collective-permute-done | bytes 393248 | tf_op jit(solution)/shard_map/ppermute | solution.py:569
  179.3 25.3 %collective-permute-done.24 = bf16[80,2048]{1,0:T(8,128)(2,1)S(1)} collective-permute-done((bf16[80,2048]{1,0:T(8,128)(2,1)S(1)}, bf16[80,2048]{1,0:T(8,128)(2,1)S(1)}, u32[]{:S(2)}, u32[]{:S(2)}) %collective-permute-start.24) | collective-permute-done | bytes 327712 | tf_op jit(solution)/shard_map/ppermute | solution.py:569
  215.0 22.9 %units.1 = (bf16[1024,1408]{1,0:T(8,128)(2,1)}, bf16[1024,1408]{1,0:T(8,128)(2,1)}, bf16[1024,1408]{1,0:T(8,128)(2,1)}) custom-call(bf16[256,2048]{1,0:T(8,128)(2,1)} %copy-done.3, bf16[256,2048]{1,0:T(8,128)(2,1)} %copy-done.11, bf16[256,2048]{1,0:T(8,128)(2,1)} %copy-done.10, bf16[256,2048]{1,0:T(8,128)(2,1)} %copy-done.12, bf16[352,2048]{1,0:T(8,128)(2,1)} %copy-done.13, ...), custom_call_target="tpu_custom_call" | custom-call | flops 1000 | bytes 1000 | tf_op jit(solution)/shard_map/units/pallas_call | solution.py:376
  243.9 11.5 %down_grad.1 = (bf16[4,176,1024]{2,1,0:T(8,128)(2,1)}, bf16[4,176,1024]{2,1,0:T(8,128)(2,1)}, bf16[4,176,1024]{2,1,0:T(8,128)(2,1)}, bf16[4,176,1024]{2,1,0:T(8,128)(2,1)}) custom-call(bf16[1024,1408]{1,0:T(8,128)(2,1)} %get-tuple-element.1063.l_ref.refs_0_, bf16[256,2048]{1,0:T(8,128)(2,1)} %bitcast.120, bf16[256,2048]{1,0:T(8,128)(2,1)} %collective-permute-done.32.refs_1_, ...), custom_call_target="tpu_custom_call" | custom-call | flops 1000 | bytes 1000 | tf_op jit(solution)/shard_map/down_grad/pallas_call | solution.py:503
  256.3 2.5 collective-permute-done.34.refs_9_.refs_4_
  260.5 14.2 %unit_grads.1 = (bf16[1024,1408]{1,0:T(8,128)(2,1)}, bf16[1024,1408]{1,0:T(8,128)(2,1)}) custom-call(bf16[256,2048]{1,0:T(8,128)(2,1)} %bitcast.121, bf16[256,2048]{1,0:T(8,128)(2,1)} %collective-permute-done.32.refs_1_, bf16[256,2048]{1,0:T(8,128)(2,1)} %collective-permute-done.33.refs_2_, bf16[256,2048]{1,0:T(8,128)(2,1)} %copy-done.28, ...), custom_call_target="tpu_custom_call" | custom-call | flops 1000 | bytes 1000 | tf_op jit(solution)/shard_map/unit_grads/pallas_call | solution.py:406
  274.7 23.7 %hidden_grads.1 = (bf16[128,2048]{1,0:T(8,128)(2,1)}, bf16[128,2048]{1,0:T(8,128)(2,1)}, bf16[128,2048]{1,0:T(8,128)(2,1)}, bf16[128,2048]{1,0:T(8,128)(2,1)}, bf16[2,256,2048]{2,1,0:T(8,128)(2,1)}) custom-call(bf16[1024,1408]{1,0:T(8,128)(2,1)} %get-tuple-element.1017.refs_0_.l_ref, bf16[1024,1408]{1,0:T(8,128)(2,1)} %get-tuple-element.1078.refs_1_.l_ref, ...), custom_call_target="tpu_custom_call" | custom-call | flops 1000 | bytes 1000 | tf_op jit(solution)/shard_map/hidden_grads/pallas_call | solution.py:456
  309.0 11.4 %gate_grad.1 = (bf16[4,176,1024]{2,1,0:T(8,128)(2,1)}, bf16[4,176,1024]{2,1,0:T(8,128)(2,1)}, bf16[4,176,1024]{2,1,0:T(8,128)(2,1)}, bf16[4,176,1024]{2,1,0:T(8,128)(2,1)}) custom-call(bf16[1024,1408]{1,0:T(8,128)(2,1)} %get-tuple-element.1017.refs_0_.l_ref, bf16[256,2048]{1,0:T(8,128)(2,1)} %copy-done.3, bf16[256,2048]{1,0:T(8,128)(2,1)} %copy-done.11, ...), custom_call_target="tpu_custom_call" | custom-call | flops 1000 | bytes 1000 | tf_op jit(solution)/shard_map/gate_grad/pallas_call | solution.py:503
  320.5 2.8 collective-permute-done.41
  331.6 11.4 %up_grad.1 = (bf16[4,176,1024]{2,1,0:T(8,128)(2,1)}, bf16[4,176,1024]{2,1,0:T(8,128)(2,1)}, bf16[4,176,1024]{2,1,0:T(8,128)(2,1)}, bf16[4,176,1024]{2,1,0:T(8,128)(2,1)}) custom-call(bf16[1024,1408]{1,0:T(8,128)(2,1)} %get-tuple-element.1078.refs_1_.l_ref, bf16[256,2048]{1,0:T(8,128)(2,1)} %copy-done.3, bf16[256,2048]{1,0:T(8,128)(2,1)} %copy-done.11, ...), custom_call_target="tpu_custom_call" | custom-call | flops 1000 | bytes 1000 | tf_op jit(solution)/shard_map/up_grad/pallas_call | solution.py:503
  343.0 15.0 %block_out.1 = (bf16[2,256,2048]{2,1,0:T(8,128)(2,1)}, bf16[2,256,2048]{2,1,0:T(8,128)(2,1)}) custom-call(bf16[1024,1408]{1,0:T(8,128)(2,1)} %get-tuple-element.1063.l_ref.refs_0_, bf16[272,2048]{1,0:T(8,128)(2,1)} %copy-done.6, bf16[272,2048]{1,0:T(8,128)(2,1)} %collective-permute-done.29.refs_7_.refs_2_, bf16[192,2048]{1,0:T(8,128)(2,1)} %copy-done.15, ...), custom_call_target="tpu_custom_call" | custom-call | flops 1000 | bytes 1000 | tf_op jit(solution)/shard_map/block_out/pallas_call | solution.py:456
  361.0 3.2 collective-permute-start.55
  371.9 16.0 %collective-permute-done.51 = bf16[176,1024]{1,0:T(8,128)(2,1)S(1)} collective-permute-done((bf16[176,1024]{1,0:T(8,128)(2,1)S(1)}, bf16[176,1024]{1,0:T(8,128)(2,1)S(1)}, u32[]{:S(2)}, u32[]{:S(2)}) %collective-permute-start.51) | collective-permute-done | bytes 360480 | tf_op jit(solution)/shard_map/ppermute | solution.py:569
  398.7 23.5 %attn_backward.1 = (bf16[1024,768]{1,0:T(8,128)(2,1)}, f32[1,2048]{1,0:T(1,128)}, bf16[128,2048]{1,0:T(8,128)(2,1)}, bf16[128,2048]{1,0:T(8,128)(2,1)}, bf16[128...) custom-call(bf16[128,2048]{1,0:T(8,128)(2,1)} %copy-done.25, ...), custom_call_target="tpu_custom_call" | custom-call | flops 1000 | bytes 1000 | tf_op jit(solution)/shard_map/attn_backward/pallas_call | solution.py:333
  422.8 3.6 collective-permute-done.62
  435.6 3.3 collective-permute-start.70
  443.6 11.9 %collective-permute-done.70 = bf16[176,1024]{1,0:T(8,128)(2,1)} collective-permute-done((bf16[176,1024]{1,0:T(8,128)(2,1)S(1)}, bf16[176,1024]{1,0:T(8,128)(2,1)}, u32[]{:S(2)}, u32[]{:S(2)}) %collective-permute-start.70) | collective-permute-done | bytes 360480 | tf_op jit(solution)/shard_map/ppermute | solution.py:569
  456.2 12.0 %attn_grads.1 = (bf16[4,160,1024]{2,1,0:T(8,128)(2,1)}, bf16[4,160,1024]{2,1,0:T(8,128)(2,1)}, bf16[4,160,1024]{2,1,0:T(8,128)(2,1)}, bf16[4,160,1024]{2,1,0:T(8,128)(2,1)}) custom-call(bf16[1024,768]{1,0:T(8,128)(2,1)} %get-tuple-element.1226.gqkv_ref, bf16[1024,2048]{1,0:T(8,128)(2,1)} %get-tuple-element.1227.hid_ref, ...), custom_call_target="tpu_custom_call" | custom-call | flops 1000 | bytes 1000 | tf_op jit(solution)/shard_map/attn_grads/pallas_call | solution.py:541
  481.7 2.8 fusion.9
  488.8 3.9 collective-permute-done.76
  492.7 10.7 %collective-permute-done.73 = bf16[4,160,1024]{2,1,0:T(8,128)(2,1)S(1)} collective-permute-done((bf16[4,160,1024]{2,1,0:T(8,128)(2,1)S(1)}, bf16[4,160,1024]{2,1,0:T(8,128)(2,1)S(1)}, u32[]{:S(2)}, u32[]{:S(2)}) %collective-permute-start.73) | collective-permute-done | bytes 1310752 | tf_op jit(solution)/shard_map/ppermute | solution.py:569
  515.8 7.6 %collective-permute-done.81 = f32[2,1,1,1,1,2,64]{6,5,4,3,2,1,0:T(2,128)S(1)} collective-permute-done((f32[2,1,1,1,1,2,64]{6,5,4,3,2,1,0:T(2,128)S(1)}, f32[2,1,1,1,1,2,64]{6,5,4,3,2,1,0:T(2,128)S(1)}, u32[]{:S(2)}, u32[]{:S(2)}) %collective-permute-start.81) | collective-permute-done | bytes 1056 | tf_op jit(solution)/shard_map/ppermute | solution.py:569
  523.3 4.1 collective-permute-done.82
  535.2 16.6 %collective-permute-done.85 = bf16[160,1024]{1,0:T(8,128)(2,1)S(1)} collective-permute-done((bf16[160,1024]{1,0:T(8,128)(2,1)S(1)}, bf16[160,1024]{1,0:T(8,128)(2,1)S(1)}, u32[]{:S(2)}, u32[]{:S(2)}) %collective-permute-start.85) | collective-permute-done | bytes 327712 | tf_op jit(solution)/shard_map/ppermute | solution.py:569
  552.0 6.8 %collective-permute-done.84 = bf16[160,1024]{1,0:T(8,128)(2,1)S(1)} collective-permute-done((bf16[160,1024]{1,0:T(8,128)(2,1)S(1)}, bf16[160,1024]{1,0:T(8,128)(2,1)S(1)}, u32[]{:S(2)}, u32[]{:S(2)}) %collective-permute-start.84) | collective-permute-done | bytes 327712 | tf_op jit(solution)/shard_map/ppermute | solution.py:569
  (509 shorter events, 174.1 us)
Async XLA Ops:
  3.1 38.7 %collective-permute-start.1 = (bf16[256,2048]{1,0:T(8,128)(2,1)}, bf16[256,2048]{1,0:T(8,128)(2,1)S(1)}, u32[]{:S(2)}, u32[]{:S(2)}) collective-permute-start(bf16[256,2048]{1,0:T(8,128)(2,1)} %pad_maximum_fusion.7), channel_id=1, source_target_pairs={{0,1},{1,0},{2,3},{3,2},{4,5},{5,4},{6,7},{7,6},{8,9},{9,8},{10,11... | collective-permute-start | bytes 3145736 | tf_op jit(solution)/shard_map/ppermute | solution.py:569
  5.2 36.6 %collective-permute-start.4 = (bf16[256,2048]{1,0:T(8,128)(2,1)S(1)}, bf16[256,2048]{1,0:T(8,128)(2,1)}, u32[]{:S(2)}, u32[]{:S(2)}) collective-permute-start(bf16[256,2048]{1,0:T(8,128)(2,1)S(1)} %bitcast.114), channel_id=1, source_target_pairs={{0,8},{8,0},{1,9},{9,1},{2,10},{10,2},{3,11},{11,3},{4,12},{12,4},... | collective-permute-start | bytes 3145736 | tf_op jit(solution)/shard_map/ppermute | solution.py:569
  8.7 33.0 %collective-permute-start.2 = (bf16[240,2048]{1,0:T(8,128)(2,1)}, bf16[240,2048]{1,0:T(8,128)(2,1)S(1)}, u32[]{:S(2)}, u32[]{:S(2)}) collective-permute-start(bf16[240,2048]{1,0:T(8,128)(2,1)} %pad_maximum_fusion.10), channel_id=1, source_target_pairs={{0,4},{4,0},{1,5},{5,1},{2,6},{6,2},{3,7},{7,3},{8,12},{12,8},{9,1... | collective-permute-start | bytes 2949128 | tf_op jit(solution)/shard_map/ppermute | solution.py:569
  10.8 30.9 %collective-permute-start = (bf16[144,2048]{1,0:T(8,128)(2,1)}, bf16[144,2048]{1,0:T(8,128)(2,1)}, u32[]{:S(2)}, u32[]{:S(2)}) collective-permute-start(bf16[144,2048]{1,0:T(8,128)(2,1)} %pad_maximum_fusion.16), channel_id=1, source_target_pairs={{0,16},{16,0},{1,17},{17,1},{2,18},{18,2},{3,19},{19,3},{4,20},{20... | collective-permute-start | bytes 1769480 | tf_op jit(solution)/shard_map/ppermute | solution.py:569
  95.8 34.7 %collective-permute-start.17 = (bf16[352,2048]{1,0:T(8,128)(2,1)S(1)}, bf16[352,2048]{1,0:T(8,128)(2,1)}, u32[]{:S(2)}, u32[]{:S(2)}) collective-permute-start(bf16[352,2048]{1,0:T(8,128)(2,1)S(1)} %constant_dynamic-update-slice_fusion.2.refs_8_.refs_6_), channel_id=1, source_target_pairs={{0,1},{1,0},{2,3},{3,2},{4,5},{5,4},{6,7},{7,6},{8,9},{9,8},{10,11... | collective-permute-start | bytes 4325384 | tf_op jit(solution)/shard_map/ppermute | solution.py:569
  96.0 34.5 %collective-permute-start.16 = (bf16[352,2048]{1,0:T(8,128)(2,1)S(1)}, bf16[352,2048]{1,0:T(8,128)(2,1)}, u32[]{:S(2)}, u32[]{:S(2)}) collective-permute-start(bf16[352,2048]{1,0:T(8,128)(2,1)S(1)} %constant_dynamic-update-slice_fusion.refs_4_.refs_2_), channel_id=1, source_target_pairs={{0,4},{4,0},{1,5},{5,1},{2,6},{6,2},{3,7},{7,3},{8,12},{12,8},{9,1... | collective-permute-start | bytes 4325384 | tf_op jit(solution)/shard_map/ppermute | solution.py:569
  98.2 32.3 %collective-permute-start.18 = (bf16[176,2048]{1,0:T(8,128)(2,1)}, bf16[176,2048]{1,0:T(8,128)(2,1)}, u32[]{:S(2)}, u32[]{:S(2)}) collective-permute-start(bf16[176,2048]{1,0:T(8,128)(2,1)} %param.22), channel_id=1, source_target_pairs={{0,16},{16,0},{1,17},{17,1},{2,18},{18,2},{3,19},{19,3},{4,20},{20... | collective-permute-start | bytes 2162696 | tf_op jit(solution)/shard_map/ppermute | solution.py:569
  135.7 32.9 %collective-permute-start.21 = (bf16[256,2048]{1,0:T(8,128)(2,1)S(1)}, bf16[256,2048]{1,0:T(8,128)(2,1)S(1)}, u32[]{:S(2)}, u32[]{:S(2)}) collective-permute-start(bf16[256,2048]{1,0:T(8,128)(2,1)S(1)} %pad_maximum_fusion.8), channel_id=1, source_target_pairs={{0,4},{4,0},{1,5},{5,1},{2,6},{6,2},{3,7},{7,3},{8,12},{12,8},{9,1... | collective-permute-start | bytes 3145736 | tf_op jit(solution)/shard_map/ppermute | solution.py:569
  135.9 32.6 %collective-permute-start.20 = (bf16[272,2048]{1,0:T(8,128)(2,1)S(1)}, bf16[272,2048]{1,0:T(8,128)(2,1)S(1)}, u32[]{:S(2)}, u32[]{:S(2)}) collective-permute-start(bf16[272,2048]{1,0:T(8,128)(2,1)S(1)} %pad_maximum_fusion.5), channel_id=1, source_target_pairs={{0,1},{1,0},{2,3},{3,2},{4,5},{5,4},{6,7},{7,6},{8,9},{9,8},{10,11... | collective-permute-start | bytes 3342344 | tf_op jit(solution)/shard_map/ppermute | solution.py:569
  137.9 32.6 %collective-permute-start.23 = (bf16[256,2048]{1,0:T(8,128)(2,1)S(1)}, bf16[256,2048]{1,0:T(8,128)(2,1)S(1)}, u32[]{:S(2)}, u32[]{:S(2)}) collective-permute-start(bf16[256,2048]{1,0:T(8,128)(2,1)S(1)} %fusion.11), channel_id=1, source_target_pairs={{0,8},{8,0},{1,9},{9,1},{2,10},{10,2},{3,11},{11,3},{4,12},{12,4},... | collective-permute-start | bytes 3145736 | tf_op jit(solution)/shard_map/ppermute | solution.py:569
  138.0 30.6 %collective-permute-start.19 = (bf16[96,2048]{1,0:T(8,128)(2,1)S(1)}, bf16[96,2048]{1,0:T(8,128)(2,1)S(1)}, u32[]{:S(2)}, u32[]{:S(2)}) collective-permute-start(bf16[96,2048]{1,0:T(8,128)(2,1)S(1)} %slice.426), channel_id=1, source_target_pairs={{0,16},{16,0},{1,17},{17,1},{2,18},{18,2},{3,19},{19,3},{4,20},{20... | collective-permute-start | bytes 1179656 | tf_op jit(solution)/shard_map/ppermute | solution.py:569
  170.8 34.9 %collective-permute-start.25 = (bf16[352,2048]{1,0:T(8,128)(2,1)S(1)}, bf16[352,2048]{1,0:T(8,128)(2,1)S(1)}, u32[]{:S(2)}, u32[]{:S(2)}) collective-permute-start(bf16[352,2048]{1,0:T(8,128)(2,1)S(1)} %pad_maximum_fusion.refs_6_.refs_4_), channel_id=1, source_target_pairs={{0,4},{4,0},{1,5},{5,1},{2,6},{6,2},{3,7},{7,3},{8,12},{12,8},{9,1... | collective-permute-start | bytes 4325384 | tf_op jit(solution)/shard_map/ppermute | solution.py:569
  173.4 32.4 %collective-permute-start.28 = (bf16[352,2048]{1,0:T(8,128)(2,1)S(1)}, bf16[352,2048]{1,0:T(8,128)(2,1)S(1)}, u32[]{:S(2)}, u32[]{:S(2)}) collective-permute-start(bf16[352,2048]{1,0:T(8,128)(2,1)S(1)} %pad_maximum_fusion.1.refs_10_.refs_8_), channel_id=1, source_target_pairs={{0,1},{1,0},{2,3},{3,2},{4,5},{5,4},{6,7},{7,6},{8,9},{9,8},{10,11... | collective-permute-start | bytes 4325384 | tf_op jit(solution)/shard_map/ppermute | solution.py:569
  175.5 30.3 %collective-permute-start.27 = (bf16[256,2048]{1,0:T(8,128)(2,1)S(1)}, bf16[256,2048]{1,0:T(8,128)(2,1)S(1)}, u32[]{:S(2)}, u32[]{:S(2)}) collective-permute-start(bf16[256,2048]{1,0:T(8,128)(2,1)S(1)} %multiply_convert_fusion.refs_0_), channel_id=1, source_target_pairs={{0,8},{8,0},{1,9},{9,1},{2,10},{10,2},{3,11},{11,3},{4,12},{12,4},... | collective-permute-start | bytes 3145736 | tf_op jit(solution)/shard_map/ppermute | solution.py:569
  176.5 29.2 %collective-permute-start.26 = (bf16[256,2048]{1,0:T(8,128)(2,1)S(1)}, bf16[256,2048]{1,0:T(8,128)(2,1)S(1)}, u32[]{:S(2)}, u32[]{:S(2)}) collective-permute-start(bf16[256,2048]{1,0:T(8,128)(2,1)S(1)} %multiply_convert_fusion.refs_0_), channel_id=1, source_target_pairs={{0,2},{2,0},{1,3},{3,1},{4,6},{6,4},{5,7},{7,5},{8,10},{10,8},{9,1... | collective-permute-start | bytes 3145736 | tf_op jit(solution)/shard_map/ppermute | solution.py:569
  209.3 28.6 %collective-permute-start.29 = (bf16[272,2048]{1,0:T(8,128)(2,1)S(1)}, bf16[272,2048]{1,0:T(8,128)(2,1)}, u32[]{:S(2)}, u32[]{:S(2)}) collective-permute-start(bf16[272,2048]{1,0:T(8,128)(2,1)S(1)} %pad_maximum_fusion.6.refs_6_.refs_1_), channel_id=1, source_target_pairs={{0,4},{4,0},{1,5},{5,1},{2,6},{6,2},{3,7},{7,3},{8,12},{12,8},{9,1... | collective-permute-start | bytes 3342344 | tf_op jit(solution)/shard_map/ppermute | solution.py:569
  258.8 44.0 %collective-permute-start.37 = (bf16[4,176,1024]{2,1,0:T(8,128)(2,1)}, bf16[4,176,1024]{2,1,0:T(8,128)(2,1)S(1)}, u32[]{:S(2)}, u32[]{:S(2)}) collective-permute-start(bf16[4,176,1024]{2,1,0:T(8,128)(2,1)} %get-tuple-element.899), channel_id=1, source_target_pairs={{0,4},{4,0},{1,5},{5,1},{2,6},{6,2},{3,7},{7,3},{8,12},{12,8},{9,1... | collective-permute-start | bytes 4325384 | tf_op jit(solution)/shard_map/ppermute | solution.py:569
  259.3 43.6 %collective-permute-start.38 = (bf16[4,176,1024]{2,1,0:T(8,128)(2,1)}, bf16[4,176,1024]{2,1,0:T(8,128)(2,1)S(1)}, u32[]{:S(2)}, u32[]{:S(2)}) collective-permute-start(bf16[4,176,1024]{2,1,0:T(8,128)(2,1)} %get-tuple-element.901), channel_id=1, source_target_pairs={{0,1},{1,0},{2,3},{3,2},{4,5},{5,4},{6,7},{7,6},{8,9},{9,8},{10,11... | collective-permute-start | bytes 4325384 | tf_op jit(solution)/shard_map/ppermute | solution.py:569
  323.5 34.6 %collective-permute-start.49 = (bf16[4,176,1024]{2,1,0:T(8,128)(2,1)}, bf16[4,176,1024]{2,1,0:T(8,128)(2,1)}, u32[]{:S(2)}, u32[]{:S(2)}) collective-permute-start(bf16[4,176,1024]{2,1,0:T(8,128)(2,1)} %get-tuple-element.1058), channel_id=1, source_target_pairs={{0,4},{4,0},{1,5},{5,1},{2,6},{6,2},{3,7},{7,3},{8,12},{12,8},{9,1... | collective-permute-start | bytes 4325384 | tf_op jit(solution)/shard_map/ppermute | solution.py:569
  324.2 33.8 %collective-permute-start.50 = (bf16[4,176,1024]{2,1,0:T(8,128)(2,1)}, bf16[4,176,1024]{2,1,0:T(8,128)(2,1)}, u32[]{:S(2)}, u32[]{:S(2)}) collective-permute-start(bf16[4,176,1024]{2,1,0:T(8,128)(2,1)} %get-tuple-element.1060), channel_id=1, source_target_pairs={{0,1},{1,0},{2,3},{3,2},{4,5},{5,4},{6,7},{7,6},{8,9},{9,8},{10,11... | collective-permute-start | bytes 4325384 | tf_op jit(solution)/shard_map/ppermute | solution.py:569
  327.0 31.1 %collective-permute-start.48 = (bf16[128,2048]{1,0:T(8,128)(2,1)S(1)}, bf16[128,2048]{1,0:T(8,128)(2,1)S(1)}, u32[]{:S(2)}, u32[]{:S(2)}) collective-permute-start(bf16[128,2048]{1,0:T(8,128)(2,1)S(1)} %get-tuple-element.1399), channel_id=1, source_target_pairs={{0,8},{8,0},{1,9},{9,1},{2,10},{10,2},{3,11},{11,3},{4,12},{12,4},... | collective-permute-start | bytes 1572872 | tf_op jit(solution)/shard_map/ppermute | solution.py:569
  327.8 30.3 %collective-permute-start.47 = (bf16[128,2048]{1,0:T(8,128)(2,1)S(1)}, bf16[128,2048]{1,0:T(8,128)(2,1)S(1)}, u32[]{:S(2)}, u32[]{:S(2)}) collective-permute-start(bf16[128,2048]{1,0:T(8,128)(2,1)S(1)} %get-tuple-element.1229.refs_0_), channel_id=1, source_target_pairs={{0,8},{8,0},{1,9},{9,1},{2,10},{10,2},{3,11},{11,3},{4,12},{12,4},... | collective-permute-start | bytes 1572872 | tf_op jit(solution)/shard_map/ppermute | solution.py:569
  360.0 29.1 %collective-permute-start.54 = (bf16[2,176,1024]{2,1,0:T(8,128)(2,1)S(1)}, bf16[2,176,1024]{2,1,0:T(8,128)(2,1)S(1)}, u32[]{:S(2)}, u32[]{:S(2)}) collective-permute-start(bf16[2,176,1024]{2,1,0:T(8,128)(2,1)S(1)} %add_convert_fusion.4), channel_id=1, source_target_pairs={{0,4},{4,0},{1,5},{5,1},{2,6},{6,2},{3,7},{7,3},{8,12},{12,8},{9,1... | collective-permute-start | bytes 2162696 | tf_op jit(solution)/shard_map/ppermute | solution.py:569
  390.9 38.3 %collective-permute-start.64 = (bf16[4,176,1024]{2,1,0:T(8,128)(2,1)}, bf16[4,176,1024]{2,1,0:T(8,128)(2,1)}, u32[]{:S(2)}, u32[]{:S(2)}) collective-permute-start(bf16[4,176,1024]{2,1,0:T(8,128)(2,1)} %get-tuple-element.1179), channel_id=1, source_target_pairs={{0,4},{4,0},{1,5},{5,1},{2,6},{6,2},{3,7},{7,3},{8,12},{12,8},{9,1... | collective-permute-start | bytes 4325384 | tf_op jit(solution)/shard_map/ppermute | solution.py:569
  392.0 37.2 %collective-permute-start.65 = (bf16[4,176,1024]{2,1,0:T(8,128)(2,1)}, bf16[4,176,1024]{2,1,0:T(8,128)(2,1)}, u32[]{:S(2)}, u32[]{:S(2)}) collective-permute-start(bf16[4,176,1024]{2,1,0:T(8,128)(2,1)} %get-tuple-element.1181), channel_id=1, source_target_pairs={{0,1},{1,0},{2,3},{3,2},{4,5},{5,4},{6,7},{7,6},{8,9},{9,8},{10,11... | collective-permute-start | bytes 4325384 | tf_op jit(solution)/shard_map/ppermute | solution.py:569
  394.4 34.8 %collective-permute-start.63 = (bf16[256,2048]{1,0:T(8,128)(2,1)}, bf16[256,2048]{1,0:T(8,128)(2,1)}, u32[]{:S(2)}, u32[]{:S(2)}) collective-permute-start(bf16[256,2048]{1,0:T(8,128)(2,1)} %fusion.12), channel_id=1, source_target_pairs={{0,8},{8,0},{1,9},{9,1},{2,10},{10,2},{3,11},{11,3},{4,12},{12,4},... | collective-permute-start | bytes 3145736 | tf_op jit(solution)/shard_map/ppermute | solution.py:569
  397.1 29.2 %collective-permute-start.62 = (bf16[176,1024]{1,0:T(8,128)(2,1)S(1)}, bf16[176,1024]{1,0:T(8,128)(2,1)}, u32[]{:S(2)}, u32[]{:S(2)}) collective-permute-start(bf16[176,1024]{1,0:T(8,128)(2,1)S(1)} %fusion.25), channel_id=1, source_target_pairs={{0,16},{16,0},{1,17},{17,1},{2,18},{18,2},{3,19},{19,3},{4,20},{20... | collective-permute-start | bytes 1081352 | tf_op jit(solution)/shard_map/ppermute | solution.py:569
  438.9 29.4 %collective-permute-start.71 = (bf16[2,176,1024]{2,1,0:T(8,128)(2,1)}, bf16[2,176,1024]{2,1,0:T(8,128)(2,1)}, u32[]{:S(2)}, u32[]{:S(2)}) collective-permute-start(bf16[2,176,1024]{2,1,0:T(8,128)(2,1)} %add_convert_fusion.3), channel_id=1, source_target_pairs={{0,1},{1,0},{2,3},{3,2},{4,5},{5,4},{6,7},{7,6},{8,9},{9,8},{10,11... | collective-permute-start | bytes 2162696 | tf_op jit(solution)/shard_map/ppermute | solution.py:569
  439.9 28.4 %collective-permute-start.72 = (bf16[2,176,1024]{2,1,0:T(8,128)(2,1)}, bf16[2,176,1024]{2,1,0:T(8,128)(2,1)}, u32[]{:S(2)}, u32[]{:S(2)}) collective-permute-start(bf16[2,176,1024]{2,1,0:T(8,128)(2,1)} %add_convert_fusion.2), channel_id=1, source_target_pairs={{0,4},{4,0},{1,5},{5,1},{2,6},{6,2},{3,7},{7,3},{8,12},{12,8},{9,1... | collective-permute-start | bytes 2162696 | tf_op jit(solution)/shard_map/ppermute | solution.py:569
  473.6 29.8 %collective-permute-start.73 = (bf16[4,160,1024]{2,1,0:T(8,128)(2,1)S(1)}, bf16[4,160,1024]{2,1,0:T(8,128)(2,1)S(1)}, u32[]{:S(2)}, u32[]{:S(2)}) collective-permute-start(bf16[4,160,1024]{2,1,0:T(8,128)(2,1)S(1)} %copy-done.92), channel_id=1, source_target_pairs={{0,4},{4,0},{1,5},{5,1},{2,6},{6,2},{3,7},{7,3},{8,12},{12,8},{9,1... | collective-permute-start | bytes 3932168 | tf_op jit(solution)/shard_map/ppermute | solution.py:569
  474.9 29.5 %collective-permute-start.74 = (bf16[4,160,1024]{2,1,0:T(8,128)(2,1)S(1)}, bf16[4,160,1024]{2,1,0:T(8,128)(2,1)S(1)}, u32[]{:S(2)}, u32[]{:S(2)}) collective-permute-start(bf16[4,160,1024]{2,1,0:T(8,128)(2,1)S(1)} %copy-done.91), channel_id=1, source_target_pairs={{0,1},{1,0},{2,3},{3,2},{4,5},{5,4},{6,7},{7,6},{8,9},{9,8},{10,11... | collective-permute-start | bytes 3932168 | tf_op jit(solution)/shard_map/ppermute | solution.py:569
  528.2 30.6 %collective-permute-start.84 = (bf16[160,1024]{1,0:T(8,128)(2,1)S(1)}, bf16[160,1024]{1,0:T(8,128)(2,1)S(1)}, u32[]{:S(2)}, u32[]{:S(2)}) collective-permute-start(bf16[160,1024]{1,0:T(8,128)(2,1)S(1)} %fusion.29), channel_id=1, source_target_pairs={{0,16},{16,0},{1,17},{17,1},{2,18},{18,2},{3,19},{19,3},{4,20},{20... | collective-permute-start | bytes 983048 | tf_op jit(solution)/shard_map/ppermute | solution.py:569
  (158 other events, 1699.1 us)

commit v2 on v1

--- a/solution.py
+++ b/solution.py
@@ -159,13 +159,17 @@
 
 def quarters(part, send_refs, keep_ref, here=slice(None)):
     step = pl.program_id(0)
-    rows = send_refs[0].shape[0]
-    for at in range(2):
-
-        @pl.when(step == at)
-        def _(at=at):
-            send_refs[2 * at][:, here] = part[:rows].astype(BF16)
-            send_refs[2 * at + 1][:, here] = part[rows:].astype(BF16)
+    near_ref, zero_ref, one_ref = send_refs
+    rows = zero_ref.shape[0]
+
+    @pl.when(step == 0)
+    def _():
+        near_ref[:, here] = part.astype(BF16)
+
+    @pl.when(step == 1)
+    def _():
+        zero_ref[:, here] = part[:rows].astype(BF16)
+        one_ref[:, here] = part[rows:].astype(BF16)
 
     @pl.when(step >= 2)
     def _():
@@ -174,10 +178,10 @@
 
 def quarters_out(tile, width):
     specs, shapes = halves_out(tile, width)
-    quarter = (tile // 2, width)
+    sizes = [(tile, width)] + [(tile // 2, width)] * 2
     return (
-        [pl.BlockSpec(quarter, lambda s: (0, 0))] * 4 + specs[1:],
-        [jax.ShapeDtypeStruct(quarter, BF16)] * 4 + shapes[1:],
+        [pl.BlockSpec(size, lambda s: (0, 0)) for size in sizes] + specs[1:],
+        [jax.ShapeDtypeStruct(size, BF16) for size in sizes] + shapes[1:],
     )
 
 
@@ -441,7 +445,7 @@
             yield here, total
 
     for here, total in pieces():
-        if len(send_refs) == 4:
+        if len(send_refs) == 3:
             quarters(total, send_refs, keep_ref, here)
         else:
             halves(total, send_refs[0], keep_ref, here)
@@ -552,6 +556,64 @@
         specs,
         shapes,
     )(gqkv, hidden, mixed, moved, *right)
+
+
+def total_kernel(ka_ref, ga_ref, kb_ref, gb_ref, ta_ref, tb_ref, *refs):
+    *last_refs, out_ref = refs
+    half = ka_ref.shape[2]
+    last = jnp.concatenate([ref[...].astype(F32) for ref in last_refs], 1)
+    a, b = (
+        keep[0].astype(F32) + got[0].astype(F32) + two[0].astype(F32)
+        for keep, got, two in ((ka_ref, ga_ref, ta_ref), (kb_ref, gb_ref, tb_ref))
+    )
+    out_ref[:, :half] = a + last[:, :half]
+    out_ref[:, half:] = b + last[:, half:]
+
+
+def total_sum(pairs):
+    _, rows, half = pairs[0].shape
+    block = pl.BlockSpec((1, rows, half), lambda s: (0, 0, 0))
+    return call(
+        total_kernel,
+        "total",
+        (1,),
+        [block] * 6 + [whole(one.shape) for one in pairs[6:]],
+        pl.BlockSpec((rows, 2 * half), lambda s: (0, 0)),
+        jax.ShapeDtypeStruct((rows, 2 * half), F32),
+    )(*pairs)
+
+
+def finish_kernel(x_ref, gain_ref, mid0_ref, mid1_ref, keep_ref, near_ref, zero_ref, one_ref,
+                  resid_ref, okeep_ref, ogot_ref, ozero_ref, oone_ref, grad_ref, out_ref):
+    rows = zero_ref.shape[0]
+    for at, far_ref, mid_ref, ofar_ref in (
+        (0, zero_ref, mid0_ref, ozero_ref),
+        (1, one_ref, mid1_ref, oone_ref),
+    ):
+        here = slice(at * rows, (at + 1) * rows)
+        x = x_ref[here].astype(F32)
+        inverse = lax.rsqrt(jnp.mean(x * x, -1, keepdims=True) + EPS)
+        grad = keep_ref[0, here].astype(F32) + near_ref[here].astype(F32)
+        grad = grad + far_ref[...].astype(F32)
+        grad = mid_ref[...] + norm_backward(grad, x * inverse, inverse, gain_ref[...])
+        grad_ref[here] = grad.astype(BF16)
+        out = okeep_ref[0, here].astype(F32) + ogot_ref[0, here].astype(F32)
+        out_ref[here] = (resid_ref[here] + (out + ofar_ref[...].astype(F32))).astype(BF16)
+
+
+def finish(x, gain, mid0, mid1, keep, near, zero, one, resid, out_keep, out_got, out_far):
+    tile, width = x.shape
+    first = pl.BlockSpec((1, tile, width), lambda s: (0, 0, 0))
+    full = lambda array: whole(array.shape)
+    return call(
+        finish_kernel,
+        "finish",
+        (1,),
+        [full(x), full(gain), full(mid0), full(mid1), first, full(near), full(zero), full(one)]
+        + [full(resid), first, first, *map(full, out_far)],
+        [pl.BlockSpec((tile, width), lambda s: (0, 0))] * 2,
+        [jax.ShapeDtypeStruct((tile, width), BF16)] * 2,
+    )(x, gain, mid0, mid1, keep, near, zero, one, resid, out_keep, out_got, *out_far)
 
 
 def norm_forward(values, gain):
@@ -788,16 +850,27 @@
     def step_two(pairs):
         return pairs[:4] + (swap(pairs[4], SUB), swap(pairs[5], MID))
 
-    def half_sum(pairs, side, at):
-        keep, got, two = pairs[2 * side], pairs[2 * side + 1], pairs[4 + side]
-        return pair_sum(keep, got, at) + up32(two[at])
-
-    def step_three(pairs, side):
-        return pairs + (swap(half_sum(pairs, side, 1).astype(BF16), ZH),)
+    def part_sum(pairs, at, low, high):
+        half = pairs[0].shape[2]
+        sums = []
+        for side in range(2):
+            here = slice(max(low - side * half, 0), min(high - side * half, half))
+            if here.start < here.stop:
+                keep, got, two = pairs[2 * side], pairs[2 * side + 1], pairs[4 + side]
+                sums.append(up32(keep[at, :, here]) + up32(got[at, :, here]) + up32(two[at, :, here]))
+        return sums[0] if len(sums) == 1 else jnp.concatenate(sums, 1)
+
+    def last_send(pairs, low, high):
+        return part_sum(pairs, 1, low, high).astype(BF16)
+
+    def step_three(pairs, send):
+        return pairs + (swap(send, ZH),)
 
     def total(pairs):
-        sides = [half_sum(pairs, side, 0) + up32(pairs[6 + side]) for side in range(2)]
-        return jnp.concatenate(sides, 1)
+        last = jnp.concatenate([up32(one) for one in pairs[6:]], 1)
+        return part_sum(pairs, 0, 0, width) + last
+
+    even, early, most = width // 2, width * 5 // 8, width * 3 // 4
 
     def gain_step(name):
         at = 1 + AXES.index(name)
@@ -806,17 +879,13 @@
         sent = jnp.where(place[name] == 0, high, low)
         v.gain_grads = mine + swap(sent, name)
 
-    def near_of(keep, got, micro_at):
-        here = slice(micro_at * row_count, (micro_at + 1) * row_count)
-        return up32(keep[0, here]) + up32(got)
-
     def far_of(keep, got, micro_at):
         here = slice(micro_at * row_count, (micro_at + 1) * row_count)
         return (up32(keep[1, here]) + up32(got)).astype(BF16)
 
     def mid_grads(micro_at, far):
         here = slice(micro_at * row_count, (micro_at + 1) * row_count)
-        gh2 = near_of(v.gh2_keep, v.gh2_near[micro_at], micro_at) + up32(far)
+        gh2 = up32(v.gh2_keep[0, here]) + up32(v.gh2_near[here]) + up32(far)
         resid = v.resid_mid[here]
         inverse = lax.rsqrt(jnp.mean(resid * resid, -1, keepdims=True) + EPS)
         normed = resid * inverse
@@ -832,24 +901,25 @@
     *send, v.gh2_keep = sum_rows(
         (v.gg, v.gu), (*v.pop.gate_parts, *v.pop.up_parts), "hidden_grads"
     )
-    v.gh2_near = tuple(send[:2])
-    v.gh2_far = (swap(send[2], CORE), swap(send[3], CORE))
+    v.gh2_near = send[0]
+    v.gh2_far = (swap(send[1], CORE), swap(send[2], CORE))
     v.cut()
     v.dg = sums_one(v.dg)
     v.cut()
 
     v.dg = step_two(v.dg)
     v.gh2_zero = swap(far_of(v.gh2_keep, v.gh2_far[0], 0), ZL)
-    v.gh2_near = tuple(swap(one, CORE) for one in v.gh2_near)
+    v.gh2_near = swap(v.gh2_near, CORE)
+    v.gh2_one = far_of(v.gh2_keep, v.gh2_far[1], 1)
     v.gw = weight_grad(v.pop.gg, v.h, "gate_grad")
     v.cut()
 
     v.gw = step_one(v.gw)
-    v.gh2_one = swap(far_of(v.gh2_keep, v.gh2_far[1], 1), ZL)
+    v.gh2_one = swap(v.gh2_one, ZL)
     v.grad_mid0, v.gb0, v.mlp_terms = mid_grads(0, v.pop.gh2_zero)
     v.gb0_far = swap(v.gb0, ZL)
-    v.dg = step_three(v.dg, 0)
-    v.uw = weight_grad(v.pop.gu, v.pop.h, "up_grad")
+    v.dg_send = last_send(v.dg, early, width)
+    v.dg = step_three(v.dg, last_send(v.dg, 0, early))
     v.out_send, v.out_keep = sum_rows((v.pop.inner,), v.pop.down_parts, "block_out", first)
     v.cut()
 
@@ -858,13 +928,16 @@
     v.gb1_far = swap(v.gb1, ZL)
     del v.gh2_keep, v.gh2_near, v.gh2_far
     v.gw = step_two(sums_one(v.gw))
-    v.dg = step_three(v.dg, 1)
+    v.dg = step_three(v.dg, v.pop.dg_send)
     v.out_got = swap(v.pop.out_send, CORE)
+    v.uw = weight_grad(v.pop.gu, v.pop.h, "up_grad")
     v.cut()
 
     v.uw = step_one(v.uw)
-    v.gw = step_three(v.gw, 0)
-    v.out_far = swap(pair_sum(v.out_keep, v.out_got, 1).astype(BF16), ZL)
+    v.gw_send = last_send(v.gw, most, width)
+    v.gw = step_three(v.gw, last_send(v.gw, 0, most))
+    v.out_zero = far_of(v.out_keep, v.out_got[1, :row_count], 0)
+    v.out_zero = swap(v.out_zero, ZL)
     gb = (v.pop.gb0, v.pop.gb1), (v.pop.gb0_far, v.pop.gb1_far)
     v.gb = tuple(
         one for rows in gb for one in (*rows, *(swap(piece, CORE) for piece in rows))
@@ -880,8 +953,8 @@
         v.pop.full_o,
         row_count,
     )
-    v.gh1_near = tuple(send[:2])
-    v.gh1_far = (swap(send[2], CORE), swap(send[3], CORE))
+    v.gh1_near = send[0]
+    v.gh1_far = (swap(send[1], CORE), swap(send[2], CORE))
     gain_grads = join(attn_terms, v.pop.mlp_terms)
     v.gain_grads = gain_grads.reshape(2, 2, 2, 2, 2, 2, gain_width)
     v.cut()
@@ -890,61 +963,66 @@
 
     v.uw = step_two(v.uw)
     v.gh1_zero = swap(far_of(v.gh1_keep, v.gh1_far[0], 0), ZL)
-    v.gh1_near = tuple(swap(one, CORE) for one in v.gh1_near)
-    v.gw = step_three(v.gw, 1)
+    v.gh1_near = swap(v.gh1_near, CORE)
+    v.gw = step_three(v.gw, v.pop.gw_send)
     v.aw = attn_grads(
         v.pop.gqkv, v.pop.hidden_one, v.pop.mixed, v.pop.gb, moved, head_rows, kv_rows
     )
+    v.gh1_one = far_of(v.gh1_keep, v.gh1_far[1], 1)
+    v.out_one = far_of(v.out_keep, v.out_got[1, row_count:], 1)
+    v.cut()
+
+    v.aw = step_one(v.aw)
+    v.gh1_one = swap(v.gh1_one, ZL)
+    v.uw_send = last_send(v.uw, early, width)
+    v.uw = step_three(v.uw, last_send(v.uw, 0, early))
+    v.cut()
+    v.aw = sums_one(v.aw)
+    v.cut()
+
+    v.aw = step_two(v.aw)
+    v.uw = step_three(v.uw, v.pop.uw_send)
+    v.out_one = swap(v.out_one, ZL)
+    gain_step(ZH)
+    v.cut()
+
+    aw = step_three(v.aw, last_send(v.aw, 0, even))
+    aw = step_three(aw, last_send(v.aw, even, width))
+    gain_step(MID)
+    gain_step(SUB)
     gain_step(CORE)
-    v.cut()
-
-    v.aw = step_one(v.aw)
-    v.gh1_one = swap(far_of(v.gh1_keep, v.gh1_far[1], 1), ZL)
-    v.uw = step_three(v.uw, 0)
-    gain_step(ZH)
-    v.block_out = (
-        v.pop.resid_mid + (pair_sum(v.pop.out_keep, v.pop.out_got, 0) + up32(v.pop.out_far))
-    ).astype(BF16)
-    v.down_grad = total(v.pop.dg)
-    v.gate_grad = total(v.pop.gw)
-    v.cut()
-    v.aw = sums_one(v.aw)
-    v.cut()
-
-    v.aw = step_two(v.aw)
-    v.uw = step_three(v.uw, 1)
     gain_step(ZL)
-    gain_step(MID)
-    gh1 = join(
-        near_of(v.gh1_keep, v.gh1_near[0], 0) + up32(v.pop.gh1_zero),
-        near_of(v.gh1_keep, v.gh1_near[1], 1) + up32(v.pop.gh1_one),
-    )
-    del v.gh1_keep, v.gh1_near, v.gh1_far
-    x_f32 = up32(v.own_x)
-    inverse_one = lax.rsqrt(jnp.mean(x_f32 * x_f32, -1, keepdims=True) + EPS)
-    v.input_grad = (
-        join(v.pop.grad_mid0, v.pop.grad_mid1)
-        + norm_backward(gh1, x_f32 * inverse_one, inverse_one, v.gain_one)
-    ).astype(BF16)
-    v.cut()
-
-    aw = step_three(step_three(v.aw, 0), 1)
-    v.up_grad = total(v.pop.uw)
-    gain_step(SUB)
+    input_grad, block_out = finish(
+        v.own_x,
+        v.gain_one,
+        v.pop.grad_mid0,
+        v.pop.grad_mid1,
+        v.pop.gh1_keep,
+        v.pop.gh1_near,
+        v.pop.gh1_zero,
+        v.pop.gh1_one,
+        v.pop.resid_mid,
+        v.pop.out_keep,
+        v.pop.out_got,
+        (v.pop.out_zero, v.pop.out_one),
+    )
+    down_grad, gate_grad, up_grad = (
+        total_sum(v.pop.dg), total_sum(v.pop.gw), total_sum(v.pop.uw)
+    )
     grads = total(aw)
     kv_grads = grads[head_rows:qkv_rows] + swap(grads[qkv_rows : qkv_rows + 2 * kv_rows], CORE)
     return (
-        v.block_out.reshape(block_input.shape),
-        v.input_grad.reshape(block_input.shape),
+        block_out.reshape(block_input.shape),
+        input_grad.reshape(block_input.shape),
         v.gain_grads[0].reshape(gain_width),
         grads[:head_rows],
         kv_grads[:kv_rows],
         kv_grads[kv_rows:],
         grads[qkv_rows + 2 * kv_rows :],
         v.gain_grads[1].reshape(gain_width),
-        v.gate_grad,
-        v.up_grad,
-        v.down_grad,
+        gate_grad,
+        up_grad,
+        down_grad,
     )
 
 

time: 571 us -> 555 us (0.972)
  waiting for transfers between devices: 212 us -> 181 us
  Pallas kernels: 169 us -> 186 us
    ppermute x86 -> x85, waiting for transfers between devices: 212 us -> 181 us  [swap(): return lax.ppermute(value, axis, [(0, 1), (1, 0)])]
    pallas_call x0 -> x4, Pallas kernels: none -> 17.3 us  [the longest x3 9.51 us: total_sum(): call(total_kernel, 'total', (1,), [block] * 6 + [whole(one.shape) for one...]
    convert_element_type x11 -> x5, other arithmetic: 14.7 us -> 7.9 us  [last_send(): return part_sum(pairs, 1, low, high).astype(BF16)]
    ppermute x86 -> x85, starting transfers between devices: 85.8 us -> 89.6 us  [swap(): return lax.ppermute(value, axis, [(0, 1), (1, 0)])]
  transfers between devices with their start and end apart: 87 -> 86, of which waited for: 28 -> 29; matrix products, arithmetic and copies ran while one was open for 11% -> 10% of each run, Pallas kernels for 30% -> 34%
where the time goes in v2:
time: 555 us; the launch traced here: 546 us
  Pallas kernels  186 us (34%)
  waiting for transfers between devices  181 us (33%)
  starting transfers between devices  90.8 us (16%)
  other arithmetic  61.8 us (11%)
  local copies, waits for them, and re-layouts  23.1 us (4%)
    ppermute x85, waiting for transfers between devices, swap(): return lax.ppermute(value, axis, [(0, 1), (1, 0)])  181 us
    ppermute x85, starting transfers between devices, swap(): return lax.ppermute(value, axis, [(0, 1), (1, 0)])  89.6 us
    pallas_call x2, Pallas kernels, sum_rows(): call(functools.partial(sum_kernel, len(lefts), first), name, (4,), [pl.Bl...  38.8 us
    pallas_call x3, Pallas kernels, weight_grad(): call(functools.partial(weight_grad_kernel, count // 8), name, (4,), [whol...  34.1 us
    pallas_call x1, Pallas kernels, attn_forward(): call(functools.partial(attn_forward_kernel, row, head_rows), 'attn_forwar...  23.8 us
    pallas_call x1, Pallas kernels, attn_backward(): call(functools.partial(attn_backward_kernel, row), 'attn_backward', (4,),...  23.4 us
    pallas_call x1, Pallas kernels, units(): call(units_kernel, 'units', (4,), [whole(one.shape) for one in (*hidden,...  22.8 us
    pallas_call x1, Pallas kernels, unit_grads(): call(functools.partial(unit_grads_kernel, first), 'unit_grads', (4,), [wh...  14.2 us
  transfers between devices with their start and end apart: 86, of which 29 were waited for; matrix products, arithmetic and copies ran while one was open for 10% of the time, Pallas kernels for 34%

profile of v2, /device:TPU:1, one launch (start us, length us, event | category | flops | bytes accessed | tf_op | source)
XLA Modules:
  0.0 545.5 jit_solution(9752489524021751540)
XLA Ops:
  13.6 28.1 %collective-permute-done.3 = bf16[1,256]{1,0:T(2,128)(2,1)S(1)} collective-permute-done((bf16[1,256]{1,0:T(2,128)(2,1)S(1)}, bf16[1,256]{1,0:T(2,128)(2,1)S(1)}, u32[]{:S(2)}, u32[]{:S(2)}) %collective-permute-start.3) | collective-permute-done | bytes 544 | tf_op jit(solution)/shard_map/ppermute | solution.py:631
  52.9 17.5 %collective-permute-done.7 = bf16[96,2048]{1,0:T(8,128)(2,1)} collective-permute-done((bf16[96,2048]{1,0:T(8,128)(2,1)}, bf16[96,2048]{1,0:T(8,128)(2,1)}, u32[]{:S(2)}, u32[]{:S(2)}) %collective-permute-start.7) | collective-permute-done | bytes 393248 | tf_op jit(solution)/shard_map/ppermute | solution.py:631
  78.8 3.1 fusion.8
  82.5 11.1 %collective-permute-done.12 = bf16[96,2048]{1,0:T(8,128)(2,1)S(1)} collective-permute-done((bf16[96,2048]{1,0:T(8,128)(2,1)S(1)}, bf16[96,2048]{1,0:T(8,128)(2,1)S(1)}, u32[]{:S(2)}, u32[]{:S(2)}) %collective-permute-start.12) | collective-permute-done | bytes 393248 | tf_op jit(solution)/shard_map/ppermute | solution.py:631
  99.8 3.0 collective-permute-start.15
  104.4 23.8 %attn_forward.1 = (bf16[1024,2048]{1,0:T(8,128)(2,1)}, bf16[1024,768]{1,0:T(8,128)(2,1)}, bf16[1024,512]{1,0:T(8,128)(2,1)}, bf16[2,256,2048]{2,1,0:T(8,128)(2,1...) custom-call(bf16[256,2048]{1,0:T(8,128)(2,1)} %bitcast.95, ...), custom_call_target="tpu_custom_call" | custom-call | flops 1000 | bytes 1000 | tf_op jit(solution)/shard_map/attn_forward/pallas_call | solution.py:260
  130.5 2.9 collective-permute-start.22
  139.9 28.7 %collective-permute-done.19 = bf16[96,2048]{1,0:T(8,128)(2,1)S(1)} collective-permute-done((bf16[96,2048]{1,0:T(8,128)(2,1)S(1)}, bf16[96,2048]{1,0:T(8,128)(2,1)S(1)}, u32[]{:S(2)}, u32[]{:S(2)}) %collective-permute-start.19) | collective-permute-done | bytes 393248 | tf_op jit(solution)/shard_map/ppermute | solution.py:631
  179.3 25.3 %collective-permute-done.24 = bf16[80,2048]{1,0:T(8,128)(2,1)S(1)} collective-permute-done((bf16[80,2048]{1,0:T(8,128)(2,1)S(1)}, bf16[80,2048]{1,0:T(8,128)(2,1)S(1)}, u32[]{:S(2)}, u32[]{:S(2)}) %collective-permute-start.24) | collective-permute-done | bytes 327712 | tf_op jit(solution)/shard_map/ppermute | solution.py:631
  215.0 22.8 %units.1 = (bf16[1024,1408]{1,0:T(8,128)(2,1)}, bf16[1024,1408]{1,0:T(8,128)(2,1)}, bf16[1024,1408]{1,0:T(8,128)(2,1)}) custom-call(bf16[256,2048]{1,0:T(8,128)(2,1)} %copy-done.3, bf16[256,2048]{1,0:T(8,128)(2,1)} %copy-done.11, bf16[256,2048]{1,0:T(8,128)(2,1)} %copy-done.10, bf16[256,2048]{1,0:T(8,128)(2,1)} %copy-done.12, bf16[352,2048]{1,0:T(8,128)(2,1)} %copy-done.13, ...), custom_call_target="tpu_custom_call" | custom-call | flops 1000 | bytes 1000 | tf_op jit(solution)/shard_map/units/pallas_call | solution.py:380
  243.8 11.4 %down_grad.1 = (bf16[4,176,1024]{2,1,0:T(8,128)(2,1)}, bf16[4,176,1024]{2,1,0:T(8,128)(2,1)}, bf16[4,176,1024]{2,1,0:T(8,128)(2,1)}, bf16[4,176,1024]{2,1,0:T(8,128)(2,1)}) custom-call(bf16[1024,1408]{1,0:T(8,128)(2,1)} %get-tuple-element.1124.l_ref.refs_0_, bf16[256,2048]{1,0:T(8,128)(2,1)} %bitcast.101, bf16[256,2048]{1,0:T(8,128)(2,1)} %collective-permute-done.32.refs_1_, ...), custom_call_target="tpu_custom_call" | custom-call | flops 1000 | bytes 1000 | tf_op jit(solution)/shard_map/down_grad/pallas_call | solution.py:507
  256.2 2.5 collective-permute-done.34.refs_9_.refs_4_
  260.5 14.2 %unit_grads.1 = (bf16[1024,1408]{1,0:T(8,128)(2,1)}, bf16[1024,1408]{1,0:T(8,128)(2,1)}) custom-call(bf16[256,2048]{1,0:T(8,128)(2,1)} %bitcast.102, bf16[256,2048]{1,0:T(8,128)(2,1)} %collective-permute-done.32.refs_1_, bf16[256,2048]{1,0:T(8,128)(2,1)} %collective-permute-done.33.refs_2_, bf16[256,2048]{1,0:T(8,128)(2,1)} %copy-done.40, ...), custom_call_target="tpu_custom_call" | custom-call | flops 1000 | bytes 1000 | tf_op jit(solution)/shard_map/unit_grads/pallas_call | solution.py:410
  274.6 23.7 %hidden_grads.1 = (bf16[256,2048]{1,0:T(8,128)(2,1)}, bf16[128,2048]{1,0:T(8,128)(2,1)}, bf16[128,2048]{1,0:T(8,128)(2,1)}, bf16[2,256,2048]{2,1,0:T(8,128)(2,1)}) custom-call(bf16[1024,1408]{1,0:T(8,128)(2,1)} %get-tuple-element.1074.refs_0_.l_ref, bf16[1024,1408]{1,0:T(8,128)(2,1)} %get-tuple-element.1177.refs_1_.l_ref, bf16[352,2048]{1,0:T(8,128)(2,1)} %copy-done.13, ...), custom_call_target="tpu_custom_call" | custom-call | flops 1000 | bytes 1000 | tf_op jit(solution)/shard_map/hidden_grads/pallas_call | solution.py:460
  310.1 11.3 %gate_grad.1 = (bf16[4,176,1024]{2,1,0:T(8,128)(2,1)}, bf16[4,176,1024]{2,1,0:T(8,128)(2,1)}, bf16[4,176,1024]{2,1,0:T(8,128)(2,1)}, bf16[4,176,1024]{2,1,0:T(8,128)(2,1)}) custom-call(bf16[1024,1408]{1,0:T(8,128)(2,1)} %get-tuple-element.1074.refs_0_.l_ref, bf16[256,2048]{1,0:T(8,128)(2,1)} %copy-done.3, bf16[256,2048]{1,0:T(8,128)(2,1)} %copy-done.11, ...), custom_call_target="tpu_custom_call" | custom-call | flops 1000 | bytes 1000 | tf_op jit(solution)/shard_map/gate_grad/pallas_call | solution.py:507
  336.9 15.1 %block_out.1 = (bf16[2,256,2048]{2,1,0:T(8,128)(2,1)}, bf16[2,256,2048]{2,1,0:T(8,128)(2,1)}) custom-call(bf16[1024,1408]{1,0:T(8,128)(2,1)} %get-tuple-element.1124.l_ref.refs_0_, bf16[272,2048]{1,0:T(8,128)(2,1)} %copy-done.6, bf16[272,2048]{1,0:T(8,128)(2,1)} %collective-permute-done.29.refs_7_.refs_2_, bf16[192,2048]{1,0:T(8,128)(2,1)} %copy-done.15, ...), custom_call_target="tpu_custom_call" | custom-call | flops 1000 | bytes 1000 | tf_op jit(solution)/shard_map/block_out/pallas_call | solution.py:460
  354.0 5.3 collective-permute-done.45.refs_0_
  370.1 2.5 fusion.40
  374.7 11.3 %up_grad.1 = (bf16[4,176,1024]{2,1,0:T(8,128)(2,1)}, bf16[4,176,1024]{2,1,0:T(8,128)(2,1)}, bf16[4,176,1024]{2,1,0:T(8,128)(2,1)}, bf16[4,176,1024]{2,1,0:T(8,128)(2,1)}) custom-call(bf16[1024,1408]{1,0:T(8,128)(2,1)} %get-tuple-element.1177.refs_1_.l_ref, bf16[256,2048]{1,0:T(8,128)(2,1)} %copy-done.3, bf16[256,2048]{1,0:T(8,128)(2,1)} %copy-done.11, ...), custom_call_target="tpu_custom_call" | custom-call | flops 1000 | bytes 1000 | tf_op jit(solution)/shard_map/up_grad/pallas_call | solution.py:507
  386.7 3.9 collective-permute-done.50.refs_1_
  404.0 23.4 %attn_backward.1 = (bf16[1024,768]{1,0:T(8,128)(2,1)}, f32[1,2048]{1,0:T(1,128)}, bf16[256,2048]{1,0:T(8,128)(2,1)}, bf16[128,2048]{1,0:T(8,128)(2,1)}, bf16[128...) custom-call(bf16[128,2048]{1,0:T(8,128)(2,1)} %copy-done.29, bf16[128,2048]{1,0:T(8,128)(2,1)} %copy-done.30, ...), custom_call_target="tpu_custom_call" | custom-call | flops 1000 | bytes 1000 | tf_op jit(solution)/shard_map/attn_backward/pallas_call | solution.py:337
  436.8 2.6 fusion.2
  443.3 12.0 %attn_grads.1 = (bf16[4,160,1024]{2,1,0:T(8,128)(2,1)}, bf16[4,160,1024]{2,1,0:T(8,128)(2,1)}, bf16[4,160,1024]{2,1,0:T(8,128)(2,1)}, bf16[4,160,1024]{2,1,0:T(8,128)(2,1)}) custom-call(bf16[1024,768]{1,0:T(8,128)(2,1)} %get-tuple-element.1283.gqkv_ref, bf16[1024,2048]{1,0:T(8,128)(2,1)} %get-tuple-element.1284.hid_ref, ...), custom_call_target="tpu_custom_call" | custom-call | flops 1000 | bytes 1000 | tf_op jit(solution)/shard_map/attn_grads/pallas_call | solution.py:545
  464.2 14.2 %collective-permute-done.73.refs_0_ = bf16[176,1280]{1,0:T(8,128)(2,1)S(1)} collective-permute-done((bf16[176,1280]{1,0:T(8,128)(2,1)S(1)}, bf16[176,1280]{1,0:T(8,128)(2,1)S(1)}, u32[]{:S(2)}, u32[]{:S(2)}) %collective-permute-start.73) | collective-permute-done | bytes 450592 | tf_op jit(solution)/shard_map/ppermute | solution.py:631
  478.5 7.1 %collective-permute-done.70 = bf16[4,160,1024]{2,1,0:T(8,128)(2,1)S(1)} collective-permute-done((bf16[4,160,1024]{2,1,0:T(8,128)(2,1)}, bf16[4,160,1024]{2,1,0:T(8,128)(2,1)S(1)}, u32[]{:S(2)}, u32[]{:S(2)}) %collective-permute-start.70) | collective-permute-done | bytes 1310752 | tf_op jit(solution)/shard_map/ppermute | solution.py:631
  494.2 11.8 %collective-permute-done.76 = f32[2,1,2,2,2,2,64]{6,5,4,3,2,1,0:T(2,128)S(1)} collective-permute-done((f32[2,1,2,2,2,2,64]{6,5,4,3,2,1,0:T(2,128)S(1)}, f32[2,1,2,2,2,2,64]{6,5,4,3,2,1,0:T(2,128)S(1)}, u32[]{:S(2)}, u32[]{:S(2)}) %collective-permute-start.76) | collective-permute-done | bytes 8224 | tf_op jit(solution)/shard_map/ppermute | solution.py:631
  514.3 5.6 %collective-permute-start.81 = (f32[2,1,2,1,1,1,64]{6,5,4,3,2,1,0:T(1,128)S(1)}, f32[2,1,2,1,1,1,64]{6,5,4,3,2,1,0:T(1,128)S(1)}, u32[]{:S(2)}, u32[]{:S(2)}) collective-permute-start(f32[2,1,2,1,1,1,64]{6,5,4,3,2,1,0:T(1,128)S(1)} %broadcast_select_fusion.4), channel_id=1, source_target_pairs={{0,2},{2,0},{1,3},{3,1},{4,6},{6,4},{5,7},{7,5},{8,10},{10,8},{9,1... | collective-permute-start | bytes 3080 | tf_op jit(solution)/shard_map/ppermute | solution.py:631
  519.9 3.2 total.3
  523.1 3.2 total.4
  526.2 3.2 total.5
  529.8 7.7 %finish.1 = (bf16[256,2048]{1,0:T(8,128)(2,1)}, bf16[256,2048]{1,0:T(8,128)(2,1)}) custom-call(bf16[256,2048]{1,0:T(8,128)(2,1)} %bitcast.97, f32[1,2048]{1,0:T(1,128)} %reshape.316.refs_4_.gain_ref, f32[128,2048]{1,0:T(8,128)} %get-tuple-element.1461.mid0_ref, f32[128,2048]{1,0:T(8,128)} %get-tuple-element.1462.mid1_ref, ...), custom_call_target="tpu_custom_call" | custom-call | flops 1000 | bytes 1000 | tf_op jit(solution)/shard_map/finish/pallas_call | solution.py:608
  538.1 3.9 collective-permute-done.84
  (498 shorter events, 177.8 us)
Async XLA Ops:
  3.1 38.7 %collective-permute-start.1 = (bf16[256,2048]{1,0:T(8,128)(2,1)}, bf16[256,2048]{1,0:T(8,128)(2,1)S(1)}, u32[]{:S(2)}, u32[]{:S(2)}) collective-permute-start(bf16[256,2048]{1,0:T(8,128)(2,1)} %pad_maximum_fusion.4), channel_id=1, source_target_pairs={{0,1},{1,0},{2,3},{3,2},{4,5},{5,4},{6,7},{7,6},{8,9},{9,8},{10,11... | collective-permute-start | bytes 3145736 | tf_op jit(solution)/shard_map/ppermute | solution.py:631
  5.2 36.6 %collective-permute-start.4 = (bf16[256,2048]{1,0:T(8,128)(2,1)S(1)}, bf16[256,2048]{1,0:T(8,128)(2,1)}, u32[]{:S(2)}, u32[]{:S(2)}) collective-permute-start(bf16[256,2048]{1,0:T(8,128)(2,1)S(1)} %bitcast.98), channel_id=1, source_target_pairs={{0,8},{8,0},{1,9},{9,1},{2,10},{10,2},{3,11},{11,3},{4,12},{12,4},... | collective-permute-start | bytes 3145736 | tf_op jit(solution)/shard_map/ppermute | solution.py:631
  8.7 33.0 %collective-permute-start.2 = (bf16[240,2048]{1,0:T(8,128)(2,1)}, bf16[240,2048]{1,0:T(8,128)(2,1)S(1)}, u32[]{:S(2)}, u32[]{:S(2)}) collective-permute-start(bf16[240,2048]{1,0:T(8,128)(2,1)} %pad_maximum_fusion.7), channel_id=1, source_target_pairs={{0,4},{4,0},{1,5},{5,1},{2,6},{6,2},{3,7},{7,3},{8,12},{12,8},{9,1... | collective-permute-start | bytes 2949128 | tf_op jit(solution)/shard_map/ppermute | solution.py:631
  10.8 30.9 %collective-permute-start = (bf16[144,2048]{1,0:T(8,128)(2,1)}, bf16[144,2048]{1,0:T(8,128)(2,1)}, u32[]{:S(2)}, u32[]{:S(2)}) collective-permute-start(bf16[144,2048]{1,0:T(8,128)(2,1)} %pad_maximum_fusion.13), channel_id=1, source_target_pairs={{0,16},{16,0},{1,17},{17,1},{2,18},{18,2},{3,19},{19,3},{4,20},{20... | collective-permute-start | bytes 1769480 | tf_op jit(solution)/shard_map/ppermute | solution.py:631
  13.3 28.4 %collective-permute-start.3 = (bf16[1,256]{1,0:T(2,128)(2,1)S(1)}, bf16[1,256]{1,0:T(2,128)(2,1)S(1)}, u32[]{:S(2)}, u32[]{:S(2)}) collective-permute-start(bf16[1,256]{1,0:T(2,128)(2,1)S(1)} %pad.8), channel_id=1, source_target_pairs={{0,8},{8,0},{1,9},{9,1},{2,10},{10,2},{3,11},{11,3},{4,12},{12,4},... | collective-permute-start | bytes 1544 | tf_op jit(solution)/shard_map/ppermute | solution.py:631
  95.8 34.7 %collective-permute-start.17 = (bf16[352,2048]{1,0:T(8,128)(2,1)S(1)}, bf16[352,2048]{1,0:T(8,128)(2,1)}, u32[]{:S(2)}, u32[]{:S(2)}) collective-permute-start(bf16[352,2048]{1,0:T(8,128)(2,1)S(1)} %constant_dynamic-update-slice_fusion.2.refs_8_.refs_6_), channel_id=1, source_target_pairs={{0,1},{1,0},{2,3},{3,2},{4,5},{5,4},{6,7},{7,6},{8,9},{9,8},{10,11... | collective-permute-start | bytes 4325384 | tf_op jit(solution)/shard_map/ppermute | solution.py:631
  96.0 34.5 %collective-permute-start.16 = (bf16[352,2048]{1,0:T(8,128)(2,1)S(1)}, bf16[352,2048]{1,0:T(8,128)(2,1)}, u32[]{:S(2)}, u32[]{:S(2)}) collective-permute-start(bf16[352,2048]{1,0:T(8,128)(2,1)S(1)} %constant_dynamic-update-slice_fusion.refs_4_.refs_2_), channel_id=1, source_target_pairs={{0,4},{4,0},{1,5},{5,1},{2,6},{6,2},{3,7},{7,3},{8,12},{12,8},{9,1... | collective-permute-start | bytes 4325384 | tf_op jit(solution)/shard_map/ppermute | solution.py:631
  98.2 32.3 %collective-permute-start.18 = (bf16[176,2048]{1,0:T(8,128)(2,1)}, bf16[176,2048]{1,0:T(8,128)(2,1)}, u32[]{:S(2)}, u32[]{:S(2)}) collective-permute-start(bf16[176,2048]{1,0:T(8,128)(2,1)} %param.22), channel_id=1, source_target_pairs={{0,16},{16,0},{1,17},{17,1},{2,18},{18,2},{3,19},{19,3},{4,20},{20... | collective-permute-start | bytes 2162696 | tf_op jit(solution)/shard_map/ppermute | solution.py:631
  135.7 32.9 %collective-permute-start.21 = (bf16[256,2048]{1,0:T(8,128)(2,1)S(1)}, bf16[256,2048]{1,0:T(8,128)(2,1)S(1)}, u32[]{:S(2)}, u32[]{:S(2)}) collective-permute-start(bf16[256,2048]{1,0:T(8,128)(2,1)S(1)} %pad_maximum_fusion.5), channel_id=1, source_target_pairs={{0,4},{4,0},{1,5},{5,1},{2,6},{6,2},{3,7},{7,3},{8,12},{12,8},{9,1... | collective-permute-start | bytes 3145736 | tf_op jit(solution)/shard_map/ppermute | solution.py:631
  135.9 32.6 %collective-permute-start.20 = (bf16[272,2048]{1,0:T(8,128)(2,1)S(1)}, bf16[272,2048]{1,0:T(8,128)(2,1)S(1)}, u32[]{:S(2)}, u32[]{:S(2)}) collective-permute-start(bf16[272,2048]{1,0:T(8,128)(2,1)S(1)} %pad_maximum_fusion.2), channel_id=1, source_target_pairs={{0,1},{1,0},{2,3},{3,2},{4,5},{5,4},{6,7},{7,6},{8,9},{9,8},{10,11... | collective-permute-start | bytes 3342344 | tf_op jit(solution)/shard_map/ppermute | solution.py:631
  137.9 32.6 %collective-permute-start.23 = (bf16[256,2048]{1,0:T(8,128)(2,1)S(1)}, bf16[256,2048]{1,0:T(8,128)(2,1)S(1)}, u32[]{:S(2)}, u32[]{:S(2)}) collective-permute-start(bf16[256,2048]{1,0:T(8,128)(2,1)S(1)} %fusion.1), channel_id=1, source_target_pairs={{0,8},{8,0},{1,9},{9,1},{2,10},{10,2},{3,11},{11,3},{4,12},{12,4},... | collective-permute-start | bytes 3145736 | tf_op jit(solution)/shard_map/ppermute | solution.py:631
  138.0 30.6 %collective-permute-start.19 = (bf16[96,2048]{1,0:T(8,128)(2,1)S(1)}, bf16[96,2048]{1,0:T(8,128)(2,1)S(1)}, u32[]{:S(2)}, u32[]{:S(2)}) collective-permute-start(bf16[96,2048]{1,0:T(8,128)(2,1)S(1)} %slice.399), channel_id=1, source_target_pairs={{0,16},{16,0},{1,17},{17,1},{2,18},{18,2},{3,19},{19,3},{4,20},{20... | collective-permute-start | bytes 1179656 | tf_op jit(solution)/shard_map/ppermute | solution.py:631
  170.8 34.9 %collective-permute-start.25 = (bf16[352,2048]{1,0:T(8,128)(2,1)S(1)}, bf16[352,2048]{1,0:T(8,128)(2,1)S(1)}, u32[]{:S(2)}, u32[]{:S(2)}) collective-permute-start(bf16[352,2048]{1,0:T(8,128)(2,1)S(1)} %pad_maximum_fusion.refs_6_.refs_4_), channel_id=1, source_target_pairs={{0,4},{4,0},{1,5},{5,1},{2,6},{6,2},{3,7},{7,3},{8,12},{12,8},{9,1... | collective-permute-start | bytes 4325384 | tf_op jit(solution)/shard_map/ppermute | solution.py:631
  173.3 32.4 %collective-permute-start.28 = (bf16[352,2048]{1,0:T(8,128)(2,1)S(1)}, bf16[352,2048]{1,0:T(8,128)(2,1)S(1)}, u32[]{:S(2)}, u32[]{:S(2)}) collective-permute-start(bf16[352,2048]{1,0:T(8,128)(2,1)S(1)} %pad_maximum_fusion.1.refs_10_.refs_8_), channel_id=1, source_target_pairs={{0,1},{1,0},{2,3},{3,2},{4,5},{5,4},{6,7},{7,6},{8,9},{9,8},{10,11... | collective-permute-start | bytes 4325384 | tf_op jit(solution)/shard_map/ppermute | solution.py:631
  175.5 30.3 %collective-permute-start.27 = (bf16[256,2048]{1,0:T(8,128)(2,1)S(1)}, bf16[256,2048]{1,0:T(8,128)(2,1)S(1)}, u32[]{:S(2)}, u32[]{:S(2)}) collective-permute-start(bf16[256,2048]{1,0:T(8,128)(2,1)S(1)} %multiply_convert_fusion.refs_0_), channel_id=1, source_target_pairs={{0,8},{8,0},{1,9},{9,1},{2,10},{10,2},{3,11},{11,3},{4,12},{12,4},... | collective-permute-start | bytes 3145736 | tf_op jit(solution)/shard_map/ppermute | solution.py:631
  176.5 29.2 %collective-permute-start.26 = (bf16[256,2048]{1,0:T(8,128)(2,1)S(1)}, bf16[256,2048]{1,0:T(8,128)(2,1)S(1)}, u32[]{:S(2)}, u32[]{:S(2)}) collective-permute-start(bf16[256,2048]{1,0:T(8,128)(2,1)S(1)} %multiply_convert_fusion.refs_0_), channel_id=1, source_target_pairs={{0,2},{2,0},{1,3},{3,1},{4,6},{6,4},{5,7},{7,5},{8,10},{10,8},{9,1... | collective-permute-start | bytes 3145736 | tf_op jit(solution)/shard_map/ppermute | solution.py:631
  209.3 28.6 %collective-permute-start.29 = (bf16[272,2048]{1,0:T(8,128)(2,1)S(1)}, bf16[272,2048]{1,0:T(8,128)(2,1)}, u32[]{:S(2)}, u32[]{:S(2)}) collective-permute-start(bf16[272,2048]{1,0:T(8,128)(2,1)S(1)} %pad_maximum_fusion.3.refs_6_.refs_1_), channel_id=1, source_target_pairs={{0,4},{4,0},{1,5},{5,1},{2,6},{6,2},{3,7},{7,3},{8,12},{12,8},{9,1... | collective-permute-start | bytes 3342344 | tf_op jit(solution)/shard_map/ppermute | solution.py:631
  210.1 27.7 %collective-permute-start.30 = (bf16[256,2048]{1,0:T(8,128)(2,1)S(1)}, bf16[256,2048]{1,0:T(8,128)(2,1)}, u32[]{:S(2)}, u32[]{:S(2)}) collective-permute-start(bf16[256,2048]{1,0:T(8,128)(2,1)S(1)} %pad_maximum_fusion.6.refs_10_.refs_5_), channel_id=1, source_target_pairs={{0,1},{1,0},{2,3},{3,2},{4,5},{5,4},{6,7},{7,6},{8,9},{9,8},{10,11... | collective-permute-start | bytes 3145736 | tf_op jit(solution)/shard_map/ppermute | solution.py:631
  258.8 44.0 %collective-permute-start.37 = (bf16[4,176,1024]{2,1,0:T(8,128)(2,1)}, bf16[4,176,1024]{2,1,0:T(8,128)(2,1)S(1)}, u32[]{:S(2)}, u32[]{:S(2)}) collective-permute-start(bf16[4,176,1024]{2,1,0:T(8,128)(2,1)} %get-tuple-element.959), channel_id=1, source_target_pairs={{0,4},{4,0},{1,5},{5,1},{2,6},{6,2},{3,7},{7,3},{8,12},{12,8},{9,1... | collective-permute-start | bytes 4325384 | tf_op jit(solution)/shard_map/ppermute | solution.py:631
  259.2 43.6 %collective-permute-start.38 = (bf16[4,176,1024]{2,1,0:T(8,128)(2,1)}, bf16[4,176,1024]{2,1,0:T(8,128)(2,1)S(1)}, u32[]{:S(2)}, u32[]{:S(2)}) collective-permute-start(bf16[4,176,1024]{2,1,0:T(8,128)(2,1)} %get-tuple-element.961), channel_id=1, source_target_pairs={{0,1},{1,0},{2,3},{3,2},{4,5},{5,4},{6,7},{7,6},{8,9},{9,8},{10,11... | collective-permute-start | bytes 4325384 | tf_op jit(solution)/shard_map/ppermute | solution.py:631
  327.6 31.7 %collective-permute-start.47 = (bf16[128,2048]{1,0:T(8,128)(2,1)}, bf16[128,2048]{1,0:T(8,128)(2,1)S(1)}, u32[]{:S(2)}, u32[]{:S(2)}) collective-permute-start(bf16[128,2048]{1,0:T(8,128)(2,1)} %get-tuple-element.1112), channel_id=1, source_target_pairs={{0,8},{8,0},{1,9},{9,1},{2,10},{10,2},{3,11},{11,3},{4,12},{12,4},... | collective-permute-start | bytes 1572872 | tf_op jit(solution)/shard_map/ppermute | solution.py:631
  327.9 33.4 %collective-permute-start.48 = (bf16[4,176,1024]{2,1,0:T(8,128)(2,1)}, bf16[4,176,1024]{2,1,0:T(8,128)(2,1)}, u32[]{:S(2)}, u32[]{:S(2)}) collective-permute-start(bf16[4,176,1024]{2,1,0:T(8,128)(2,1)} %get-tuple-element.1115), channel_id=1, source_target_pairs={{0,4},{4,0},{1,5},{5,1},{2,6},{6,2},{3,7},{7,3},{8,12},{12,8},{9,1... | collective-permute-start | bytes 4325384 | tf_op jit(solution)/shard_map/ppermute | solution.py:631
  329.2 32.2 %collective-permute-start.49 = (bf16[4,176,1024]{2,1,0:T(8,128)(2,1)}, bf16[4,176,1024]{2,1,0:T(8,128)(2,1)}, u32[]{:S(2)}, u32[]{:S(2)}) collective-permute-start(bf16[4,176,1024]{2,1,0:T(8,128)(2,1)} %get-tuple-element.1117), channel_id=1, source_target_pairs={{0,1},{1,0},{2,3},{3,2},{4,5},{5,4},{6,7},{7,6},{8,9},{9,8},{10,11... | collective-permute-start | bytes 4325384 | tf_op jit(solution)/shard_map/ppermute | solution.py:631
  332.2 29.1 %collective-permute-start.46 = (bf16[128,2048]{1,0:T(8,128)(2,1)S(1)}, bf16[128,2048]{1,0:T(8,128)(2,1)S(1)}, u32[]{:S(2)}, u32[]{:S(2)}) collective-permute-start(bf16[128,2048]{1,0:T(8,128)(2,1)S(1)} %get-tuple-element.1286.refs_0_), channel_id=1, source_target_pairs={{0,8},{8,0},{1,9},{9,1},{2,10},{10,2},{3,11},{11,3},{4,12},{12,4},... | collective-permute-start | bytes 1572872 | tf_op jit(solution)/shard_map/ppermute | solution.py:631
  363.7 27.7 %collective-permute-start.53 = (bf16[2,176,1024]{2,1,0:T(8,128)(2,1)}, bf16[2,176,1024]{2,1,0:T(8,128)(2,1)}, u32[]{:S(2)}, u32[]{:S(2)}) collective-permute-start(bf16[2,176,1024]{2,1,0:T(8,128)(2,1)} %add_convert_fusion.3), channel_id=1, source_target_pairs={{0,4},{4,0},{1,5},{5,1},{2,6},{6,2},{3,7},{7,3},{8,12},{12,8},{9,1... | collective-permute-start | bytes 2162696 | tf_op jit(solution)/shard_map/ppermute | solution.py:631
  393.0 37.7 %collective-permute-start.63 = (bf16[4,176,1024]{2,1,0:T(8,128)(2,1)}, bf16[4,176,1024]{2,1,0:T(8,128)(2,1)}, u32[]{:S(2)}, u32[]{:S(2)}) collective-permute-start(bf16[4,176,1024]{2,1,0:T(8,128)(2,1)} %get-tuple-element.1236), channel_id=1, source_target_pairs={{0,4},{4,0},{1,5},{5,1},{2,6},{6,2},{3,7},{7,3},{8,12},{12,8},{9,1... | collective-permute-start | bytes 4325384 | tf_op jit(solution)/shard_map/ppermute | solution.py:631
  394.0 36.7 %collective-permute-start.64 = (bf16[4,176,1024]{2,1,0:T(8,128)(2,1)}, bf16[4,176,1024]{2,1,0:T(8,128)(2,1)}, u32[]{:S(2)}, u32[]{:S(2)}) collective-permute-start(bf16[4,176,1024]{2,1,0:T(8,128)(2,1)} %get-tuple-element.1238), channel_id=1, source_target_pairs={{0,1},{1,0},{2,3},{3,2},{4,5},{5,4},{6,7},{7,6},{8,9},{9,8},{10,11... | collective-permute-start | bytes 4325384 | tf_op jit(solution)/shard_map/ppermute | solution.py:631
  395.7 32.4 %collective-permute-start.62 = (bf16[128,2048]{1,0:T(8,128)(2,1)}, bf16[128,2048]{1,0:T(8,128)(2,1)}, u32[]{:S(2)}, u32[]{:S(2)}) collective-permute-start(bf16[128,2048]{1,0:T(8,128)(2,1)} %fusion.9), channel_id=1, source_target_pairs={{0,8},{8,0},{1,9},{9,1},{2,10},{10,2},{3,11},{11,3},{4,12},{12,4},... | collective-permute-start | bytes 1572872 | tf_op jit(solution)/shard_map/ppermute | solution.py:631
  456.5 29.1 %collective-permute-start.70 = (bf16[4,160,1024]{2,1,0:T(8,128)(2,1)}, bf16[4,160,1024]{2,1,0:T(8,128)(2,1)S(1)}, u32[]{:S(2)}, u32[]{:S(2)}) collective-permute-start(bf16[4,160,1024]{2,1,0:T(8,128)(2,1)} %get-tuple-element.1334), channel_id=1, source_target_pairs={{0,4},{4,0},{1,5},{5,1},{2,6},{6,2},{3,7},{7,3},{8,12},{12,8},{9,1... | collective-permute-start | bytes 3932168 | tf_op jit(solution)/shard_map/ppermute | solution.py:631
  457.5 28.9 %collective-permute-start.71 = (bf16[4,160,1024]{2,1,0:T(8,128)(2,1)}, bf16[4,160,1024]{2,1,0:T(8,128)(2,1)S(1)}, u32[]{:S(2)}, u32[]{:S(2)}) collective-permute-start(bf16[4,160,1024]{2,1,0:T(8,128)(2,1)} %get-tuple-element.1336), channel_id=1, source_target_pairs={{0,1},{1,0},{2,3},{3,2},{4,5},{5,4},{6,7},{7,6},{8,9},{9,8},{10,11... | collective-permute-start | bytes 3932168 | tf_op jit(solution)/shard_map/ppermute | solution.py:631
  510.5 27.6 %collective-permute-start.83 = (bf16[160,1024]{1,0:T(8,128)(2,1)S(1)}, bf16[160,1024]{1,0:T(8,128)(2,1)S(1)}, u32[]{:S(2)}, u32[]{:S(2)}) collective-permute-start(bf16[160,1024]{1,0:T(8,128)(2,1)S(1)} %get-tuple-element.1519), channel_id=1, source_target_pairs={{0,16},{16,0},{1,17},{17,1},{2,18},{18,2},{3,19},{19,3},{4,20},{20... | collective-permute-start | bytes 983048 | tf_op jit(solution)/shard_map/ppermute | solution.py:631
  512.4 29.6 %collective-permute-start.84 = (bf16[160,1024]{1,0:T(8,128)(2,1)S(1)}, bf16[160,1024]{1,0:T(8,128)(2,1)S(1)}, u32[]{:S(2)}, u32[]{:S(2)}) collective-permute-start(bf16[160,1024]{1,0:T(8,128)(2,1)S(1)} %get-tuple-element.1521), channel_id=1, source_target_pairs={{0,16},{16,0},{1,17},{17,1},{2,18},{18,2},{3,19},{19,3},{4,20},{20... | collective-permute-start | bytes 983048 | tf_op jit(solution)/shard_map/ppermute | solution.py:631
  (156 other events, 1933.7 us)

commit v3 on v2

--- a/solution.py
+++ b/solution.py
@@ -14,7 +14,7 @@
 EPS = 1e-05
 ROPE_BASE = 10000.0
 NEG_LARGE = -1e30
-SUM_COLUMNS = 512
+SUM_STEPS = 4
 F32 = jnp.float32
 BF16 = jnp.bfloat16
 NT = (((1,), (1,)), ((), ()))
@@ -424,48 +424,50 @@
     lefts, parts = refs[:count], refs[count : count + 8]
     *send_refs, keep_ref = refs[count + 8 : len(refs) - count]
     weights = refs[len(refs) - count :]
-    step = pl.program_id(0)
     rows = weights[0].shape[0] // 8
-
-    @pl.when(step == 0)
-    def _():
-        if count == 1:
-            assemble_down(parts, weights[0], first)
-        else:
-            assemble(parts[:4], weights[0], "a", rows)
-            assemble(parts[4:], weights[1], "b", rows)
-
-    def pieces():
-        size = keep_ref.shape[2]
-        for low in range(0, size, SUM_COLUMNS):
-            here = slice(low, min(low + SUM_COLUMNS, size))
-            total = dot(lefts[0][...], weights[0][:, here])
-            for left, weight in zip(lefts[1:], weights[1:]):
-                total = total + dot(left[...], weight[:, here])
-            yield here, total
-
-    for here, total in pieces():
-        if len(send_refs) == 3:
-            quarters(total, send_refs, keep_ref, here)
-        else:
-            halves(total, send_refs[0], keep_ref, here)
+    if count == 1:
+        assemble_down(parts, weights[0], first)
+    else:
+        assemble(parts[:4], weights[0], "a", rows)
+        assemble(parts[4:], weights[1], "b", rows)
+    total = dot(lefts[0][...], weights[0][...])
+    for left, weight in zip(lefts[1:], weights[1:]):
+        total = total + dot(left[...], weight[...])
+    tile = keep_ref.shape[1]
+    near, far = total[tile : 2 * tile].astype(BF16), total[3 * tile :].astype(BF16)
+    keep_ref[0] = total[:tile].astype(BF16)
+    keep_ref[1] = total[2 * tile : 3 * tile].astype(BF16)
+    if len(send_refs) == 1:
+        send_refs[0][0] = near
+        send_refs[0][1] = far
+    else:
+        near_ref, zero_ref, one_ref = send_refs
+        near_ref[...] = near
+        zero_ref[...] = far[: tile // 2]
+        one_ref[...] = far[tile // 2 :]
 
 
 def sum_rows(lefts, parts, name, first=0):
     tokens, count = lefts[0].shape
-    width = parts[0].shape[-1]
-    tile = tokens // 4
-    out = halves_out if len(lefts) == 1 else quarters_out
-    half_specs, half_shapes = out(tile, width)
+    width = parts[0].shape[1]
+    tile, columns = tokens // 4, width // SUM_STEPS
+    both = (2, tile)
+    sizes = [both, both] if len(lefts) == 1 else [(tile,), (tile // 2,), (tile // 2,), both]
+    shape = jax.ShapeDtypeStruct
+
+    def block(size):
+        zeros = (0,) * len(size)
+        return pl.BlockSpec((*size, columns), lambda s: (*zeros, s))
+
     return call(
         functools.partial(sum_kernel, len(lefts), first),
         name,
-        (4,),
-        [pl.BlockSpec((tile, count), lambda s: (tile_at(s), 0)) for one in lefts]
-        + [whole(one.shape) for one in parts],
-        half_specs,
-        half_shapes,
-        [pltpu.VMEM((count, width), BF16)] * len(lefts),
+        (SUM_STEPS,),
+        [whole(one.shape) for one in lefts]
+        + [pl.BlockSpec((one.shape[0], columns), lambda s: (0, s)) for one in parts],
+        [block(size) for size in sizes],
+        [shape((*size, width), BF16) for size in sizes],
+        [pltpu.VMEM((count, columns), BF16)] * len(lefts),
     )(*lefts, *parts)
 
 

time: 555 us -> 550 us (level)
  Pallas kernels: 186 us -> 178 us
    pallas_call x2, Pallas kernels: 38.8 us -> 29.8 us  [sum_rows(): call(functools.partial(sum_kernel, len(lefts), first), name, (SUM_STEPS,)...]
  transfers between devices with their start and end apart: 86 -> 86, of which waited for: 29 -> 31; matrix products, arithmetic and copies ran while one was open for 10% -> 10% of each run, Pallas kernels for 34% -> 33%
where the time goes in v3:
time: 550 us; the launch traced here: 540 us
  waiting for transfers between devices  184 us (33%)
  Pallas kernels  178 us (32%)
  starting transfers between devices  91.3 us (17%)
  other arithmetic  61.8 us (11%)
  local copies, waits for them, and re-layouts  23.1 us (4%)
    ppermute x85, waiting for transfers between devices, swap(): return lax.ppermute(value, axis, [(0, 1), (1, 0)])  184 us
    ppermute x85, starting transfers between devices, swap(): return lax.ppermute(value, axis, [(0, 1), (1, 0)])  90.1 us
    pallas_call x3, Pallas kernels, weight_grad(): call(functools.partial(weight_grad_kernel, count // 8), name, (4,), [whol...  34.5 us
    pallas_call x2, Pallas kernels, sum_rows(): call(functools.partial(sum_kernel, len(lefts), first), name, (SUM_STEPS,)...  29.8 us
    pallas_call x1, Pallas kernels, attn_forward(): call(functools.partial(attn_forward_kernel, row, head_rows), 'attn_forwar...  23.8 us
    pallas_call x1, Pallas kernels, attn_backward(): call(functools.partial(attn_backward_kernel, row), 'attn_backward', (4,),...  23.6 us
    pallas_call x1, Pallas kernels, units(): call(units_kernel, 'units', (4,), [whole(one.shape) for one in (*hidden,...  22.6 us
    pallas_call x1, Pallas kernels, unit_grads(): call(functools.partial(unit_grads_kernel, first), 'unit_grads', (4,), [wh...  14.2 us
  transfers between devices with their start and end apart: 86, of which 31 were waited for; matrix products, arithmetic and copies ran while one was open for 10% of the time, Pallas kernels for 33%

profile of v3, /device:TPU:1, one launch (start us, length us, event | category | flops | bytes accessed | tf_op | source)
XLA Modules:
  0.0 540.4 jit_solution(6665531890528219495)
XLA Ops:
  13.6 28.1 %collective-permute-done.3 = bf16[1,256]{1,0:T(2,128)(2,1)S(1)} collective-permute-done((bf16[1,256]{1,0:T(2,128)(2,1)S(1)}, bf16[1,256]{1,0:T(2,128)(2,1)S(1)}, u32[]{:S(2)}, u32[]{:S(2)}) %collective-permute-start.3) | collective-permute-done | bytes 544 | tf_op jit(solution)/shard_map/ppermute | solution.py:633
  52.9 17.5 %collective-permute-done.7 = bf16[96,2048]{1,0:T(8,128)(2,1)} collective-permute-done((bf16[96,2048]{1,0:T(8,128)(2,1)}, bf16[96,2048]{1,0:T(8,128)(2,1)}, u32[]{:S(2)}, u32[]{:S(2)}) %collective-permute-start.7) | collective-permute-done | bytes 393248 | tf_op jit(solution)/shard_map/ppermute | solution.py:633
  78.8 3.1 fusion.8
  82.5 11.1 %collective-permute-done.12 = bf16[96,2048]{1,0:T(8,128)(2,1)S(1)} collective-permute-done((bf16[96,2048]{1,0:T(8,128)(2,1)S(1)}, bf16[96,2048]{1,0:T(8,128)(2,1)S(1)}, u32[]{:S(2)}, u32[]{:S(2)}) %collective-permute-start.12) | collective-permute-done | bytes 393248 | tf_op jit(solution)/shard_map/ppermute | solution.py:633
  99.8 3.0 collective-permute-start.15
  104.4 23.8 %attn_forward.1 = (bf16[1024,2048]{1,0:T(8,128)(2,1)}, bf16[1024,768]{1,0:T(8,128)(2,1)}, bf16[1024,512]{1,0:T(8,128)(2,1)}, bf16[2,256,2048]{2,1,0:T(8,128)(2,1...) custom-call(bf16[256,2048]{1,0:T(8,128)(2,1)} %bitcast.95, ...), custom_call_target="tpu_custom_call" | custom-call | flops 1000 | bytes 1000 | tf_op jit(solution)/shard_map/attn_forward/pallas_call | solution.py:260
  130.5 2.9 collective-permute-start.22
  139.9 28.7 %collective-permute-done.19 = bf16[96,2048]{1,0:T(8,128)(2,1)S(1)} collective-permute-done((bf16[96,2048]{1,0:T(8,128)(2,1)S(1)}, bf16[96,2048]{1,0:T(8,128)(2,1)S(1)}, u32[]{:S(2)}, u32[]{:S(2)}) %collective-permute-start.19) | collective-permute-done | bytes 393248 | tf_op jit(solution)/shard_map/ppermute | solution.py:633
  179.3 25.3 %collective-permute-done.24 = bf16[80,2048]{1,0:T(8,128)(2,1)S(1)} collective-permute-done((bf16[80,2048]{1,0:T(8,128)(2,1)S(1)}, bf16[80,2048]{1,0:T(8,128)(2,1)S(1)}, u32[]{:S(2)}, u32[]{:S(2)}) %collective-permute-start.24) | collective-permute-done | bytes 327712 | tf_op jit(solution)/shard_map/ppermute | solution.py:633
  215.0 22.6 %units.1 = (bf16[1024,1408]{1,0:T(8,128)(2,1)}, bf16[1024,1408]{1,0:T(8,128)(2,1)}, bf16[1024,1408]{1,0:T(8,128)(2,1)}) custom-call(bf16[256,2048]{1,0:T(8,128)(2,1)} %copy-done.3, bf16[256,2048]{1,0:T(8,128)(2,1)} %copy-done.11, bf16[256,2048]{1,0:T(8,128)(2,1)} %copy-done.10, bf16[256,2048]{1,0:T(8,128)(2,1)} %copy-done.12, bf16[352,2048]{1,0:T(8,128)(2,1)} %copy-done.13, ...), custom_call_target="tpu_custom_call" | custom-call | flops 1000 | bytes 1000 | tf_op jit(solution)/shard_map/units/pallas_call | solution.py:380
  243.6 11.4 %down_grad.1 = (bf16[4,176,1024]{2,1,0:T(8,128)(2,1)}, bf16[4,176,1024]{2,1,0:T(8,128)(2,1)}, bf16[4,176,1024]{2,1,0:T(8,128)(2,1)}, bf16[4,176,1024]{2,1,0:T(8,128)(2,1)}) custom-call(bf16[1024,1408]{1,0:T(8,128)(2,1)} %get-tuple-element.1124.l_ref.refs_0_, bf16[256,2048]{1,0:T(8,128)(2,1)} %bitcast.101, bf16[256,2048]{1,0:T(8,128)(2,1)} %collective-permute-done.32.refs_1_, ...), custom_call_target="tpu_custom_call" | custom-call | flops 1000 | bytes 1000 | tf_op jit(solution)/shard_map/down_grad/pallas_call | solution.py:509
  256.0 2.5 collective-permute-done.34.refs_9_.refs_4_
  260.2 14.2 %unit_grads.1 = (bf16[1024,1408]{1,0:T(8,128)(2,1)}, bf16[1024,1408]{1,0:T(8,128)(2,1)}) custom-call(bf16[256,2048]{1,0:T(8,128)(2,1)} %bitcast.102, bf16[256,2048]{1,0:T(8,128)(2,1)} %collective-permute-done.32.refs_1_, bf16[256,2048]{1,0:T(8,128)(2,1)} %collective-permute-done.33.refs_2_, bf16[256,2048]{1,0:T(8,128)(2,1)} %copy-done.40, ...), custom_call_target="tpu_custom_call" | custom-call | flops 1000 | bytes 1000 | tf_op jit(solution)/shard_map/unit_grads/pallas_call | solution.py:410
  274.4 18.6 %hidden_grads.1 = (bf16[256,2048]{1,0:T(8,128)(2,1)}, bf16[128,2048]{1,0:T(8,128)(2,1)}, bf16[128,2048]{1,0:T(8,128)(2,1)}, bf16[2,256,2048]{2,1,0:T(8,128)(2,1)}) custom-call(bf16[1024,1408]{1,0:T(8,128)(2,1)} %get-tuple-element.1074.refs_0_.l_ref, bf16[1024,1408]{1,0:T(8,128)(2,1)} %get-tuple-element.1177.refs_1_.l_ref, bf16[352,2048]{1,0:T(8,128)(2,1)} %copy-done.13, ...), custom_call_target="tpu_custom_call" | custom-call | flops 1000 | bytes 1000 | tf_op jit(solution)/shard_map/hidden_grads/pallas_call | solution.py:462
  305.0 11.8 %gate_grad.1 = (bf16[4,176,1024]{2,1,0:T(8,128)(2,1)}, bf16[4,176,1024]{2,1,0:T(8,128)(2,1)}, bf16[4,176,1024]{2,1,0:T(8,128)(2,1)}, bf16[4,176,1024]{2,1,0:T(8,128)(2,1)}) custom-call(bf16[1024,1408]{1,0:T(8,128)(2,1)} %get-tuple-element.1074.refs_0_.l_ref, bf16[256,2048]{1,0:T(8,128)(2,1)} %copy-done.3, bf16[256,2048]{1,0:T(8,128)(2,1)} %copy-done.11, ...), custom_call_target="tpu_custom_call" | custom-call | flops 1000 | bytes 1000 | tf_op jit(solution)/shard_map/gate_grad/pallas_call | solution.py:509
  331.8 11.2 %block_out.1 = (bf16[2,256,2048]{2,1,0:T(8,128)(2,1)}, bf16[2,256,2048]{2,1,0:T(8,128)(2,1)}) custom-call(bf16[1024,1408]{1,0:T(8,128)(2,1)} %get-tuple-element.1124.l_ref.refs_0_, bf16[272,2048]{1,0:T(8,128)(2,1)} %copy-done.6, bf16[272,2048]{1,0:T(8,128)(2,1)} %collective-permute-done.29.refs_7_.refs_2_, bf16[192,2048]{1,0:T(8,128)(2,1)} %copy-done.15, ...), custom_call_target="tpu_custom_call" | custom-call | flops 1000 | bytes 1000 | tf_op jit(solution)/shard_map/block_out/pallas_call | solution.py:462
  345.0 9.2 %collective-permute-done.45.refs_0_ = bf16[176,1280]{1,0:T(8,128)(2,1)} collective-permute-done((bf16[176,1280]{1,0:T(8,128)(2,1)}, bf16[176,1280]{1,0:T(8,128)(2,1)}, u32[]{:S(2)}, u32[]{:S(2)}) %collective-permute-start.45) | collective-permute-done | bytes 450592 | tf_op jit(solution)/shard_map/ppermute | solution.py:633
  365.1 2.5 fusion.40
  369.7 11.3 %up_grad.1 = (bf16[4,176,1024]{2,1,0:T(8,128)(2,1)}, bf16[4,176,1024]{2,1,0:T(8,128)(2,1)}, bf16[4,176,1024]{2,1,0:T(8,128)(2,1)}, bf16[4,176,1024]{2,1,0:T(8,128)(2,1)}) custom-call(bf16[1024,1408]{1,0:T(8,128)(2,1)} %get-tuple-element.1177.refs_1_.l_ref, bf16[256,2048]{1,0:T(8,128)(2,1)} %copy-done.3, bf16[256,2048]{1,0:T(8,128)(2,1)} %copy-done.11, ...), custom_call_target="tpu_custom_call" | custom-call | flops 1000 | bytes 1000 | tf_op jit(solution)/shard_map/up_grad/pallas_call | solution.py:509
  381.6 3.9 collective-permute-done.50.refs_1_
  398.9 23.6 %attn_backward.1 = (bf16[1024,768]{1,0:T(8,128)(2,1)}, f32[1,2048]{1,0:T(1,128)}, bf16[256,2048]{1,0:T(8,128)(2,1)}, bf16[128,2048]{1,0:T(8,128)(2,1)}, bf16[128...) custom-call(bf16[128,2048]{1,0:T(8,128)(2,1)} %copy-done.29, bf16[128,2048]{1,0:T(8,128)(2,1)} %copy-done.30, ...), custom_call_target="tpu_custom_call" | custom-call | flops 1000 | bytes 1000 | tf_op jit(solution)/shard_map/attn_backward/pallas_call | solution.py:337
  431.8 2.6 fusion.2
  438.4 11.9 %attn_grads.1 = (bf16[4,160,1024]{2,1,0:T(8,128)(2,1)}, bf16[4,160,1024]{2,1,0:T(8,128)(2,1)}, bf16[4,160,1024]{2,1,0:T(8,128)(2,1)}, bf16[4,160,1024]{2,1,0:T(8,128)(2,1)}) custom-call(bf16[1024,768]{1,0:T(8,128)(2,1)} %get-tuple-element.1283.gqkv_ref, bf16[1024,2048]{1,0:T(8,128)(2,1)} %get-tuple-element.1284.hid_ref, ...), custom_call_target="tpu_custom_call" | custom-call | flops 1000 | bytes 1000 | tf_op jit(solution)/shard_map/attn_grads/pallas_call | solution.py:547
  459.4 14.3 %collective-permute-done.73.refs_0_ = bf16[176,1280]{1,0:T(8,128)(2,1)S(1)} collective-permute-done((bf16[176,1280]{1,0:T(8,128)(2,1)S(1)}, bf16[176,1280]{1,0:T(8,128)(2,1)S(1)}, u32[]{:S(2)}, u32[]{:S(2)}) %collective-permute-start.73) | collective-permute-done | bytes 450592 | tf_op jit(solution)/shard_map/ppermute | solution.py:633
  473.6 6.8 %collective-permute-done.70 = bf16[4,160,1024]{2,1,0:T(8,128)(2,1)S(1)} collective-permute-done((bf16[4,160,1024]{2,1,0:T(8,128)(2,1)}, bf16[4,160,1024]{2,1,0:T(8,128)(2,1)S(1)}, u32[]{:S(2)}, u32[]{:S(2)}) %collective-permute-start.70) | collective-permute-done | bytes 1310752 | tf_op jit(solution)/shard_map/ppermute | solution.py:633
  489.3 11.8 %collective-permute-done.76 = f32[2,1,2,2,2,2,64]{6,5,4,3,2,1,0:T(2,128)S(1)} collective-permute-done((f32[2,1,2,2,2,2,64]{6,5,4,3,2,1,0:T(2,128)S(1)}, f32[2,1,2,2,2,2,64]{6,5,4,3,2,1,0:T(2,128)S(1)}, u32[]{:S(2)}, u32[]{:S(2)}) %collective-permute-start.76) | collective-permute-done | bytes 8224 | tf_op jit(solution)/shard_map/ppermute | solution.py:633
  509.6 5.4 %collective-permute-start.81 = (f32[2,1,2,1,1,1,64]{6,5,4,3,2,1,0:T(1,128)S(1)}, f32[2,1,2,1,1,1,64]{6,5,4,3,2,1,0:T(1,128)S(1)}, u32[]{:S(2)}, u32[]{:S(2)}) collective-permute-start(f32[2,1,2,1,1,1,64]{6,5,4,3,2,1,0:T(1,128)S(1)} %broadcast_select_fusion.4), channel_id=1, source_target_pairs={{0,2},{2,0},{1,3},{3,1},{4,6},{6,4},{5,7},{7,5},{8,10},{10,8},{9,1... | collective-permute-start | bytes 3080 | tf_op jit(solution)/shard_map/ppermute | solution.py:633
  515.0 3.2 total.3
  518.2 3.2 total.4
  521.3 3.2 total.5
  524.9 7.7 %finish.1 = (bf16[256,2048]{1,0:T(8,128)(2,1)}, bf16[256,2048]{1,0:T(8,128)(2,1)}) custom-call(bf16[256,2048]{1,0:T(8,128)(2,1)} %bitcast.97, f32[1,2048]{1,0:T(1,128)} %reshape.316.refs_4_.gain_ref, f32[128,2048]{1,0:T(8,128)} %get-tuple-element.1461.mid0_ref, f32[128,2048]{1,0:T(8,128)} %get-tuple-element.1462.mid1_ref, ...), custom_call_target="tpu_custom_call" | custom-call | flops 1000 | bytes 1000 | tf_op jit(solution)/shard_map/finish/pallas_call | solution.py:610
  533.2 3.9 collective-permute-done.84
  (498 shorter events, 177.9 us)
Async XLA Ops:
  3.1 38.7 %collective-permute-start.1 = (bf16[256,2048]{1,0:T(8,128)(2,1)}, bf16[256,2048]{1,0:T(8,128)(2,1)S(1)}, u32[]{:S(2)}, u32[]{:S(2)}) collective-permute-start(bf16[256,2048]{1,0:T(8,128)(2,1)} %pad_maximum_fusion.4), channel_id=1, source_target_pairs={{0,1},{1,0},{2,3},{3,2},{4,5},{5,4},{6,7},{7,6},{8,9},{9,8},{10,11... | collective-permute-start | bytes 3145736 | tf_op jit(solution)/shard_map/ppermute | solution.py:633
  5.2 36.6 %collective-permute-start.4 = (bf16[256,2048]{1,0:T(8,128)(2,1)S(1)}, bf16[256,2048]{1,0:T(8,128)(2,1)}, u32[]{:S(2)}, u32[]{:S(2)}) collective-permute-start(bf16[256,2048]{1,0:T(8,128)(2,1)S(1)} %bitcast.98), channel_id=1, source_target_pairs={{0,8},{8,0},{1,9},{9,1},{2,10},{10,2},{3,11},{11,3},{4,12},{12,4},... | collective-permute-start | bytes 3145736 | tf_op jit(solution)/shard_map/ppermute | solution.py:633
  8.7 33.0 %collective-permute-start.2 = (bf16[240,2048]{1,0:T(8,128)(2,1)}, bf16[240,2048]{1,0:T(8,128)(2,1)S(1)}, u32[]{:S(2)}, u32[]{:S(2)}) collective-permute-start(bf16[240,2048]{1,0:T(8,128)(2,1)} %pad_maximum_fusion.7), channel_id=1, source_target_pairs={{0,4},{4,0},{1,5},{5,1},{2,6},{6,2},{3,7},{7,3},{8,12},{12,8},{9,1... | collective-permute-start | bytes 2949128 | tf_op jit(solution)/shard_map/ppermute | solution.py:633
  10.8 30.9 %collective-permute-start = (bf16[144,2048]{1,0:T(8,128)(2,1)}, bf16[144,2048]{1,0:T(8,128)(2,1)}, u32[]{:S(2)}, u32[]{:S(2)}) collective-permute-start(bf16[144,2048]{1,0:T(8,128)(2,1)} %pad_maximum_fusion.13), channel_id=1, source_target_pairs={{0,16},{16,0},{1,17},{17,1},{2,18},{18,2},{3,19},{19,3},{4,20},{20... | collective-permute-start | bytes 1769480 | tf_op jit(solution)/shard_map/ppermute | solution.py:633
  13.3 28.4 %collective-permute-start.3 = (bf16[1,256]{1,0:T(2,128)(2,1)S(1)}, bf16[1,256]{1,0:T(2,128)(2,1)S(1)}, u32[]{:S(2)}, u32[]{:S(2)}) collective-permute-start(bf16[1,256]{1,0:T(2,128)(2,1)S(1)} %pad.8), channel_id=1, source_target_pairs={{0,8},{8,0},{1,9},{9,1},{2,10},{10,2},{3,11},{11,3},{4,12},{12,4},... | collective-permute-start | bytes 1544 | tf_op jit(solution)/shard_map/ppermute | solution.py:633
  95.8 34.7 %collective-permute-start.17 = (bf16[352,2048]{1,0:T(8,128)(2,1)S(1)}, bf16[352,2048]{1,0:T(8,128)(2,1)}, u32[]{:S(2)}, u32[]{:S(2)}) collective-permute-start(bf16[352,2048]{1,0:T(8,128)(2,1)S(1)} %constant_dynamic-update-slice_fusion.2.refs_8_.refs_6_), channel_id=1, source_target_pairs={{0,1},{1,0},{2,3},{3,2},{4,5},{5,4},{6,7},{7,6},{8,9},{9,8},{10,11... | collective-permute-start | bytes 4325384 | tf_op jit(solution)/shard_map/ppermute | solution.py:633
  96.0 34.5 %collective-permute-start.16 = (bf16[352,2048]{1,0:T(8,128)(2,1)S(1)}, bf16[352,2048]{1,0:T(8,128)(2,1)}, u32[]{:S(2)}, u32[]{:S(2)}) collective-permute-start(bf16[352,2048]{1,0:T(8,128)(2,1)S(1)} %constant_dynamic-update-slice_fusion.refs_4_.refs_2_), channel_id=1, source_target_pairs={{0,4},{4,0},{1,5},{5,1},{2,6},{6,2},{3,7},{7,3},{8,12},{12,8},{9,1... | collective-permute-start | bytes 4325384 | tf_op jit(solution)/shard_map/ppermute | solution.py:633
  98.2 32.3 %collective-permute-start.18 = (bf16[176,2048]{1,0:T(8,128)(2,1)}, bf16[176,2048]{1,0:T(8,128)(2,1)}, u32[]{:S(2)}, u32[]{:S(2)}) collective-permute-start(bf16[176,2048]{1,0:T(8,128)(2,1)} %param.22), channel_id=1, source_target_pairs={{0,16},{16,0},{1,17},{17,1},{2,18},{18,2},{3,19},{19,3},{4,20},{20... | collective-permute-start | bytes 2162696 | tf_op jit(solution)/shard_map/ppermute | solution.py:633
  135.7 32.9 %collective-permute-start.21 = (bf16[256,2048]{1,0:T(8,128)(2,1)S(1)}, bf16[256,2048]{1,0:T(8,128)(2,1)S(1)}, u32[]{:S(2)}, u32[]{:S(2)}) collective-permute-start(bf16[256,2048]{1,0:T(8,128)(2,1)S(1)} %pad_maximum_fusion.5), channel_id=1, source_target_pairs={{0,4},{4,0},{1,5},{5,1},{2,6},{6,2},{3,7},{7,3},{8,12},{12,8},{9,1... | collective-permute-start | bytes 3145736 | tf_op jit(solution)/shard_map/ppermute | solution.py:633
  135.9 32.6 %collective-permute-start.20 = (bf16[272,2048]{1,0:T(8,128)(2,1)S(1)}, bf16[272,2048]{1,0:T(8,128)(2,1)S(1)}, u32[]{:S(2)}, u32[]{:S(2)}) collective-permute-start(bf16[272,2048]{1,0:T(8,128)(2,1)S(1)} %pad_maximum_fusion.2), channel_id=1, source_target_pairs={{0,1},{1,0},{2,3},{3,2},{4,5},{5,4},{6,7},{7,6},{8,9},{9,8},{10,11... | collective-permute-start | bytes 3342344 | tf_op jit(solution)/shard_map/ppermute | solution.py:633
  137.9 32.6 %collective-permute-start.23 = (bf16[256,2048]{1,0:T(8,128)(2,1)S(1)}, bf16[256,2048]{1,0:T(8,128)(2,1)S(1)}, u32[]{:S(2)}, u32[]{:S(2)}) collective-permute-start(bf16[256,2048]{1,0:T(8,128)(2,1)S(1)} %fusion.1), channel_id=1, source_target_pairs={{0,8},{8,0},{1,9},{9,1},{2,10},{10,2},{3,11},{11,3},{4,12},{12,4},... | collective-permute-start | bytes 3145736 | tf_op jit(solution)/shard_map/ppermute | solution.py:633
  138.0 30.6 %collective-permute-start.19 = (bf16[96,2048]{1,0:T(8,128)(2,1)S(1)}, bf16[96,2048]{1,0:T(8,128)(2,1)S(1)}, u32[]{:S(2)}, u32[]{:S(2)}) collective-permute-start(bf16[96,2048]{1,0:T(8,128)(2,1)S(1)} %slice.399), channel_id=1, source_target_pairs={{0,16},{16,0},{1,17},{17,1},{2,18},{18,2},{3,19},{19,3},{4,20},{20... | collective-permute-start | bytes 1179656 | tf_op jit(solution)/shard_map/ppermute | solution.py:633
  170.8 34.9 %collective-permute-start.25 = (bf16[352,2048]{1,0:T(8,128)(2,1)S(1)}, bf16[352,2048]{1,0:T(8,128)(2,1)S(1)}, u32[]{:S(2)}, u32[]{:S(2)}) collective-permute-start(bf16[352,2048]{1,0:T(8,128)(2,1)S(1)} %pad_maximum_fusion.refs_6_.refs_4_), channel_id=1, source_target_pairs={{0,4},{4,0},{1,5},{5,1},{2,6},{6,2},{3,7},{7,3},{8,12},{12,8},{9,1... | collective-permute-start | bytes 4325384 | tf_op jit(solution)/shard_map/ppermute | solution.py:633
  173.3 32.4 %collective-permute-start.28 = (bf16[352,2048]{1,0:T(8,128)(2,1)S(1)}, bf16[352,2048]{1,0:T(8,128)(2,1)S(1)}, u32[]{:S(2)}, u32[]{:S(2)}) collective-permute-start(bf16[352,2048]{1,0:T(8,128)(2,1)S(1)} %pad_maximum_fusion.1.refs_10_.refs_8_), channel_id=1, source_target_pairs={{0,1},{1,0},{2,3},{3,2},{4,5},{5,4},{6,7},{7,6},{8,9},{9,8},{10,11... | collective-permute-start | bytes 4325384 | tf_op jit(solution)/shard_map/ppermute | solution.py:633
  175.5 30.3 %collective-permute-start.27 = (bf16[256,2048]{1,0:T(8,128)(2,1)S(1)}, bf16[256,2048]{1,0:T(8,128)(2,1)S(1)}, u32[]{:S(2)}, u32[]{:S(2)}) collective-permute-start(bf16[256,2048]{1,0:T(8,128)(2,1)S(1)} %multiply_convert_fusion.refs_0_), channel_id=1, source_target_pairs={{0,8},{8,0},{1,9},{9,1},{2,10},{10,2},{3,11},{11,3},{4,12},{12,4},... | collective-permute-start | bytes 3145736 | tf_op jit(solution)/shard_map/ppermute | solution.py:633
  176.5 29.2 %collective-permute-start.26 = (bf16[256,2048]{1,0:T(8,128)(2,1)S(1)}, bf16[256,2048]{1,0:T(8,128)(2,1)S(1)}, u32[]{:S(2)}, u32[]{:S(2)}) collective-permute-start(bf16[256,2048]{1,0:T(8,128)(2,1)S(1)} %multiply_convert_fusion.refs_0_), channel_id=1, source_target_pairs={{0,2},{2,0},{1,3},{3,1},{4,6},{6,4},{5,7},{7,5},{8,10},{10,8},{9,1... | collective-permute-start | bytes 3145736 | tf_op jit(solution)/shard_map/ppermute | solution.py:633
  209.3 28.4 %collective-permute-start.29 = (bf16[272,2048]{1,0:T(8,128)(2,1)S(1)}, bf16[272,2048]{1,0:T(8,128)(2,1)}, u32[]{:S(2)}, u32[]{:S(2)}) collective-permute-start(bf16[272,2048]{1,0:T(8,128)(2,1)S(1)} %pad_maximum_fusion.3.refs_6_.refs_1_), channel_id=1, source_target_pairs={{0,4},{4,0},{1,5},{5,1},{2,6},{6,2},{3,7},{7,3},{8,12},{12,8},{9,1... | collective-permute-start | bytes 3342344 | tf_op jit(solution)/shard_map/ppermute | solution.py:633
  258.6 39.0 %collective-permute-start.37 = (bf16[4,176,1024]{2,1,0:T(8,128)(2,1)}, bf16[4,176,1024]{2,1,0:T(8,128)(2,1)S(1)}, u32[]{:S(2)}, u32[]{:S(2)}) collective-permute-start(bf16[4,176,1024]{2,1,0:T(8,128)(2,1)} %get-tuple-element.959), channel_id=1, source_target_pairs={{0,4},{4,0},{1,5},{5,1},{2,6},{6,2},{3,7},{7,3},{8,12},{12,8},{9,1... | collective-permute-start | bytes 4325384 | tf_op jit(solution)/shard_map/ppermute | solution.py:633
  259.0 38.5 %collective-permute-start.38 = (bf16[4,176,1024]{2,1,0:T(8,128)(2,1)}, bf16[4,176,1024]{2,1,0:T(8,128)(2,1)S(1)}, u32[]{:S(2)}, u32[]{:S(2)}) collective-permute-start(bf16[4,176,1024]{2,1,0:T(8,128)(2,1)} %get-tuple-element.961), channel_id=1, source_target_pairs={{0,1},{1,0},{2,3},{3,2},{4,5},{5,4},{6,7},{7,6},{8,9},{9,8},{10,11... | collective-permute-start | bytes 4325384 | tf_op jit(solution)/shard_map/ppermute | solution.py:633
  322.3 31.9 %collective-permute-start.47 = (bf16[128,2048]{1,0:T(8,128)(2,1)}, bf16[128,2048]{1,0:T(8,128)(2,1)S(1)}, u32[]{:S(2)}, u32[]{:S(2)}) collective-permute-start(bf16[128,2048]{1,0:T(8,128)(2,1)} %get-tuple-element.1112), channel_id=1, source_target_pairs={{0,8},{8,0},{1,9},{9,1},{2,10},{10,2},{3,11},{11,3},{4,12},{12,4},... | collective-permute-start | bytes 1572872 | tf_op jit(solution)/shard_map/ppermute | solution.py:633
  322.9 33.2 %collective-permute-start.48 = (bf16[4,176,1024]{2,1,0:T(8,128)(2,1)}, bf16[4,176,1024]{2,1,0:T(8,128)(2,1)}, u32[]{:S(2)}, u32[]{:S(2)}) collective-permute-start(bf16[4,176,1024]{2,1,0:T(8,128)(2,1)} %get-tuple-element.1115), channel_id=1, source_target_pairs={{0,4},{4,0},{1,5},{5,1},{2,6},{6,2},{3,7},{7,3},{8,12},{12,8},{9,1... | collective-permute-start | bytes 4325384 | tf_op jit(solution)/shard_map/ppermute | solution.py:633
  324.1 31.9 %collective-permute-start.49 = (bf16[4,176,1024]{2,1,0:T(8,128)(2,1)}, bf16[4,176,1024]{2,1,0:T(8,128)(2,1)}, u32[]{:S(2)}, u32[]{:S(2)}) collective-permute-start(bf16[4,176,1024]{2,1,0:T(8,128)(2,1)} %get-tuple-element.1117), channel_id=1, source_target_pairs={{0,1},{1,0},{2,3},{3,2},{4,5},{5,4},{6,7},{7,6},{8,9},{9,8},{10,11... | collective-permute-start | bytes 4325384 | tf_op jit(solution)/shard_map/ppermute | solution.py:633
  327.1 28.9 %collective-permute-start.46 = (bf16[128,2048]{1,0:T(8,128)(2,1)S(1)}, bf16[128,2048]{1,0:T(8,128)(2,1)S(1)}, u32[]{:S(2)}, u32[]{:S(2)}) collective-permute-start(bf16[128,2048]{1,0:T(8,128)(2,1)S(1)} %get-tuple-element.1286.refs_0_), channel_id=1, source_target_pairs={{0,8},{8,0},{1,9},{9,1},{2,10},{10,2},{3,11},{11,3},{4,12},{12,4},... | collective-permute-start | bytes 1572872 | tf_op jit(solution)/shard_map/ppermute | solution.py:633
  358.5 28.1 %collective-permute-start.53 = (bf16[2,176,1024]{2,1,0:T(8,128)(2,1)}, bf16[2,176,1024]{2,1,0:T(8,128)(2,1)}, u32[]{:S(2)}, u32[]{:S(2)}) collective-permute-start(bf16[2,176,1024]{2,1,0:T(8,128)(2,1)} %add_convert_fusion.3), channel_id=1, source_target_pairs={{0,4},{4,0},{1,5},{5,1},{2,6},{6,2},{3,7},{7,3},{8,12},{12,8},{9,1... | collective-permute-start | bytes 2162696 | tf_op jit(solution)/shard_map/ppermute | solution.py:633
  358.9 27.7 %collective-permute-start.54 = (bf16[2,256,2048]{2,1,0:T(8,128)(2,1)}, bf16[2,256,2048]{2,1,0:T(8,128)(2,1)S(1)}, u32[]{:S(2)}, u32[]{:S(2)}) collective-permute-start(bf16[2,256,2048]{2,1,0:T(8,128)(2,1)} %get-tuple-element.1171), channel_id=1, source_target_pairs={{0,2},{2,0},{1,3},{3,1},{4,6},{6,4},{5,7},{7,5},{8,10},{10,8},{9,1... | collective-permute-start | bytes 6291464 | tf_op jit(solution)/shard_map/ppermute | solution.py:633
  387.9 37.9 %collective-permute-start.63 = (bf16[4,176,1024]{2,1,0:T(8,128)(2,1)}, bf16[4,176,1024]{2,1,0:T(8,128)(2,1)}, u32[]{:S(2)}, u32[]{:S(2)}) collective-permute-start(bf16[4,176,1024]{2,1,0:T(8,128)(2,1)} %get-tuple-element.1236), channel_id=1, source_target_pairs={{0,4},{4,0},{1,5},{5,1},{2,6},{6,2},{3,7},{7,3},{8,12},{12,8},{9,1... | collective-permute-start | bytes 4325384 | tf_op jit(solution)/shard_map/ppermute | solution.py:633
  388.8 37.1 %collective-permute-start.64 = (bf16[4,176,1024]{2,1,0:T(8,128)(2,1)}, bf16[4,176,1024]{2,1,0:T(8,128)(2,1)}, u32[]{:S(2)}, u32[]{:S(2)}) collective-permute-start(bf16[4,176,1024]{2,1,0:T(8,128)(2,1)} %get-tuple-element.1238), channel_id=1, source_target_pairs={{0,1},{1,0},{2,3},{3,2},{4,5},{5,4},{6,7},{7,6},{8,9},{9,8},{10,11... | collective-permute-start | bytes 4325384 | tf_op jit(solution)/shard_map/ppermute | solution.py:633
  390.7 32.6 %collective-permute-start.62 = (bf16[128,2048]{1,0:T(8,128)(2,1)}, bf16[128,2048]{1,0:T(8,128)(2,1)}, u32[]{:S(2)}, u32[]{:S(2)}) collective-permute-start(bf16[128,2048]{1,0:T(8,128)(2,1)} %fusion.9), channel_id=1, source_target_pairs={{0,8},{8,0},{1,9},{9,1},{2,10},{10,2},{3,11},{11,3},{4,12},{12,4},... | collective-permute-start | bytes 1572872 | tf_op jit(solution)/shard_map/ppermute | solution.py:633
  451.4 29.1 %collective-permute-start.70 = (bf16[4,160,1024]{2,1,0:T(8,128)(2,1)}, bf16[4,160,1024]{2,1,0:T(8,128)(2,1)S(1)}, u32[]{:S(2)}, u32[]{:S(2)}) collective-permute-start(bf16[4,160,1024]{2,1,0:T(8,128)(2,1)} %get-tuple-element.1334), channel_id=1, source_target_pairs={{0,4},{4,0},{1,5},{5,1},{2,6},{6,2},{3,7},{7,3},{8,12},{12,8},{9,1... | collective-permute-start | bytes 3932168 | tf_op jit(solution)/shard_map/ppermute | solution.py:633
  452.6 28.9 %collective-permute-start.71 = (bf16[4,160,1024]{2,1,0:T(8,128)(2,1)}, bf16[4,160,1024]{2,1,0:T(8,128)(2,1)S(1)}, u32[]{:S(2)}, u32[]{:S(2)}) collective-permute-start(bf16[4,160,1024]{2,1,0:T(8,128)(2,1)} %get-tuple-element.1336), channel_id=1, source_target_pairs={{0,1},{1,0},{2,3},{3,2},{4,5},{5,4},{6,7},{7,6},{8,9},{9,8},{10,11... | collective-permute-start | bytes 3932168 | tf_op jit(solution)/shard_map/ppermute | solution.py:633
  505.5 27.7 %collective-permute-start.83 = (bf16[160,1024]{1,0:T(8,128)(2,1)S(1)}, bf16[160,1024]{1,0:T(8,128)(2,1)S(1)}, u32[]{:S(2)}, u32[]{:S(2)}) collective-permute-start(bf16[160,1024]{1,0:T(8,128)(2,1)S(1)} %get-tuple-element.1519), channel_id=1, source_target_pairs={{0,16},{16,0},{1,17},{17,1},{2,18},{18,2},{3,19},{19,3},{4,20},{20... | collective-permute-start | bytes 983048 | tf_op jit(solution)/shard_map/ppermute | solution.py:633
  507.5 29.6 %collective-permute-start.84 = (bf16[160,1024]{1,0:T(8,128)(2,1)S(1)}, bf16[160,1024]{1,0:T(8,128)(2,1)S(1)}, u32[]{:S(2)}, u32[]{:S(2)}) collective-permute-start(bf16[160,1024]{1,0:T(8,128)(2,1)S(1)} %get-tuple-element.1521), channel_id=1, source_target_pairs={{0,16},{16,0},{1,17},{17,1},{2,18},{18,2},{3,19},{19,3},{4,20},{20... | collective-permute-start | bytes 983048 | tf_op jit(solution)/shard_map/ppermute | solution.py:633
  (156 other events, 1928.2 us)

commit v4 on v3

--- a/solution.py
+++ b/solution.py
@@ -920,8 +920,8 @@
     v.gh2_one = swap(v.gh2_one, ZL)
     v.grad_mid0, v.gb0, v.mlp_terms = mid_grads(0, v.pop.gh2_zero)
     v.gb0_far = swap(v.gb0, ZL)
-    v.dg_send = last_send(v.dg, early, width)
-    v.dg = step_three(v.dg, last_send(v.dg, 0, early))
+    v.dg_send = last_send(v.dg, most, width)
+    v.dg = step_three(v.dg, last_send(v.dg, 0, most))
     v.out_send, v.out_keep = sum_rows((v.pop.inner,), v.pop.down_parts, "block_out", first)
     v.cut()
 

time: 550 us -> 552 us (level)
  transfers between devices with their start and end apart: 86 -> 86, of which waited for: 31 -> 32; matrix products, arithmetic and copies ran while one was open for 10% -> 10% of each run, Pallas kernels for 33% -> 33%
where the time goes in v4:
time: 552 us; the launch traced here: 543 us
  waiting for transfers between devices  186 us (34%)
  Pallas kernels  178 us (32%)
  starting transfers between devices  92.3 us (17%)
  other arithmetic  62.4 us (11%)
  local copies, waits for them, and re-layouts  22.4 us (4%)
    ppermute x85, waiting for transfers between devices, swap(): return lax.ppermute(value, axis, [(0, 1), (1, 0)])  186 us
    ppermute x85, starting transfers between devices, swap(): return lax.ppermute(value, axis, [(0, 1), (1, 0)])  91.1 us
    pallas_call x3, Pallas kernels, weight_grad(): call(functools.partial(weight_grad_kernel, count // 8), name, (4,), [whol...  34.5 us
    pallas_call x2, Pallas kernels, sum_rows(): call(functools.partial(sum_kernel, len(lefts), first), name, (SUM_STEPS,)...  29.7 us
    pallas_call x1, Pallas kernels, attn_forward(): call(functools.partial(attn_forward_kernel, row, head_rows), 'attn_forwar...  23.8 us
    pallas_call x1, Pallas kernels, attn_backward(): call(functools.partial(attn_backward_kernel, row), 'attn_backward', (4,),...  23.6 us
    pallas_call x1, Pallas kernels, units(): call(units_kernel, 'units', (4,), [whole(one.shape) for one in (*hidden,...  22.6 us
    pallas_call x1, Pallas kernels, unit_grads(): call(functools.partial(unit_grads_kernel, first), 'unit_grads', (4,), [wh...  14.2 us
  transfers between devices with their start and end apart: 86, of which 32 were waited for; matrix products, arithmetic and copies ran while one was open for 10% of the time, Pallas kernels for 33%

profile of v4, /device:TPU:1, one launch (start us, length us, event | category | flops | bytes accessed | tf_op | source)
XLA Modules:
  0.0 542.7 jit_solution(10252509235849967405)
XLA Ops:
  13.6 28.1 %collective-permute-done.3 = bf16[1,256]{1,0:T(2,128)(2,1)S(1)} collective-permute-done((bf16[1,256]{1,0:T(2,128)(2,1)S(1)}, bf16[1,256]{1,0:T(2,128)(2,1)S(1)}, u32[]{:S(2)}, u32[]{:S(2)}) %collective-permute-start.3) | collective-permute-done | bytes 544 | tf_op jit(solution)/shard_map/ppermute | solution.py:633
  52.9 17.5 %collective-permute-done.7 = bf16[96,2048]{1,0:T(8,128)(2,1)} collective-permute-done((bf16[96,2048]{1,0:T(8,128)(2,1)}, bf16[96,2048]{1,0:T(8,128)(2,1)}, u32[]{:S(2)}, u32[]{:S(2)}) %collective-permute-start.7) | collective-permute-done | bytes 393248 | tf_op jit(solution)/shard_map/ppermute | solution.py:633
  78.8 3.1 fusion.8
  82.5 11.1 %collective-permute-done.12 = bf16[96,2048]{1,0:T(8,128)(2,1)S(1)} collective-permute-done((bf16[96,2048]{1,0:T(8,128)(2,1)S(1)}, bf16[96,2048]{1,0:T(8,128)(2,1)S(1)}, u32[]{:S(2)}, u32[]{:S(2)}) %collective-permute-start.12) | collective-permute-done | bytes 393248 | tf_op jit(solution)/shard_map/ppermute | solution.py:633
  99.8 3.0 collective-permute-start.15
  104.4 23.8 %attn_forward.1 = (bf16[1024,2048]{1,0:T(8,128)(2,1)}, bf16[1024,768]{1,0:T(8,128)(2,1)}, bf16[1024,512]{1,0:T(8,128)(2,1)}, bf16[2,256,2048]{2,1,0:T(8,128)(2,1...) custom-call(bf16[256,2048]{1,0:T(8,128)(2,1)} %bitcast.95, ...), custom_call_target="tpu_custom_call" | custom-call | flops 1000 | bytes 1000 | tf_op jit(solution)/shard_map/attn_forward/pallas_call | solution.py:260
  130.5 2.9 collective-permute-start.22
  139.9 28.7 %collective-permute-done.19 = bf16[96,2048]{1,0:T(8,128)(2,1)S(1)} collective-permute-done((bf16[96,2048]{1,0:T(8,128)(2,1)S(1)}, bf16[96,2048]{1,0:T(8,128)(2,1)S(1)}, u32[]{:S(2)}, u32[]{:S(2)}) %collective-permute-start.19) | collective-permute-done | bytes 393248 | tf_op jit(solution)/shard_map/ppermute | solution.py:633
  179.3 25.3 %collective-permute-done.24 = bf16[80,2048]{1,0:T(8,128)(2,1)S(1)} collective-permute-done((bf16[80,2048]{1,0:T(8,128)(2,1)S(1)}, bf16[80,2048]{1,0:T(8,128)(2,1)S(1)}, u32[]{:S(2)}, u32[]{:S(2)}) %collective-permute-start.24) | collective-permute-done | bytes 327712 | tf_op jit(solution)/shard_map/ppermute | solution.py:633
  215.0 22.6 %units.1 = (bf16[1024,1408]{1,0:T(8,128)(2,1)}, bf16[1024,1408]{1,0:T(8,128)(2,1)}, bf16[1024,1408]{1,0:T(8,128)(2,1)}) custom-call(bf16[256,2048]{1,0:T(8,128)(2,1)} %copy-done.3, bf16[256,2048]{1,0:T(8,128)(2,1)} %copy-done.11, bf16[256,2048]{1,0:T(8,128)(2,1)} %copy-done.10, bf16[256,2048]{1,0:T(8,128)(2,1)} %copy-done.12, bf16[352,2048]{1,0:T(8,128)(2,1)} %copy-done.13, ...), custom_call_target="tpu_custom_call" | custom-call | flops 1000 | bytes 1000 | tf_op jit(solution)/shard_map/units/pallas_call | solution.py:380
  243.6 11.4 %down_grad.1 = (bf16[4,176,1024]{2,1,0:T(8,128)(2,1)}, bf16[4,176,1024]{2,1,0:T(8,128)(2,1)}, bf16[4,176,1024]{2,1,0:T(8,128)(2,1)}, bf16[4,176,1024]{2,1,0:T(8,128)(2,1)}) custom-call(bf16[1024,1408]{1,0:T(8,128)(2,1)} %get-tuple-element.1124.l_ref.refs_0_, bf16[256,2048]{1,0:T(8,128)(2,1)} %bitcast.101, bf16[256,2048]{1,0:T(8,128)(2,1)} %collective-permute-done.32.refs_1_, ...), custom_call_target="tpu_custom_call" | custom-call | flops 1000 | bytes 1000 | tf_op jit(solution)/shard_map/down_grad/pallas_call | solution.py:509
  256.0 2.5 collective-permute-done.34.refs_9_.refs_4_
  260.2 14.2 %unit_grads.1 = (bf16[1024,1408]{1,0:T(8,128)(2,1)}, bf16[1024,1408]{1,0:T(8,128)(2,1)}) custom-call(bf16[256,2048]{1,0:T(8,128)(2,1)} %bitcast.102, bf16[256,2048]{1,0:T(8,128)(2,1)} %collective-permute-done.32.refs_1_, bf16[256,2048]{1,0:T(8,128)(2,1)} %collective-permute-done.33.refs_2_, bf16[256,2048]{1,0:T(8,128)(2,1)} %copy-done.40, ...), custom_call_target="tpu_custom_call" | custom-call | flops 1000 | bytes 1000 | tf_op jit(solution)/shard_map/unit_grads/pallas_call | solution.py:410
  274.4 18.6 %hidden_grads.1 = (bf16[256,2048]{1,0:T(8,128)(2,1)}, bf16[128,2048]{1,0:T(8,128)(2,1)}, bf16[128,2048]{1,0:T(8,128)(2,1)}, bf16[2,256,2048]{2,1,0:T(8,128)(2,1)}) custom-call(bf16[1024,1408]{1,0:T(8,128)(2,1)} %get-tuple-element.1074.refs_0_.l_ref, bf16[1024,1408]{1,0:T(8,128)(2,1)} %get-tuple-element.1177.refs_1_.l_ref, bf16[352,2048]{1,0:T(8,128)(2,1)} %copy-done.13, ...), custom_call_target="tpu_custom_call" | custom-call | flops 1000 | bytes 1000 | tf_op jit(solution)/shard_map/hidden_grads/pallas_call | solution.py:462
  306.8 11.8 %gate_grad.1 = (bf16[4,176,1024]{2,1,0:T(8,128)(2,1)}, bf16[4,176,1024]{2,1,0:T(8,128)(2,1)}, bf16[4,176,1024]{2,1,0:T(8,128)(2,1)}, bf16[4,176,1024]{2,1,0:T(8,128)(2,1)}) custom-call(bf16[1024,1408]{1,0:T(8,128)(2,1)} %get-tuple-element.1074.refs_0_.l_ref, bf16[256,2048]{1,0:T(8,128)(2,1)} %copy-done.3, bf16[256,2048]{1,0:T(8,128)(2,1)} %copy-done.11, ...), custom_call_target="tpu_custom_call" | custom-call | flops 1000 | bytes 1000 | tf_op jit(solution)/shard_map/gate_grad/pallas_call | solution.py:509
  332.7 11.1 %block_out.1 = (bf16[2,256,2048]{2,1,0:T(8,128)(2,1)}, bf16[2,256,2048]{2,1,0:T(8,128)(2,1)}) custom-call(bf16[1024,1408]{1,0:T(8,128)(2,1)} %get-tuple-element.1124.l_ref.refs_0_, bf16[272,2048]{1,0:T(8,128)(2,1)} %copy-done.6, bf16[272,2048]{1,0:T(8,128)(2,1)} %collective-permute-done.29.refs_7_.refs_2_, bf16[192,2048]{1,0:T(8,128)(2,1)} %copy-done.15, ...), custom_call_target="tpu_custom_call" | custom-call | flops 1000 | bytes 1000 | tf_op jit(solution)/shard_map/block_out/pallas_call | solution.py:462
  343.8 12.7 %collective-permute-done.46.refs_4_ = bf16[128,2048]{1,0:T(8,128)(2,1)S(1)} collective-permute-done((bf16[128,2048]{1,0:T(8,128)(2,1)S(1)}, bf16[128,2048]{1,0:T(8,128)(2,1)S(1)}, u32[]{:S(2)}, u32[]{:S(2)}) %collective-permute-start.46) | collective-permute-done | bytes 524320 | tf_op jit(solution)/shard_map/ppermute | solution.py:633
  361.4 3.3 collective-permute-start.54
  369.8 2.5 fusion.40
  374.5 11.3 %up_grad.1 = (bf16[4,176,1024]{2,1,0:T(8,128)(2,1)}, bf16[4,176,1024]{2,1,0:T(8,128)(2,1)}, bf16[4,176,1024]{2,1,0:T(8,128)(2,1)}, bf16[4,176,1024]{2,1,0:T(8,128)(2,1)}) custom-call(bf16[1024,1408]{1,0:T(8,128)(2,1)} %get-tuple-element.1177.refs_1_.l_ref, bf16[256,2048]{1,0:T(8,128)(2,1)} %copy-done.3, bf16[256,2048]{1,0:T(8,128)(2,1)} %copy-done.11, ...), custom_call_target="tpu_custom_call" | custom-call | flops 1000 | bytes 1000 | tf_op jit(solution)/shard_map/up_grad/pallas_call | solution.py:509
  401.7 23.6 %attn_backward.1 = (bf16[1024,768]{1,0:T(8,128)(2,1)}, f32[1,2048]{1,0:T(1,128)}, bf16[256,2048]{1,0:T(8,128)(2,1)}, bf16[128,2048]{1,0:T(8,128)(2,1)}, bf16[128...) custom-call(bf16[128,2048]{1,0:T(8,128)(2,1)} %copy-done.29, bf16[128,2048]{1,0:T(8,128)(2,1)} %copy-done.30, ...), custom_call_target="tpu_custom_call" | custom-call | flops 1000 | bytes 1000 | tf_op jit(solution)/shard_map/attn_backward/pallas_call | solution.py:337
  434.5 2.6 fusion.2
  440.8 11.9 %attn_grads.1 = (bf16[4,160,1024]{2,1,0:T(8,128)(2,1)}, bf16[4,160,1024]{2,1,0:T(8,128)(2,1)}, bf16[4,160,1024]{2,1,0:T(8,128)(2,1)}, bf16[4,160,1024]{2,1,0:T(8,128)(2,1)}) custom-call(bf16[1024,768]{1,0:T(8,128)(2,1)} %get-tuple-element.1283.gqkv_ref, bf16[1024,2048]{1,0:T(8,128)(2,1)} %get-tuple-element.1284.hid_ref, ...), custom_call_target="tpu_custom_call" | custom-call | flops 1000 | bytes 1000 | tf_op jit(solution)/shard_map/attn_grads/pallas_call | solution.py:547
  461.9 14.5 %collective-permute-done.73.refs_0_ = bf16[176,1280]{1,0:T(8,128)(2,1)S(1)} collective-permute-done((bf16[176,1280]{1,0:T(8,128)(2,1)S(1)}, bf16[176,1280]{1,0:T(8,128)(2,1)S(1)}, u32[]{:S(2)}, u32[]{:S(2)}) %collective-permute-start.73) | collective-permute-done | bytes 450592 | tf_op jit(solution)/shard_map/ppermute | solution.py:633
  476.4 6.7 %collective-permute-done.70 = bf16[4,160,1024]{2,1,0:T(8,128)(2,1)S(1)} collective-permute-done((bf16[4,160,1024]{2,1,0:T(8,128)(2,1)}, bf16[4,160,1024]{2,1,0:T(8,128)(2,1)S(1)}, u32[]{:S(2)}, u32[]{:S(2)}) %collective-permute-start.70) | collective-permute-done | bytes 1310752 | tf_op jit(solution)/shard_map/ppermute | solution.py:633
  491.2 12.0 %collective-permute-done.76 = f32[2,1,2,2,2,2,64]{6,5,4,3,2,1,0:T(2,128)S(1)} collective-permute-done((f32[2,1,2,2,2,2,64]{6,5,4,3,2,1,0:T(2,128)S(1)}, f32[2,1,2,2,2,2,64]{6,5,4,3,2,1,0:T(2,128)S(1)}, u32[]{:S(2)}, u32[]{:S(2)}) %collective-permute-start.76) | collective-permute-done | bytes 8224 | tf_op jit(solution)/shard_map/ppermute | solution.py:633
  511.5 6.1 %collective-permute-start.81 = (f32[2,1,2,1,1,1,64]{6,5,4,3,2,1,0:T(1,128)S(1)}, f32[2,1,2,1,1,1,64]{6,5,4,3,2,1,0:T(1,128)S(1)}, u32[]{:S(2)}, u32[]{:S(2)}) collective-permute-start(f32[2,1,2,1,1,1,64]{6,5,4,3,2,1,0:T(1,128)S(1)} %broadcast_select_fusion.4), channel_id=1, source_target_pairs={{0,2},{2,0},{1,3},{3,1},{4,6},{6,4},{5,7},{7,5},{8,10},{10,8},{9,1... | collective-permute-start | bytes 3080 | tf_op jit(solution)/shard_map/ppermute | solution.py:633
  517.6 3.2 total.3
  520.8 3.2 total.4
  524.0 3.2 total.5
  527.2 7.8 %finish.1 = (bf16[256,2048]{1,0:T(8,128)(2,1)}, bf16[256,2048]{1,0:T(8,128)(2,1)}) custom-call(bf16[256,2048]{1,0:T(8,128)(2,1)} %bitcast.97, f32[1,2048]{1,0:T(1,128)} %reshape.316.refs_4_.gain_ref, f32[128,2048]{1,0:T(8,128)} %get-tuple-element.1461.mid0_ref, f32[128,2048]{1,0:T(8,128)} %get-tuple-element.1462.mid1_ref, ...), custom_call_target="tpu_custom_call" | custom-call | flops 1000 | bytes 1000 | tf_op jit(solution)/shard_map/finish/pallas_call | solution.py:610
  535.5 3.8 collective-permute-done.84
  (491 shorter events, 176.3 us)
Async XLA Ops:
  3.1 38.7 %collective-permute-start.1 = (bf16[256,2048]{1,0:T(8,128)(2,1)}, bf16[256,2048]{1,0:T(8,128)(2,1)S(1)}, u32[]{:S(2)}, u32[]{:S(2)}) collective-permute-start(bf16[256,2048]{1,0:T(8,128)(2,1)} %pad_maximum_fusion.4), channel_id=1, source_target_pairs={{0,1},{1,0},{2,3},{3,2},{4,5},{5,4},{6,7},{7,6},{8,9},{9,8},{10,11... | collective-permute-start | bytes 3145736 | tf_op jit(solution)/shard_map/ppermute | solution.py:633
  5.2 36.6 %collective-permute-start.4 = (bf16[256,2048]{1,0:T(8,128)(2,1)S(1)}, bf16[256,2048]{1,0:T(8,128)(2,1)}, u32[]{:S(2)}, u32[]{:S(2)}) collective-permute-start(bf16[256,2048]{1,0:T(8,128)(2,1)S(1)} %bitcast.98), channel_id=1, source_target_pairs={{0,8},{8,0},{1,9},{9,1},{2,10},{10,2},{3,11},{11,3},{4,12},{12,4},... | collective-permute-start | bytes 3145736 | tf_op jit(solution)/shard_map/ppermute | solution.py:633
  8.7 33.0 %collective-permute-start.2 = (bf16[240,2048]{1,0:T(8,128)(2,1)}, bf16[240,2048]{1,0:T(8,128)(2,1)S(1)}, u32[]{:S(2)}, u32[]{:S(2)}) collective-permute-start(bf16[240,2048]{1,0:T(8,128)(2,1)} %pad_maximum_fusion.7), channel_id=1, source_target_pairs={{0,4},{4,0},{1,5},{5,1},{2,6},{6,2},{3,7},{7,3},{8,12},{12,8},{9,1... | collective-permute-start | bytes 2949128 | tf_op jit(solution)/shard_map/ppermute | solution.py:633
  10.8 30.9 %collective-permute-start = (bf16[144,2048]{1,0:T(8,128)(2,1)}, bf16[144,2048]{1,0:T(8,128)(2,1)}, u32[]{:S(2)}, u32[]{:S(2)}) collective-permute-start(bf16[144,2048]{1,0:T(8,128)(2,1)} %pad_maximum_fusion.13), channel_id=1, source_target_pairs={{0,16},{16,0},{1,17},{17,1},{2,18},{18,2},{3,19},{19,3},{4,20},{20... | collective-permute-start | bytes 1769480 | tf_op jit(solution)/shard_map/ppermute | solution.py:633
  13.3 28.4 %collective-permute-start.3 = (bf16[1,256]{1,0:T(2,128)(2,1)S(1)}, bf16[1,256]{1,0:T(2,128)(2,1)S(1)}, u32[]{:S(2)}, u32[]{:S(2)}) collective-permute-start(bf16[1,256]{1,0:T(2,128)(2,1)S(1)} %pad.8), channel_id=1, source_target_pairs={{0,8},{8,0},{1,9},{9,1},{2,10},{10,2},{3,11},{11,3},{4,12},{12,4},... | collective-permute-start | bytes 1544 | tf_op jit(solution)/shard_map/ppermute | solution.py:633
  95.8 34.7 %collective-permute-start.17 = (bf16[352,2048]{1,0:T(8,128)(2,1)S(1)}, bf16[352,2048]{1,0:T(8,128)(2,1)}, u32[]{:S(2)}, u32[]{:S(2)}) collective-permute-start(bf16[352,2048]{1,0:T(8,128)(2,1)S(1)} %constant_dynamic-update-slice_fusion.2.refs_8_.refs_6_), channel_id=1, source_target_pairs={{0,1},{1,0},{2,3},{3,2},{4,5},{5,4},{6,7},{7,6},{8,9},{9,8},{10,11... | collective-permute-start | bytes 4325384 | tf_op jit(solution)/shard_map/ppermute | solution.py:633
  96.0 34.5 %collective-permute-start.16 = (bf16[352,2048]{1,0:T(8,128)(2,1)S(1)}, bf16[352,2048]{1,0:T(8,128)(2,1)}, u32[]{:S(2)}, u32[]{:S(2)}) collective-permute-start(bf16[352,2048]{1,0:T(8,128)(2,1)S(1)} %constant_dynamic-update-slice_fusion.refs_4_.refs_2_), channel_id=1, source_target_pairs={{0,4},{4,0},{1,5},{5,1},{2,6},{6,2},{3,7},{7,3},{8,12},{12,8},{9,1... | collective-permute-start | bytes 4325384 | tf_op jit(solution)/shard_map/ppermute | solution.py:633
  98.2 32.3 %collective-permute-start.18 = (bf16[176,2048]{1,0:T(8,128)(2,1)}, bf16[176,2048]{1,0:T(8,128)(2,1)}, u32[]{:S(2)}, u32[]{:S(2)}) collective-permute-start(bf16[176,2048]{1,0:T(8,128)(2,1)} %param.22), channel_id=1, source_target_pairs={{0,16},{16,0},{1,17},{17,1},{2,18},{18,2},{3,19},{19,3},{4,20},{20... | collective-permute-start | bytes 2162696 | tf_op jit(solution)/shard_map/ppermute | solution.py:633
  135.7 32.9 %collective-permute-start.21 = (bf16[256,2048]{1,0:T(8,128)(2,1)S(1)}, bf16[256,2048]{1,0:T(8,128)(2,1)S(1)}, u32[]{:S(2)}, u32[]{:S(2)}) collective-permute-start(bf16[256,2048]{1,0:T(8,128)(2,1)S(1)} %pad_maximum_fusion.5), channel_id=1, source_target_pairs={{0,4},{4,0},{1,5},{5,1},{2,6},{6,2},{3,7},{7,3},{8,12},{12,8},{9,1... | collective-permute-start | bytes 3145736 | tf_op jit(solution)/shard_map/ppermute | solution.py:633
  135.9 32.6 %collective-permute-start.20 = (bf16[272,2048]{1,0:T(8,128)(2,1)S(1)}, bf16[272,2048]{1,0:T(8,128)(2,1)S(1)}, u32[]{:S(2)}, u32[]{:S(2)}) collective-permute-start(bf16[272,2048]{1,0:T(8,128)(2,1)S(1)} %pad_maximum_fusion.2), channel_id=1, source_target_pairs={{0,1},{1,0},{2,3},{3,2},{4,5},{5,4},{6,7},{7,6},{8,9},{9,8},{10,11... | collective-permute-start | bytes 3342344 | tf_op jit(solution)/shard_map/ppermute | solution.py:633
  137.9 32.6 %collective-permute-start.23 = (bf16[256,2048]{1,0:T(8,128)(2,1)S(1)}, bf16[256,2048]{1,0:T(8,128)(2,1)S(1)}, u32[]{:S(2)}, u32[]{:S(2)}) collective-permute-start(bf16[256,2048]{1,0:T(8,128)(2,1)S(1)} %fusion.1), channel_id=1, source_target_pairs={{0,8},{8,0},{1,9},{9,1},{2,10},{10,2},{3,11},{11,3},{4,12},{12,4},... | collective-permute-start | bytes 3145736 | tf_op jit(solution)/shard_map/ppermute | solution.py:633
  138.0 30.6 %collective-permute-start.19 = (bf16[96,2048]{1,0:T(8,128)(2,1)S(1)}, bf16[96,2048]{1,0:T(8,128)(2,1)S(1)}, u32[]{:S(2)}, u32[]{:S(2)}) collective-permute-start(bf16[96,2048]{1,0:T(8,128)(2,1)S(1)} %slice.399), channel_id=1, source_target_pairs={{0,16},{16,0},{1,17},{17,1},{2,18},{18,2},{3,19},{19,3},{4,20},{20... | collective-permute-start | bytes 1179656 | tf_op jit(solution)/shard_map/ppermute | solution.py:633
  170.8 34.9 %collective-permute-start.25 = (bf16[352,2048]{1,0:T(8,128)(2,1)S(1)}, bf16[352,2048]{1,0:T(8,128)(2,1)S(1)}, u32[]{:S(2)}, u32[]{:S(2)}) collective-permute-start(bf16[352,2048]{1,0:T(8,128)(2,1)S(1)} %pad_maximum_fusion.refs_6_.refs_4_), channel_id=1, source_target_pairs={{0,4},{4,0},{1,5},{5,1},{2,6},{6,2},{3,7},{7,3},{8,12},{12,8},{9,1... | collective-permute-start | bytes 4325384 | tf_op jit(solution)/shard_map/ppermute | solution.py:633
  173.3 32.4 %collective-permute-start.28 = (bf16[352,2048]{1,0:T(8,128)(2,1)S(1)}, bf16[352,2048]{1,0:T(8,128)(2,1)S(1)}, u32[]{:S(2)}, u32[]{:S(2)}) collective-permute-start(bf16[352,2048]{1,0:T(8,128)(2,1)S(1)} %pad_maximum_fusion.1.refs_10_.refs_8_), channel_id=1, source_target_pairs={{0,1},{1,0},{2,3},{3,2},{4,5},{5,4},{6,7},{7,6},{8,9},{9,8},{10,11... | collective-permute-start | bytes 4325384 | tf_op jit(solution)/shard_map/ppermute | solution.py:633
  175.5 30.3 %collective-permute-start.27 = (bf16[256,2048]{1,0:T(8,128)(2,1)S(1)}, bf16[256,2048]{1,0:T(8,128)(2,1)S(1)}, u32[]{:S(2)}, u32[]{:S(2)}) collective-permute-start(bf16[256,2048]{1,0:T(8,128)(2,1)S(1)} %multiply_convert_fusion.refs_0_), channel_id=1, source_target_pairs={{0,8},{8,0},{1,9},{9,1},{2,10},{10,2},{3,11},{11,3},{4,12},{12,4},... | collective-permute-start | bytes 3145736 | tf_op jit(solution)/shard_map/ppermute | solution.py:633
  176.5 29.2 %collective-permute-start.26 = (bf16[256,2048]{1,0:T(8,128)(2,1)S(1)}, bf16[256,2048]{1,0:T(8,128)(2,1)S(1)}, u32[]{:S(2)}, u32[]{:S(2)}) collective-permute-start(bf16[256,2048]{1,0:T(8,128)(2,1)S(1)} %multiply_convert_fusion.refs_0_), channel_id=1, source_target_pairs={{0,2},{2,0},{1,3},{3,1},{4,6},{6,4},{5,7},{7,5},{8,10},{10,8},{9,1... | collective-permute-start | bytes 3145736 | tf_op jit(solution)/shard_map/ppermute | solution.py:633
  209.3 28.3 %collective-permute-start.29 = (bf16[272,2048]{1,0:T(8,128)(2,1)S(1)}, bf16[272,2048]{1,0:T(8,128)(2,1)}, u32[]{:S(2)}, u32[]{:S(2)}) collective-permute-start(bf16[272,2048]{1,0:T(8,128)(2,1)S(1)} %pad_maximum_fusion.3.refs_6_.refs_1_), channel_id=1, source_target_pairs={{0,4},{4,0},{1,5},{5,1},{2,6},{6,2},{3,7},{7,3},{8,12},{12,8},{9,1... | collective-permute-start | bytes 3342344 | tf_op jit(solution)/shard_map/ppermute | solution.py:633
  210.1 27.4 %collective-permute-start.30 = (bf16[256,2048]{1,0:T(8,128)(2,1)S(1)}, bf16[256,2048]{1,0:T(8,128)(2,1)}, u32[]{:S(2)}, u32[]{:S(2)}) collective-permute-start(bf16[256,2048]{1,0:T(8,128)(2,1)S(1)} %pad_maximum_fusion.6.refs_10_.refs_5_), channel_id=1, source_target_pairs={{0,1},{1,0},{2,3},{3,2},{4,5},{5,4},{6,7},{7,6},{8,9},{9,8},{10,11... | collective-permute-start | bytes 3145736 | tf_op jit(solution)/shard_map/ppermute | solution.py:633
  258.5 39.0 %collective-permute-start.37 = (bf16[4,176,1024]{2,1,0:T(8,128)(2,1)}, bf16[4,176,1024]{2,1,0:T(8,128)(2,1)S(1)}, u32[]{:S(2)}, u32[]{:S(2)}) collective-permute-start(bf16[4,176,1024]{2,1,0:T(8,128)(2,1)} %get-tuple-element.959), channel_id=1, source_target_pairs={{0,4},{4,0},{1,5},{5,1},{2,6},{6,2},{3,7},{7,3},{8,12},{12,8},{9,1... | collective-permute-start | bytes 4325384 | tf_op jit(solution)/shard_map/ppermute | solution.py:633
  259.0 38.5 %collective-permute-start.38 = (bf16[4,176,1024]{2,1,0:T(8,128)(2,1)}, bf16[4,176,1024]{2,1,0:T(8,128)(2,1)S(1)}, u32[]{:S(2)}, u32[]{:S(2)}) collective-permute-start(bf16[4,176,1024]{2,1,0:T(8,128)(2,1)} %get-tuple-element.961), channel_id=1, source_target_pairs={{0,1},{1,0},{2,3},{3,2},{4,5},{5,4},{6,7},{7,6},{8,9},{9,8},{10,11... | collective-permute-start | bytes 4325384 | tf_op jit(solution)/shard_map/ppermute | solution.py:633
  325.2 31.3 %collective-permute-start.45 = (bf16[176,1536]{1,0:T(8,128)(2,1)}, bf16[176,1536]{1,0:T(8,128)(2,1)S(1)}, u32[]{:S(2)}, u32[]{:S(2)}) collective-permute-start(bf16[176,1536]{1,0:T(8,128)(2,1)} %pad_maximum_fusion.14), channel_id=1, source_target_pairs={{0,16},{16,0},{1,17},{17,1},{2,18},{18,2},{3,19},{19,3},{4,20},{20... | collective-permute-start | bytes 1622024 | tf_op jit(solution)/shard_map/ppermute | solution.py:633
  326.5 31.6 %collective-permute-start.48 = (bf16[4,176,1024]{2,1,0:T(8,128)(2,1)}, bf16[4,176,1024]{2,1,0:T(8,128)(2,1)}, u32[]{:S(2)}, u32[]{:S(2)}) collective-permute-start(bf16[4,176,1024]{2,1,0:T(8,128)(2,1)} %get-tuple-element.1115), channel_id=1, source_target_pairs={{0,4},{4,0},{1,5},{5,1},{2,6},{6,2},{3,7},{7,3},{8,12},{12,8},{9,1... | collective-permute-start | bytes 4325384 | tf_op jit(solution)/shard_map/ppermute | solution.py:633
  327.6 31.3 %collective-permute-start.49 = (bf16[4,176,1024]{2,1,0:T(8,128)(2,1)}, bf16[4,176,1024]{2,1,0:T(8,128)(2,1)}, u32[]{:S(2)}, u32[]{:S(2)}) collective-permute-start(bf16[4,176,1024]{2,1,0:T(8,128)(2,1)} %get-tuple-element.1117), channel_id=1, source_target_pairs={{0,1},{1,0},{2,3},{3,2},{4,5},{5,4},{6,7},{7,6},{8,9},{9,8},{10,11... | collective-permute-start | bytes 4325384 | tf_op jit(solution)/shard_map/ppermute | solution.py:633
  361.1 28.4 %collective-permute-start.53 = (bf16[2,176,1024]{2,1,0:T(8,128)(2,1)}, bf16[2,176,1024]{2,1,0:T(8,128)(2,1)}, u32[]{:S(2)}, u32[]{:S(2)}) collective-permute-start(bf16[2,176,1024]{2,1,0:T(8,128)(2,1)} %add_convert_fusion.3), channel_id=1, source_target_pairs={{0,4},{4,0},{1,5},{5,1},{2,6},{6,2},{3,7},{7,3},{8,12},{12,8},{9,1... | collective-permute-start | bytes 2162696 | tf_op jit(solution)/shard_map/ppermute | solution.py:633
  361.4 28.0 %collective-permute-start.54 = (bf16[2,256,2048]{2,1,0:T(8,128)(2,1)}, bf16[2,256,2048]{2,1,0:T(8,128)(2,1)S(1)}, u32[]{:S(2)}, u32[]{:S(2)}) collective-permute-start(bf16[2,256,2048]{2,1,0:T(8,128)(2,1)} %get-tuple-element.1171), channel_id=1, source_target_pairs={{0,2},{2,0},{1,3},{3,1},{4,6},{6,4},{5,7},{7,5},{8,10},{10,8},{9,1... | collective-permute-start | bytes 6291464 | tf_op jit(solution)/shard_map/ppermute | solution.py:633
  390.7 37.9 %collective-permute-start.63 = (bf16[4,176,1024]{2,1,0:T(8,128)(2,1)}, bf16[4,176,1024]{2,1,0:T(8,128)(2,1)}, u32[]{:S(2)}, u32[]{:S(2)}) collective-permute-start(bf16[4,176,1024]{2,1,0:T(8,128)(2,1)} %get-tuple-element.1236), channel_id=1, source_target_pairs={{0,4},{4,0},{1,5},{5,1},{2,6},{6,2},{3,7},{7,3},{8,12},{12,8},{9,1... | collective-permute-start | bytes 4325384 | tf_op jit(solution)/shard_map/ppermute | solution.py:633
  391.1 37.5 %collective-permute-start.64 = (bf16[4,176,1024]{2,1,0:T(8,128)(2,1)}, bf16[4,176,1024]{2,1,0:T(8,128)(2,1)}, u32[]{:S(2)}, u32[]{:S(2)}) collective-permute-start(bf16[4,176,1024]{2,1,0:T(8,128)(2,1)} %get-tuple-element.1238), channel_id=1, source_target_pairs={{0,1},{1,0},{2,3},{3,2},{4,5},{5,4},{6,7},{7,6},{8,9},{9,8},{10,11... | collective-permute-start | bytes 4325384 | tf_op jit(solution)/shard_map/ppermute | solution.py:633
  393.2 32.8 %collective-permute-start.62 = (bf16[128,2048]{1,0:T(8,128)(2,1)}, bf16[128,2048]{1,0:T(8,128)(2,1)}, u32[]{:S(2)}, u32[]{:S(2)}) collective-permute-start(bf16[128,2048]{1,0:T(8,128)(2,1)} %fusion.9), channel_id=1, source_target_pairs={{0,8},{8,0},{1,9},{9,1},{2,10},{10,2},{3,11},{11,3},{4,12},{12,4},... | collective-permute-start | bytes 1572872 | tf_op jit(solution)/shard_map/ppermute | solution.py:633
  454.1 29.0 %collective-permute-start.70 = (bf16[4,160,1024]{2,1,0:T(8,128)(2,1)}, bf16[4,160,1024]{2,1,0:T(8,128)(2,1)S(1)}, u32[]{:S(2)}, u32[]{:S(2)}) collective-permute-start(bf16[4,160,1024]{2,1,0:T(8,128)(2,1)} %get-tuple-element.1334), channel_id=1, source_target_pairs={{0,4},{4,0},{1,5},{5,1},{2,6},{6,2},{3,7},{7,3},{8,12},{12,8},{9,1... | collective-permute-start | bytes 3932168 | tf_op jit(solution)/shard_map/ppermute | solution.py:633
  454.4 28.7 %collective-permute-start.71 = (bf16[4,160,1024]{2,1,0:T(8,128)(2,1)}, bf16[4,160,1024]{2,1,0:T(8,128)(2,1)S(1)}, u32[]{:S(2)}, u32[]{:S(2)}) collective-permute-start(bf16[4,160,1024]{2,1,0:T(8,128)(2,1)} %get-tuple-element.1336), channel_id=1, source_target_pairs={{0,1},{1,0},{2,3},{3,2},{4,5},{5,4},{6,7},{7,6},{8,9},{9,8},{10,11... | collective-permute-start | bytes 3932168 | tf_op jit(solution)/shard_map/ppermute | solution.py:633
  508.0 27.5 %collective-permute-start.83 = (bf16[160,1024]{1,0:T(8,128)(2,1)S(1)}, bf16[160,1024]{1,0:T(8,128)(2,1)S(1)}, u32[]{:S(2)}, u32[]{:S(2)}) collective-permute-start(bf16[160,1024]{1,0:T(8,128)(2,1)S(1)} %get-tuple-element.1521), channel_id=1, source_target_pairs={{0,16},{16,0},{1,17},{17,1},{2,18},{18,2},{3,19},{19,3},{4,20},{20... | collective-permute-start | bytes 983048 | tf_op jit(solution)/shard_map/ppermute | solution.py:633
  509.6 29.7 %collective-permute-start.84 = (bf16[160,1024]{1,0:T(8,128)(2,1)S(1)}, bf16[160,1024]{1,0:T(8,128)(2,1)S(1)}, u32[]{:S(2)}, u32[]{:S(2)}) collective-permute-start(bf16[160,1024]{1,0:T(8,128)(2,1)S(1)} %get-tuple-element.1523), channel_id=1, source_target_pairs={{0,16},{16,0},{1,17},{17,1},{2,18},{18,2},{3,19},{19,3},{4,20},{20... | collective-permute-start | bytes 983048 | tf_op jit(solution)/shard_map/ppermute | solution.py:633
  (153 other events, 1911.6 us)
